TPU v7x, 256 devices: a whole 4x4x8 slice. The times are simulated.
256 devices in a mesh: lat: 8 (over y, core), lon: 32 (over x, z).
Axes of the slice: x: 4, y: 4, z: 8, core: 2. Of those that a mesh axis runs over, the one named last changes fastest.
Arguments:
- x_field: float32 [8, 32, 128, 512], P('lat', 'lon'), may hold values from -6 to 6
- residual: float32 [8, 32, 128, 512], P('lat', 'lon'), may hold values from -120 to 120
- direction: float32 [8, 32, 128, 512], P('lat', 'lon'), may hold values from -120 to 120
- a_node: bfloat16 [8, 32, 128, 512], P('lat', 'lon'), may hold values from -6 to 6
- a_edge: bfloat16 [8, 32, 1024, 512], P('lat', 'lon'), may hold values from -6 to 6
- senders: int32 [8, 32, 1024], P('lat', 'lon'), may hold values from -1 to 1151, as said below
- receivers: int32 [8, 32, 1024], P('lat', 'lon'), may hold values from -1 to 127, as said below
- obs_weight: float32 [8, 32, 128], P('lat', 'lon'), may hold values from 0.5 to 4
- w_send: bfloat16 [512, 512], replicated, may hold values from -0.25 to 0.25
- w_recv: bfloat16 [512, 512], replicated, may hold values from -0.25 to 0.25
- w_edge_out: bfloat16 [512, 512], replicated, may hold values from -0.25 to 0.25
- w_node_self: bfloat16 [512, 512], replicated, may hold values from -0.25 to 0.25
- w_node_msg: bfloat16 [512, 512], replicated, may hold values from -0.25 to 0.25
- w_node_out: bfloat16 [512, 512], replicated, may hold values from -0.25 to 0.25
Outputs:
- new_field: float32 [8, 32, 128, 512], P('lat', 'lon')
- new_residual: float32 [8, 32, 128, 512], P('lat', 'lon')
- new_direction: float32 [8, 32, 128, 512], P('lat', 'lon')
Inputs may be any that keep to these rules, and one draw needn't show every extreme that they name: `senders`: -1 marks a padded slot, exactly where receivers is -1; in each region the live slots come first; otherwise s // 128 is a block of the 3 x 3 neighbourhood whose latitude offset stays inside the mesh, and some region has no padded slot. `receivers`: -1 exactly at padded slots.
All inputs are finite; a program needn't handle non-finite values.
Results may differ from a plain program's by a relative error of at most 0.008.
Values may be sent and summed in bfloat16 or wider, within the bound.
No kernel may reach another device: no remote copies, remote signals or barrier semaphores. Data moves between devices by JAX's collectives and lax.ppermute only.
A program may use at most 64 MiB of HBM per device.

v0:
```python
import jax
import jax.numpy as jnp
from jax import lax
from jax.sharding import PartitionSpec as P


def padded(cells, sides, width):
    for axis, dim in sides:
        count = lax.axis_size(axis)
        head = lax.slice_in_dim(cells, 0, width, axis=dim)
        tail = lax.slice_in_dim(cells, cells.shape[dim] - width, cells.shape[dim], axis=dim)
        cells = jnp.concatenate(
            [
                lax.ppermute(tail, axis, [(i, (i + 1) % count) for i in range(count)]),
                cells,
                lax.ppermute(head, axis, [((i + 1) % count, i) for i in range(count)]),
            ],
            axis=dim,
        )
    return cells


def silu_slope(value):
    sigmoid_value = jax.nn.sigmoid(value)
    return sigmoid_value * (1.0 + value * (1.0 - sigmoid_value))


def dot_back(left, weight):
    return lax.dot_general(
        left, weight, (((1,), (1,)), ((), ())), preferred_element_type=jnp.float32
    )


def collect(picker, values):
    return lax.dot_general(
        picker, values, (((0,), (0,)), ((), ())), preferred_element_type=jnp.float32
    )


def body(
    x_field,
    residual,
    direction,
    a_node,
    a_edge,
    senders,
    receivers,
    obs_weight,
    w_send,
    w_recv,
    w_edge_out,
    w_node_self,
    w_node_msg,
    w_node_out,
):
    nodes_dev = x_field.shape[2]
    width = x_field.shape[3]
    edges_dev = a_edge.shape[2]
    block_total = edges_dev // 128
    search = direction.reshape(nodes_dev, width)
    send_flat = senders.reshape(edges_dev)
    recv_flat = receivers.reshape(edges_dev)
    act_flat = a_edge.reshape(edges_dev, width)
    search_bf = search.astype(jnp.bfloat16)
    send_term = jnp.dot(search_bf, w_send, preferred_element_type=jnp.float32).astype(jnp.bfloat16)
    recv_term = jnp.dot(search_bf, w_recv, preferred_element_type=jnp.float32).astype(jnp.bfloat16)
    own_rows = send_term.reshape(1, 1, nodes_dev, width)
    beside_all = padded(own_rows, (("lat", 0), ("lon", 1)), 1)
    sender_table = beside_all.reshape(9 * nodes_dev, width)
    slot_ids = jnp.arange(9 * nodes_dev, dtype=jnp.int32)
    own_ids = jnp.arange(nodes_dev, dtype=jnp.int32)

    def pickers(step_index):
        start = step_index * 128
        sends = lax.dynamic_slice_in_dim(send_flat, start, 128)
        recvs = lax.dynamic_slice_in_dim(recv_flat, start, 128)
        edge_act = lax.dynamic_slice_in_dim(act_flat, start, 128).astype(jnp.float32)
        pick_send = (sends[:, None] == slot_ids[None, :]).astype(jnp.bfloat16)
        pick_recv = (recvs[:, None] == own_ids[None, :]).astype(jnp.bfloat16)
        return (pick_send, pick_recv, silu_slope(edge_act))

    def tangent_block(step_index, total):
        pick_send, pick_recv, slope = pickers(step_index)
        gathered = jnp.dot(pick_send, sender_table, preferred_element_type=jnp.float32) + jnp.dot(
            pick_recv, recv_term, preferred_element_type=jnp.float32
        )
        hidden = (slope * gathered).astype(jnp.bfloat16)
        message = jnp.dot(hidden, w_edge_out, preferred_element_type=jnp.float32).astype(
            jnp.bfloat16
        )
        return total + collect(pick_recv, message)

    inbox = lax.fori_loop(0, block_total, tangent_block, jnp.zeros((nodes_dev, width), jnp.float32))
    node_slope = silu_slope(a_node.reshape(nodes_dev, width).astype(jnp.float32))
    pre_node = jnp.dot(search_bf, w_node_self, preferred_element_type=jnp.float32) + jnp.dot(
        inbox.astype(jnp.bfloat16), w_node_msg, preferred_element_type=jnp.float32
    )
    node_hidden = (node_slope * pre_node).astype(jnp.bfloat16)
    changed = search + jnp.dot(node_hidden, w_node_out, preferred_element_type=jnp.float32)
    observed = obs_weight.reshape(nodes_dev, 1) * changed
    observed_bf = observed.astype(jnp.bfloat16)
    node_grad = (dot_back(observed_bf, w_node_out) * node_slope).astype(jnp.bfloat16)
    back_self = dot_back(node_grad, w_node_self)
    msg_grad = dot_back(node_grad, w_node_msg).astype(jnp.bfloat16)

    def adjoint_block(step_index, carry):
        send_sums, recv_sums = carry
        pick_send, pick_recv, slope = pickers(step_index)
        edge_in = jnp.dot(pick_recv, msg_grad, preferred_element_type=jnp.float32).astype(
            jnp.bfloat16
        )
        edge_grad = (dot_back(edge_in, w_edge_out) * slope).astype(jnp.bfloat16)
        to_send = dot_back(edge_grad, w_send).astype(jnp.bfloat16)
        to_recv = dot_back(edge_grad, w_recv).astype(jnp.bfloat16)
        return (send_sums + collect(pick_send, to_send), recv_sums + collect(pick_recv, to_recv))

    start_carry = (
        jnp.zeros((9 * nodes_dev, width), jnp.float32),
        jnp.zeros((nodes_dev, width), jnp.float32),
    )
    send_sums, back_recv = lax.fori_loop(0, block_total, adjoint_block, start_carry)
    grid_sums = send_sums.reshape(3, 3, nodes_dev, width)
    arrived = padded(grid_sums.astype(jnp.bfloat16), (("lat", 0), ("lon", 1)), 1).astype(
        grid_sums.dtype
    )
    back_send = (
        grid_sums[1, 1]
        + arrived[0, 0]
        + arrived[0, 2]
        + arrived[0, 4]
        + arrived[2, 0]
        + arrived[2, 4]
        + arrived[4, 0]
        + arrived[4, 2]
        + arrived[4, 4]
    )
    product = (search + observed + back_self + back_send + back_recv).reshape(direction.shape)
    norm_now, curvature = lax.psum(
        (jnp.sum(residual * residual), jnp.sum(direction * product)), ("lat", "lon")
    )
    alpha = norm_now / curvature
    new_residual = residual - alpha * product
    norm_next = lax.psum(jnp.sum(new_residual * new_residual), ("lat", "lon"))
    new_field = x_field + alpha * direction
    new_direction = new_residual + norm_next / norm_now * direction
    return (new_field, new_residual, new_direction)


def solution(mesh):
    return jax.shard_map(
        body,
        mesh=mesh,
        in_specs=(
            P("lat", "lon", None, None),
            P("lat", "lon", None, None),
            P("lat", "lon", None, None),
            P("lat", "lon", None, None),
            P("lat", "lon", None, None),
            P("lat", "lon", None),
            P("lat", "lon", None),
            P("lat", "lon", None),
            P(),
            P(),
            P(),
            P(),
            P(),
            P(),
        ),
        out_specs=(
            P("lat", "lon", None, None),
            P("lat", "lon", None, None),
            P("lat", "lon", None, None),
        ),
        check_vma=False,
    )
```

profile of v0, /device:TPU:1, one launch (start us, length us, event | category | flops | bytes accessed | tf_op | source)
XLA Modules:
  0.0 327.8 jit_solution(2978387409693767192)
XLA Ops:
  0.7 1.4 fusion.33
  2.1 3.3 collective-permute-start.1
  5.4 2.2 collective-permute-done.1
  8.6 7.8 %collective-permute-start.3 = (bf16[3,1,128,512]{3,2,1,0:T(8,128)(2,1)S(1)}, bf16[3,1,128,512]{3,2,1,0:T(8,128)(2,1)S(1)}, u32[]{:S(2)}, u32[]{:S(2)}) collective-permute-start(bf16[3,1,128,512]{3,2,1,0:T(8,128)(2,1)S(1)} %pad_maximum_fusion.4), channel_id=1, source_target_pairs={{1,0},{2,1},{3,2},{4,3},{5,4},{6,5},{7,6},{8,7},{9,8},{10,9},{11,1... | collective-permute-start | bytes 1179656 | tf_op jit(solution)/shard_map/ppermute | solution.py:16
  16.4 1.8 fusion.58
  19.2 1.9 collective-permute-done.3
  21.1 5.2 %collective-permute-done.2 = bf16[3,1,128,512]{3,2,1,0:T(8,128)(2,1)S(1)} collective-permute-done((bf16[3,1,128,512]{3,2,1,0:T(8,128)(2,1)S(1)}, bf16[3,1,128,512]{3,2,1,0:T(8,128)(2,1)S(1)}, u32[]{:S(2)}, u32[]{:S(2)}) %collective-permute-start.2) | collective-permute-done | bytes 393248 | tf_op jit(solution)/shard_map/ppermute | solution.py:14
  26.4 2.1 pad_maximum_fusion
  28.5 50.5 %while.30 = (s32[]{:T(128)}, f32[128,512]{1,0:T(8,128)}, s32[1024]{0:T(1024)}, bf16[1024,512]{1,0:T(8,128)(2,1)}, s32[1024]{0:T(1024)}, /*index=5*/bf16[1152,512...) while((s32[]{:T(128)}, f32[128,512]{1,0:T(8,128)}, ...), condition=%wide.region_3.0_spmd.clone, body=%wide.region_2.0_spmd.clone.sunk | while | flops 252755968 | bytes 3804893 | solution.py:93
  29.3 1.6 fusion.106
  31.8 1.1 fusion.107
  34.8 1.6 fusion.106
  37.2 1.1 fusion.107
  38.4 2.1 convolution_add_fusion.10
  41.2 1.6 fusion.106
  44.8 2.1 convolution_add_fusion.10
  47.7 1.6 fusion.106
  51.2 2.1 convolution_add_fusion.10
  54.1 1.6 fusion.106
  56.5 1.1 fusion.107
  57.7 2.1 convolution_add_fusion.10
  60.5 1.6 fusion.106
  64.1 2.1 convolution_add_fusion.10
  66.9 1.6 fusion.106
  70.5 2.1 convolution_add_fusion.10
  73.4 1.6 fusion.106
  77.0 2.1 convolution_add_fusion.10
  79.0 2.6 fusion.30
  81.6 1.5 fusion.31
  84.1 53.3 %while.31 = (s32[]{:T(128)}, f32[1152,512]{1,0:T(8,128)S(1)}, f32[128,512]{1,0:T(8,128)}, s32[1024]{0:T(1024)}, s32[1024]{0:T(1024)}, /*index=5*/bf16[128,512]{1...) while((s32[]{:T(128)}, f32[1152,512]{1,0:T(8,128)S(1)}, ...), condition=%wide.region_5.0_spmd.clone, body=%wide.region_4.0_spmd.clone.sunk | while | flops 388218880 | bytes 7474898 | solution.py:121
  84.9 1.5 fusion.114
  87.2 1.3 convolution_add_fusion.11
  88.5 2.2 convolution_add_fusion.12
  91.5 1.5 fusion.114
  93.8 1.3 convolution_add_fusion.11
  95.1 2.3 convolution_add_fusion.12
  98.2 1.5 fusion.114
  100.5 1.3 convolution_add_fusion.11
  101.8 2.3 convolution_add_fusion.12
  104.9 1.5 fusion.114
  107.2 1.3 convolution_add_fusion.11
  108.5 2.3 convolution_add_fusion.12
  111.5 1.5 fusion.114
  113.8 1.3 convolution_add_fusion.11
  115.2 2.3 convolution_add_fusion.12
  118.2 1.5 fusion.114
  120.5 1.3 convolution_add_fusion.11
  121.8 2.3 convolution_add_fusion.12
  124.9 1.5 fusion.114
  127.2 1.3 convolution_add_fusion.11
  128.5 2.3 convolution_add_fusion.12
  131.6 1.5 fusion.114
  133.9 1.3 convolution_add_fusion.11
  135.2 2.3 convolution_add_fusion.12
  137.7 5.7 %collective-permute-start.5 = (bf16[1,3,128,512]{3,2,1,0:T(8,128)(2,1)S(1)}, bf16[1,3,128,512]{3,2,1,0:T(8,128)(2,1)S(1)}, u32[]{:S(2)}, u32[]{:S(2)}) collective-permute-start(bf16[1,3,128,512]{3,2,1,0:T(8,128)(2,1)S(1)} %get-tuple-element.488), channel_id=1, source_target_pairs={{32,0},{64,32},{96,64},{128,96},{160,128},{192,160},{224,192},{0,2... | collective-permute-start | bytes 1179656 | tf_op jit(solution)/shard_map/ppermute | solution.py:16
  144.1 5.4 %collective-permute-done.5 = bf16[1,3,128,512]{3,2,1,0:T(8,128)(2,1)S(1)} collective-permute-done((bf16[1,3,128,512]{3,2,1,0:T(8,128)(2,1)S(1)}, bf16[1,3,128,512]{3,2,1,0:T(8,128)(2,1)S(1)}, u32[]{:S(2)}, u32[]{:S(2)}) %collective-permute-start.5) | collective-permute-done | bytes 393248 | tf_op jit(solution)/shard_map/ppermute | solution.py:16
  149.7 1.5 collective-permute-start.6
  151.9 8.9 %collective-permute-done.7 = bf16[5,1,128,512]{3,2,1,0:T(8,128)(2,1)S(1)} collective-permute-done((bf16[5,1,128,512]{3,2,1,0:T(8,128)(2,1)S(1)}, bf16[5,1,128,512]{3,2,1,0:T(8,128)(2,1)S(1)}, u32[]{:S(2)}, u32[]{:S(2)}) %collective-permute-start.7) | collective-permute-done | bytes 655392 | tf_op jit(solution)/shard_map/ppermute | solution.py:16
  160.8 3.0 collective-permute-done.6
  163.8 1.7 fusion.43
  165.5 81.7 %all-reduce = (f32[]{:T(128)}, f32[]{:T(128)}) all-reduce(f32[]{:T(128)} %multiply_reduce_fusion.1, f32[]{:T(128)} %get-tuple-element.483), channel_id=1, replica_groups=mesh['lat'=8,'lon'=32] {'lat','lon'}, use_global_device_ids=true, to_apply=%region_1.0 | all-reduce | flops 2 | bytes 16 | tf_op jit(solution)/shard_map/psum | solution.py:138
  248.6 1.6 multiply_reduce_fusion
  250.3 74.4 %psum.23 = f32[]{:T(128)} all-reduce(f32[]{:T(128)} %get-tuple-element.481), channel_id=1, replica_groups=mesh['lat'=8,'lon'=32] {'lat','lon'}, use_global_device_ids=true, to_apply=%region_9.0 | all-reduce | flops 1 | bytes 8 | tf_op jit(solution)/shard_map/psum | solution.py:143
  326.0 1.8 multiply_add_fusion
  (100 shorter events, 36.4 us)
Async XLA Ops:
  0.6 17.6 %copy-start = (bf16[512,512]{1,0:T(8,128)(2,1)S(1)}, bf16[512,512]{1,0:T(8,128)(2,1)}, u32[]{:S(2)}) copy-start(bf16[512,512]{1,0:T(8,128)(2,1)} %param.29) | copy-start | bytes 1572868
  0.6 15.8 %copy-start.2 = (bf16[512,512]{1,0:T(8,128)(2,1)S(1)}, bf16[512,512]{1,0:T(8,128)(2,1)}, u32[]{:S(2)}) copy-start(bf16[512,512]{1,0:T(8,128)(2,1)} %param.27) | copy-start | bytes 1572868
  2.1 5.5 %collective-permute-start.1 = (bf16[1,1,128,512]{3,2,1,0:T(8,128)(2,1)S(1)}, bf16[1,1,128,512]{3,2,1,0:T(8,128)(2,1)}, u32[]{:S(2)}, u32[]{:S(2)}) collective-permute-start(bf16[1,1,128,512]{3,2,1,0:T(8,128)(2,1)S(1)} %fusion.33), channel_id=1, source_target_pairs={{32,0},{64,32},{96,64},{128,96},{160,128},{192,160},{224,192},{0,2... | collective-permute-start | bytes 393224 | tf_op jit(solution)/shard_map/ppermute | solution.py:16
  5.3 2.2 collective-permute-start
  5.4 12.9 %copy-start.5 = (f32[1,1,128,512]{3,2,1,0:T(8,128)S(1)}, f32[1,1,128,512]{3,2,1,0:T(8,128)}, u32[]{:S(2)}) copy-start(f32[1,1,128,512]{3,2,1,0:T(8,128)} %param.20) | copy-start | bytes 786436
  8.6 12.6 %collective-permute-start.3 = (bf16[3,1,128,512]{3,2,1,0:T(8,128)(2,1)S(1)}, bf16[3,1,128,512]{3,2,1,0:T(8,128)(2,1)S(1)}, u32[]{:S(2)}, u32[]{:S(2)}) collective-permute-start(bf16[3,1,128,512]{3,2,1,0:T(8,128)(2,1)S(1)} %pad_maximum_fusion.4), channel_id=1, source_target_pairs={{1,0},{2,1},{3,2},{4,3},{5,4},{6,5},{7,6},{8,7},{9,8},{10,9},{11,1... | collective-permute-start | bytes 1179656 | tf_op jit(solution)/shard_map/ppermute | solution.py:16
  16.4 9.9 %collective-permute-start.2 = (bf16[3,1,128,512]{3,2,1,0:T(8,128)(2,1)S(1)}, bf16[3,1,128,512]{3,2,1,0:T(8,128)(2,1)S(1)}, u32[]{:S(2)}, u32[]{:S(2)}) collective-permute-start(bf16[3,1,128,512]{3,2,1,0:T(8,128)(2,1)S(1)} %pad_maximum_fusion.4), channel_id=1, source_target_pairs={{0,1},{1,2},{2,3},{3,4},{4,5},{5,6},{6,7},{7,8},{8,9},{9,10},{10,1... | collective-permute-start | bytes 1179656 | tf_op jit(solution)/shard_map/ppermute | solution.py:14
  19.2 9.3 %copy-start.3 = (bf16[512,512]{1,0:T(8,128)(2,1)S(1)}, bf16[512,512]{1,0:T(8,128)(2,1)}, u32[]{:S(2)}) copy-start(bf16[512,512]{1,0:T(8,128)(2,1)} %param.28) | copy-start | bytes 1572868
  28.5 50.5 %copy-start.14 = (f32[1,1,128]{2,1,0:T(1,128)S(1)}, f32[1,1,128]{2,1,0:T(1,128)}, u32[]{:S(2)}) copy-start(f32[1,1,128]{2,1,0:T(1,128)} %param.25) | copy-start | bytes 1540
  28.5 3.2 copy-start.10
  34.0 3.2 copy-start.10
  40.4 3.2 copy-start.10
  46.9 3.2 copy-start.10
  53.3 3.2 copy-start.10
  59.7 3.2 copy-start.10
  66.2 3.2 copy-start.10
  72.6 3.2 copy-start.10
  79.0 2.6 copy-start.13
  81.6 1.5 copy-start.9
  81.6 2.5 copy-start.1
  83.2 1.0 copy-start.11
  137.7 11.8 %collective-permute-start.5 = (bf16[1,3,128,512]{3,2,1,0:T(8,128)(2,1)S(1)}, bf16[1,3,128,512]{3,2,1,0:T(8,128)(2,1)S(1)}, u32[]{:S(2)}, u32[]{:S(2)}) collective-permute-start(bf16[1,3,128,512]{3,2,1,0:T(8,128)(2,1)S(1)} %get-tuple-element.488), channel_id=1, source_target_pairs={{32,0},{64,32},{96,64},{128,96},{160,128},{192,160},{224,192},{0,2... | collective-permute-start | bytes 1179656 | tf_op jit(solution)/shard_map/ppermute | solution.py:16
  143.4 7.8 %copy-start.7 = (f32[1,1,128,512]{3,2,1,0:T(8,128)S(1)}, f32[1,1,128,512]{3,2,1,0:T(8,128)}, u32[]{:S(2)}) copy-start(f32[1,1,128,512]{3,2,1,0:T(8,128)} %param.19) | copy-start | bytes 786436
  143.4 20.4 %copy-start.4 = (f32[128,512]{1,0:T(8,128)S(1)}, f32[128,512]{1,0:T(8,128)}, u32[]{:S(2)}) copy-start(f32[128,512]{1,0:T(8,128)} %get-tuple-element.374) | copy-start | bytes 786436
  143.4 20.4 %copy-start.6 = (f32[1,1,128,512]{3,2,1,0:T(8,128)S(1)}, f32[1,1,128,512]{3,2,1,0:T(8,128)}, u32[]{:S(2)}) copy-start(f32[1,1,128,512]{3,2,1,0:T(8,128)} %param.20) | copy-start | bytes 786436
  143.4 20.4 %copy-start.12 = (bf16[128,512]{1,0:T(8,128)(2,1)S(1)}, bf16[128,512]{1,0:T(8,128)(2,1)}, u32[]{:S(2)}) copy-start(bf16[128,512]{1,0:T(8,128)(2,1)} %copy-done.11) | copy-start | bytes 393220
  143.4 20.4 %copy-start.15 = (f32[128,512]{1,0:T(8,128)S(1)}, f32[128,512]{1,0:T(8,128)}, u32[]{:S(2)}) copy-start(f32[128,512]{1,0:T(8,128)} %fusion.30) | copy-start | bytes 786436
  143.4 6.1 %collective-permute-start.4 = (bf16[1,3,128,512]{3,2,1,0:T(8,128)(2,1)S(1)}, bf16[1,3,128,512]{3,2,1,0:T(8,128)(2,1)S(1)}, u32[]{:S(2)}, u32[]{:S(2)}) collective-permute-start(bf16[1,3,128,512]{3,2,1,0:T(8,128)(2,1)S(1)} %get-tuple-element.487), channel_id=1, source_target_pairs={{0,32},{32,64},{64,96},{96,128},{128,160},{160,192},{192,224},{224... | collective-permute-start | bytes 1179656 | tf_op jit(solution)/shard_map/ppermute | solution.py:14
  149.6 11.2 %collective-permute-start.7 = (bf16[5,1,128,512]{3,2,1,0:T(8,128)(2,1)S(1)}, bf16[5,1,128,512]{3,2,1,0:T(8,128)(2,1)S(1)}, u32[]{:S(2)}, u32[]{:S(2)}) collective-permute-start(bf16[5,1,128,512]{3,2,1,0:T(8,128)(2,1)S(1)} %get-tuple-element.486), channel_id=1, source_target_pairs={{1,0},{2,1},{3,2},{4,3},{5,4},{6,5},{7,6},{8,7},{9,8},{10,9},{11,1... | collective-permute-start | bytes 1966088 | tf_op jit(solution)/shard_map/ppermute | solution.py:16
  149.7 14.1 %collective-permute-start.6 = (bf16[5,1,128,512]{3,2,1,0:T(8,128)(2,1)S(1)}, bf16[5,1,128,512]{3,2,1,0:T(8,128)(2,1)S(1)}, u32[]{:S(2)}, u32[]{:S(2)}) collective-permute-start(bf16[5,1,128,512]{3,2,1,0:T(8,128)(2,1)S(1)} %get-tuple-element.485), channel_id=1, source_target_pairs={{0,1},{1,2},{2,3},{3,4},{4,5},{5,6},{6,7},{7,8},{8,9},{9,10},{10,1... | collective-permute-start | bytes 1966088 | tf_op jit(solution)/shard_map/ppermute | solution.py:14
  250.3 77.5 %copy-start.8 = (f32[1,1,128,512]{3,2,1,0:T(8,128)}, f32[1,1,128,512]{3,2,1,0:T(8,128)S(1)}, u32[]{:S(2)}) copy-start(f32[1,1,128,512]{3,2,1,0:T(8,128)S(1)} %get-tuple-element.482) | copy-start | bytes 786436
where the time goes:
time: 330 us; the launch traced here: 328 us
  blocking collectives  156 us (47%)
  matrix products  89.8 us (27%)
  waiting for transfers between devices  26.6 us (8%)
  local copies, waits for them, and re-layouts  24.8 us (8%)
  starting transfers between devices  19 us (6%)
  other arithmetic  7.64 us (2%)
  between operations  3.44 us (1%)
    psum x1, blocking collectives, body(): lax.psum((jnp.sum(residual * residual), jnp.sum(direction * product)), ('...  81.7 us
    psum x1, blocking collectives, body(): norm_next = lax.psum(jnp.sum(new_residual * new_residual), ('lat', 'lon'))  74.4 us
    dot_general x24, matrix products, collect(): lax.dot_general(picker, values, (((0,), (0,)), ((), ())), preferred_eleme...  44.3 us
    ppermute x4, waiting for transfers between devices, padded(): lax.ppermute(head, axis, [((i + 1) % count, i) for i in range(count)])  18.4 us
    ppermute x4, starting transfers between devices, padded(): lax.ppermute(head, axis, [((i + 1) % count, i) for i in range(count)])  16.8 us
    dot_general x11, matrix products, dot_back(): lax.dot_general(left, weight, (((1,), (1,)), ((), ())), preferred_element...  16.4 us
    dot_general x8, matrix products, tangent_block(): jnp.dot(pick_send, sender_table, preferred_element_type=jnp.float32)  13.2 us
    dynamic_slice x16, local copies, waits for them, and re-layouts, pickers(): sends = lax.dynamic_slice_in_dim(send_flat, start, 128)  12.5 us
  transfers between devices with their start and end apart: 8, of which 6 were waited for; matrix products, arithmetic and copies ran while one was open for 1% of the time, Pallas kernels for 0%

commit v1 on v0

v1 whole, which is shorter than its diff:
```python
import jax
import jax.numpy as jnp
from jax import lax
from jax.experimental import pallas as pl
from jax.experimental.pallas import tpu as pltpu
from jax.sharding import PartitionSpec as P

BF = jnp.bfloat16
F32 = jnp.float32
ORDER = (0, 2, 6, 8, 1, 7, 3, 5, 4)
VMEM_LIMIT = 12 * 1024 * 1024


def dot(left, right):
    return jnp.dot(left, right, preferred_element_type=F32)


def dot_back(left, weight):
    return lax.dot_general(left, weight, (((1,), (1,)), ((), ())), preferred_element_type=F32)


def silu_slope(value):
    sig = 0.5 * jnp.tanh(0.5 * value) + 0.5
    return sig * (1.0 + value * (1.0 - sig))


def call(kernel, name, out_shape, *args):
    spec = pl.BlockSpec(memory_space=pltpu.VMEM)
    return pl.pallas_call(
        kernel,
        out_shape=out_shape,
        in_specs=[spec] * len(args),
        out_specs=jax.tree.map(lambda _: spec, out_shape),
        compiler_params=pltpu.CompilerParams(vmem_limit_bytes=VMEM_LIMIT),
        name=name,
    )(*args)


def shape(rows, cols, kind):
    return jax.ShapeDtypeStruct((rows, cols), kind)


def send_kernel(d_ref, w_ref, out_ref):
    out_ref[...] = dot(d_ref[...].astype(BF), w_ref[...]).astype(BF)


def pick_kernel(act, send_col, send_row, recv_col, recv_row, slope, pick, pick_t):
    edges = act.shape[0]
    nodes = 128
    slope[...] = silu_slope(act[...].astype(F32))
    lanes = lax.broadcasted_iota(jnp.int32, (edges, nodes), 1)
    rows = lax.broadcasted_iota(jnp.int32, (nodes, edges), 0)
    s_col = jnp.broadcast_to(send_col[...], (edges, nodes)) - lanes
    s_row = jnp.broadcast_to(send_row[...], (nodes, edges)) - rows
    for k, b in enumerate(ORDER):
        pick[:, k * nodes : (k + 1) * nodes] = jnp.where(s_col == b * nodes, 1.0, 0.0).astype(BF)
        pick_t[k * nodes : (k + 1) * nodes, :] = jnp.where(s_row == b * nodes, 1.0, 0.0).astype(BF)
    k = len(ORDER)
    r_col = jnp.broadcast_to(recv_col[...], (edges, nodes))
    r_row = jnp.broadcast_to(recv_row[...], (nodes, edges))
    pick[:, k * nodes :] = jnp.where(r_col == lanes, 1.0, 0.0).astype(BF)
    pick_t[k * nodes :, :] = jnp.where(r_row == rows, 1.0, 0.0).astype(BF)


def base_kernel(
    d, own, north, south, west, east, pick, a_node, w_recv, w_self, w_edge, w_msg,
    base, node_slope, self_pre, fold, table,
):
    d_bf = d[...].astype(BF)
    for k, part in enumerate((north, south, west, east, own)):
        table[k * 128 : (k + 1) * 128, :] = part[...]
    table[5 * 128 :, :] = dot(d_bf, w_recv[...]).astype(BF)
    base[...] = dot(pick[:, 512:], table[...])
    node_slope[...] = silu_slope(a_node[...].astype(F32))
    self_pre[...] = dot(d_bf, w_self[...])
    fold[...] = dot(w_edge[...], w_msg[...]).astype(BF)


def main_kernel(
    nw, ne, sw, se, base, slope, pick, pick_t, d, node_slope, self_pre, fold, w_out, obs,
    to_north, to_south, edge_grad, node_grad, observed, table,
):
    for k, part in enumerate((nw, ne, sw, se)):
        table[k * 128 : (k + 1) * 128, :] = part[...]
    gathered = base[...] + dot(pick[:, :512], table[...])
    hidden = (slope[...] * gathered).astype(BF)
    hidden_sum = dot(pick_t[1152:, :], hidden).astype(BF)
    pre_node = self_pre[...] + dot(hidden_sum, fold[...])
    node_hidden = (node_slope[...] * pre_node).astype(BF)
    changed = d[...] + dot(node_hidden, w_out[...])
    seen = obs[...] * changed
    observed[...] = seen
    grad = (dot_back(seen.astype(BF), w_out[...]) * node_slope[...]).astype(BF)
    node_grad[...] = grad
    edge_back = dot_back(grad, fold[...]).astype(BF)
    e_grad = (dot(pick[:, 1152:], edge_back) * slope[...]).astype(BF)
    edge_grad[...] = e_grad
    sums = dot(pick_t[:768, :], e_grad).astype(BF)
    to_north[0:128, :] = sums[0:128, :]
    to_north[128:256, :] = sums[512:640, :]
    to_north[256:384, :] = sums[128:256, :]
    to_south[0:128, :] = sums[256:384, :]
    to_south[128:256, :] = sums[640:768, :]
    to_south[256:384, :] = sums[384:512, :]


def rest_kernel(edge_grad, pick_t, node_grad, observed, d, w_recv, w_self, mid, partial):
    sums = dot(pick_t[768:, :], edge_grad[...])
    mid[...] = sums[:384, :]
    back = dot_back(node_grad[...], w_self[...]) + dot_back(sums[384:, :].astype(BF), w_recv[...])
    partial[...] = d[...] + observed[...] + back


def merge_kernel(mid, from_north, from_south, to_west, to_east, center):
    def both(rows):
        return from_north[rows, :].astype(F32) + from_south[rows, :].astype(F32)

    to_west[...] = (mid[0:128, :] + both(pl.ds(0, 128))).astype(BF)
    to_east[...] = (mid[128:256, :] + both(pl.ds(256, 128))).astype(BF)
    center[...] = mid[256:384, :] + both(pl.ds(128, 128))


def product_kernel(center, from_west, from_east, partial, w_send, d, r, product, sums):
    total = center[...] + from_west[...].astype(F32) + from_east[...].astype(F32)
    prod = partial[...] + dot_back(total.astype(BF), w_send[...])
    product[...] = prod
    res = r[...]
    lane = lax.broadcasted_iota(jnp.int32, sums.shape, 1)
    out = jnp.zeros(sums.shape, F32)
    for k, value in enumerate((res * res, d[...] * prod, res * prod, prod * prod)):
        out = jnp.where(lane == k, jnp.sum(value), out)
    sums[...] = out


def final_kernel(sums, x, r, d, product, new_x, new_r, new_d):
    total = jnp.sum(sums[...], axis=0, keepdims=True)
    norm_now, curvature = total[:, 0:1], total[:, 1:2]
    cross, square = total[:, 2:3], total[:, 3:4]
    alpha = norm_now / curvature
    norm_next = jnp.maximum(norm_now + alpha * (alpha * square - 2.0 * cross), 0.0)
    beta = norm_next / norm_now
    search = d[...]
    new_x[...] = x[...] + alpha * search
    left = r[...] - alpha * product[...]
    new_r[...] = left
    new_d[...] = left + beta * search


def shifted(value, axis, step):
    count = lax.axis_size(axis)
    return lax.ppermute(value, axis, [(i, (i + step) % count) for i in range(count)])


def total_rows(value, axis):
    return lax.all_to_all(value, axis, 0, 0, tiled=True)


def body(
    x_field, residual, direction, a_node, a_edge, senders, receivers, obs_weight,
    w_send, w_recv, w_edge_out, w_node_self, w_node_msg, w_node_out,
):
    nodes, width = x_field.shape[2:]
    edges = a_edge.shape[2]
    x = x_field.reshape(nodes, width)
    r = residual.reshape(nodes, width)
    d = direction.reshape(nodes, width)
    own = call(send_kernel, "send_term", shape(nodes, width, BF), d, w_send)
    west = shifted(own, "lon", 1)
    east = shifted(own, "lon", -1)
    north = shifted(own, "lat", 1)
    south = shifted(own, "lat", -1)
    slope, pick, pick_t = call(
        pick_kernel,
        "pickers",
        (shape(edges, width, F32), shape(edges, 10 * nodes, BF), shape(10 * nodes, edges, BF)),
        a_edge.reshape(edges, width),
        senders.reshape(edges, 1),
        senders.reshape(1, edges),
        receivers.reshape(edges, 1),
        receivers.reshape(1, edges),
    )
    nw = shifted(west, "lat", 1)
    ne = shifted(east, "lat", 1)
    sw = shifted(west, "lat", -1)
    se = shifted(east, "lat", -1)

    spec = pl.BlockSpec(memory_space=pltpu.VMEM)
    params = pltpu.CompilerParams(vmem_limit_bytes=VMEM_LIMIT)
    base, node_slope, self_pre, fold = pl.pallas_call(
        base_kernel,
        out_shape=(
            shape(edges, width, F32),
            shape(nodes, width, F32),
            shape(nodes, width, F32),
            shape(width, width, BF),
        ),
        in_specs=[spec] * 12,
        out_specs=(spec,) * 4,
        scratch_shapes=[pltpu.VMEM((6 * nodes, width), BF)],
        compiler_params=params,
        name="base",
    )(
        d, own, north, south, west, east, pick, a_node.reshape(nodes, width),
        w_recv, w_node_self, w_edge_out, w_node_msg,
    )
    to_north, to_south, edge_grad, node_grad, observed = pl.pallas_call(
        main_kernel,
        out_shape=(
            shape(3 * nodes, width, BF),
            shape(3 * nodes, width, BF),
            shape(edges, width, BF),
            shape(nodes, width, BF),
            shape(nodes, width, F32),
        ),
        in_specs=[spec] * 14,
        out_specs=(spec,) * 5,
        scratch_shapes=[pltpu.VMEM((4 * nodes, width), BF)],
        compiler_params=params,
        name="main",
    )(
        nw, ne, sw, se, base, slope, pick, pick_t, d, node_slope, self_pre, fold, w_node_out,
        obs_weight.reshape(nodes, 1),
    )
    from_south = shifted(to_north, "lat", -1)
    from_north = shifted(to_south, "lat", 1)
    mid, partial = call(
        rest_kernel,
        "rest",
        (shape(3 * nodes, width, F32), shape(nodes, width, F32)),
        edge_grad, pick_t, node_grad, observed, d, w_recv, w_node_self,
    )
    to_west, to_east, center = call(
        merge_kernel,
        "merge",
        (shape(nodes, width, BF), shape(nodes, width, BF), shape(nodes, width, F32)),
        mid, from_north, from_south,
    )
    from_east = shifted(to_west, "lon", -1)
    from_west = shifted(to_east, "lon", 1)
    n_lat, n_lon = lax.axis_size("lat"), lax.axis_size("lon")
    product, sums = call(
        product_kernel,
        "product",
        (shape(nodes, width, F32), shape(n_lat, 128, F32)),
        center, from_west, from_east, partial, w_send, d, r,
    )
    band = jnp.sum(total_rows(sums, "lat"), axis=0, keepdims=True)
    every = total_rows(jnp.broadcast_to(band, (n_lon, 128)), "lon")
    outs = call(
        final_kernel, "final", (shape(nodes, width, F32),) * 3, every, x, r, d, product
    )
    return tuple(out.reshape(x_field.shape) for out in outs)


def solution(mesh):
    field = P("lat", "lon", None, None)
    flat = P("lat", "lon", None)
    return jax.shard_map(
        body,
        mesh=mesh,
        in_specs=(field,) * 5 + (flat,) * 3 + (P(),) * 6,
        out_specs=(field,) * 3,
        check_vma=False,
    )
```

time: 330 us -> 82 us (0.25)
  blocking collectives: 156 us -> 24.2 us
  matrix products: 89.8 us -> 0 us
  waiting for transfers between devices: 26.6 us -> 11.8 us
  local copies, waits for them, and re-layouts: 24.8 us -> 10.7 us
  Pallas kernels: 0 us -> 11.6 us
  other arithmetic: 7.64 us -> 0.03 us
    psum x2 -> x0, blocking collectives: 156 us -> none  [the longest x1 81.7 us: body(): lax.psum((jnp.sum(residual * residual), jnp.sum(direction * product)), ('...]
    dot_general x55 -> x0, matrix products: 89.8 us -> none  [the longest x24 44.3 us: collect(): lax.dot_general(picker, values, (((0,), (0,)), ((), ())), preferred_eleme...]
    dynamic_slice x32 -> x0, local copies, waits for them, and re-layouts: 24.7 us -> none  [the longest x16 12.5 us: pickers(): sends = lax.dynamic_slice_in_dim(send_flat, start, 128)]
    all_to_all x0 -> x2, blocking collectives: none -> 24.2 us  [total_rows(): return lax.all_to_all(value, axis, 0, 0, tiled=True)]
    ppermute x8 -> x12, waiting for transfers between devices: 26.6 us -> 11.8 us  [shifted(): lax.ppermute(value, axis, [(i, (i + step) % count) for i in range(count)])]
    pallas_call x0 -> x8, Pallas kernels: none -> 11.6 us  [the longest x6 5.27 us: call(): pl.pallas_call(kernel, out_shape=out_shape, in_specs=[spec] * len(args),...]
    unnamed x30 -> x34, local copies, waits for them, and re-layouts: 0.07 us -> 8.11 us
    ppermute x8 -> x12, starting transfers between devices: 19 us -> 22.2 us  [shifted(): lax.ppermute(value, axis, [(i, (i + step) % count) for i in range(count)])]
  transfers between devices with their start and end apart: 8 -> 12, of which waited for: 6 -> 4; matrix products, arithmetic and copies ran while one was open for 1% -> 3% of each run, Pallas kernels for 0% -> 7%
where the time goes in v1:
time: 82 us; the launch traced here: 81.4 us
  blocking collectives  24.2 us (30%)
  starting transfers between devices  22.2 us (27%)
  waiting for transfers between devices  11.8 us (14%)
  Pallas kernels  11.6 us (14%)
  local copies, waits for them, and re-layouts  10.7 us (13%)
  between operations  0.84 us (1%)
    all_to_all x2, blocking collectives, total_rows(): return lax.all_to_all(value, axis, 0, 0, tiled=True)  24.2 us
    ppermute x12, starting transfers between devices, shifted(): lax.ppermute(value, axis, [(i, (i + step) % count) for i in range(count)])  22.2 us
    ppermute x12, waiting for transfers between devices, shifted(): lax.ppermute(value, axis, [(i, (i + step) % count) for i in range(count)])  11.8 us
    unnamed x34, local copies, waits for them, and re-layouts  8.11 us
    pallas_call x6, Pallas kernels, call(): pl.pallas_call(kernel, out_shape=out_shape, in_specs=[spec] * len(args),...  5.27 us
    pallas_call x1, Pallas kernels, body(): pl.pallas_call(main_kernel, out_shape=(shape(3 * nodes, width, BF), shape...  3.76 us
    pallas_call x1, Pallas kernels, body(): pl.pallas_call(base_kernel, out_shape=(shape(edges, width, F32), shape(no...  2.55 us
  transfers between devices with their start and end apart: 12, of which 4 were waited for; matrix products, arithmetic and copies ran while one was open for 3% of the time, Pallas kernels for 7%

profile of v1, /device:TPU:1, one launch (start us, length us, event | category | flops | bytes accessed | tf_op | source)
XLA Modules:
  0.0 81.4 jit_solution(11113961088205060578)
XLA Ops:
  0.6 0.0 copy-start
  0.6 0.9 %copy-done = f32[1,1,128,512]{3,2,1,0:T(8,128)S(1)} copy-done((f32[1,1,128,512]{3,2,1,0:T(8,128)S(1)}, f32[1,1,128,512]{3,2,1,0:T(8,128)}, u32[]{:S(2)}) %copy-start) | copy-done | bytes 262168
  1.6 0.0 copy-start.2
  1.6 1.0 %copy-done.2 = bf16[512,512]{1,0:T(8,128)(2,1)S(1)} copy-done((bf16[512,512]{1,0:T(8,128)(2,1)S(1)}, bf16[512,512]{1,0:T(8,128)(2,1)}, u32[]{:S(2)}) %copy-start.2) | copy-done | bytes 524312
  2.6 0.0 copy-start.1
  2.6 0.0 copy-start.4
  2.6 0.0 copy-start.9
  2.6 0.2 send_term.1.own
  2.9 8.7 %collective-permute-start.2 = (bf16[128,512]{1,0:T(8,128)(2,1)S(1)}, bf16[128,512]{1,0:T(8,128)(2,1)}, u32[]{:S(2)}, u32[]{:S(2)}) collective-permute-start(bf16[128,512]{1,0:T(8,128)(2,1)S(1)} %send_term.1.own), channel_id=1, source_target_pairs={{0,31},{1,0},{2,1},{3,2},{4,3},{5,4},{6,5},{7,6},{8,7},{9,8},{10,9... | collective-permute-start | bytes 393224 | tf_op jit(solution)/shard_map/ppermute | solution.py:151
  11.5 0.0 collective-permute-start
  11.6 1.0 %collective-permute-start.7 = (bf16[128,512]{1,0:T(8,128)(2,1)S(1)}, bf16[128,512]{1,0:T(8,128)(2,1)S(1)}, u32[]{:S(2)}, u32[]{:S(2)}) collective-permute-start(bf16[128,512]{1,0:T(8,128)(2,1)S(1)} %send_term.1.own), channel_id=1, source_target_pairs={{0,224},{32,0},{64,32},{96,64},{128,96},{160,128},{192,160},{224,1... | collective-permute-start | bytes 393224 | tf_op jit(solution)/shard_map/ppermute | solution.py:151
  12.5 1.2 %collective-permute-start.6 = (bf16[128,512]{1,0:T(8,128)(2,1)S(1)}, bf16[128,512]{1,0:T(8,128)(2,1)}, u32[]{:S(2)}, u32[]{:S(2)}) collective-permute-start(bf16[128,512]{1,0:T(8,128)(2,1)S(1)} %send_term.1.own), channel_id=1, source_target_pairs={{0,32},{32,64},{64,96},{96,128},{128,160},{160,192},{192,224},{224... | collective-permute-start | bytes 393224 | tf_op jit(solution)/shard_map/ppermute | solution.py:151
  13.7 0.0 collective-permute-done.2.east
  13.7 1.5 %collective-permute-start.5 = (bf16[128,512]{1,0:T(8,128)(2,1)}, bf16[128,512]{1,0:T(8,128)(2,1)S(1)}, u32[]{:S(2)}, u32[]{:S(2)}) collective-permute-start(bf16[128,512]{1,0:T(8,128)(2,1)} %collective-permute-done.2.east), channel_id=1, source_target_pairs={{0,224},{32,0},{64,32},{96,64},{128,96},{160,128},{192,160},{224,1... | collective-permute-start | bytes 393224 | tf_op jit(solution)/shard_map/ppermute | solution.py:151
  15.3 1.2 %collective-permute-start.3 = (bf16[128,512]{1,0:T(8,128)(2,1)}, bf16[128,512]{1,0:T(8,128)(2,1)S(1)}, u32[]{:S(2)}, u32[]{:S(2)}) collective-permute-start(bf16[128,512]{1,0:T(8,128)(2,1)} %collective-permute-done.2.east), channel_id=1, source_target_pairs={{0,32},{32,64},{64,96},{96,128},{128,160},{160,192},{192,224},{224... | collective-permute-start | bytes 393224 | tf_op jit(solution)/shard_map/ppermute | solution.py:151
  16.4 2.3 %collective-permute-done.west = bf16[128,512]{1,0:T(8,128)(2,1)} collective-permute-done((bf16[128,512]{1,0:T(8,128)(2,1)S(1)}, bf16[128,512]{1,0:T(8,128)(2,1)}, u32[]{:S(2)}, u32[]{:S(2)}) %collective-permute-start) | collective-permute-done | bytes 131104 | tf_op jit(solution)/shard_map/ppermute | solution.py:151
  18.8 2.1 %collective-permute-start.4 = (bf16[128,512]{1,0:T(8,128)(2,1)}, bf16[128,512]{1,0:T(8,128)(2,1)S(1)}, u32[]{:S(2)}, u32[]{:S(2)}) collective-permute-start(bf16[128,512]{1,0:T(8,128)(2,1)} %collective-permute-done.west), channel_id=1, source_target_pairs={{0,224},{32,0},{64,32},{96,64},{128,96},{160,128},{192,160},{224,1... | collective-permute-start | bytes 393224 | tf_op jit(solution)/shard_map/ppermute | solution.py:151
  20.9 0.0 collective-permute-done.7.south
  20.9 0.0 copy-start.13
  20.9 0.7 copy-done.13
  21.6 1.2 %collective-permute-start.1 = (bf16[128,512]{1,0:T(8,128)(2,1)}, bf16[128,512]{1,0:T(8,128)(2,1)}, u32[]{:S(2)}, u32[]{:S(2)}) collective-permute-start(bf16[128,512]{1,0:T(8,128)(2,1)} %collective-permute-done.west), channel_id=1, source_target_pairs={{0,32},{32,64},{64,96},{96,128},{128,160},{160,192},{192,224},{224... | collective-permute-start | bytes 393224 | tf_op jit(solution)/shard_map/ppermute | solution.py:151
  22.7 0.8 copy.23.obs
  23.5 0.9 %copy.22.recv_col = s32[1024,1]{1,0:T(8,128)S(1)} copy(s32[1024,1]{0,1:T(1,128)} %bitcast.31) | data formatting | bytes 8192 | tf_op jit(solution)/shard_map/reshape | solution.py:179
  24.4 0.9 %copy.21.send_col = s32[1024,1]{1,0:T(8,128)S(1)} copy(s32[1024,1]{0,1:T(1,128)} %bitcast.29) | data formatting | bytes 8192 | tf_op jit(solution)/shard_map/reshape | solution.py:177
  25.3 0.0 copy-start.6
  25.3 1.2 %copy-done.6 = bf16[1,1,1024,512]{3,2,1,0:T(8,128)(2,1)S(1)} copy-done((bf16[1,1,1024,512]{3,2,1,0:T(8,128)(2,1)S(1)}, bf16[1,1,1024,512]{3,2,1,0:T(8,128)(2,1)}, u32[]{:S(2)}) %copy-start.6) | copy-done | bytes 1048600
  26.6 0.0 copy-start.15
  26.6 0.7 copy-done.15
  27.2 0.7 copy-done.16
  27.9 2.4 %pickers.1 = (f32[1024,512]{1,0:T(8,128)S(1)}, bf16[1024,1280]{1,0:T(8,128)(2,1)S(1)}, bf16[1280,1024]{1,0:T(8,128)(2,1)S(1)}) custom-call(bf16[1024,512]{1,0:T(8,128)(2,1)S(1)} %bitcast.23, s32[1024,1]{1,0:T(8,128)S(1)} %copy.21.send_col, s32[1,1024]{1,0:T(1,128)S(1)} %bitcast.30, s32[1024,1]{1,0:T(8,128)S(1)} %copy.22.recv_col, s32[1,1024]{1,0:T(1,128)S(1)} %bitcast.32), custom_call_target="tpu_custom_call" | custom-call | tf_op jit(solution)/shard_map/pickers/pallas_call | solution.py:29
  30.3 0.0 collective-permute-done.6.north
  30.3 0.0 copy-done.1
  30.3 0.0 copy-done.4
  30.3 0.0 copy-done.5
  30.3 0.0 copy-done.9
  30.3 0.0 copy-start.10
  30.4 1.0 %copy-done.10 = bf16[512,512]{1,0:T(8,128)(2,1)S(1)} copy-done((bf16[512,512]{1,0:T(8,128)(2,1)S(1)}, bf16[512,512]{1,0:T(8,128)(2,1)}, u32[]{:S(2)}) %copy-start.10) | copy-done | bytes 524312
  31.4 0.9 %copy-done.12 = bf16[1,1,128,512]{3,2,1,0:T(8,128)(2,1)S(1)} copy-done((bf16[1,1,128,512]{3,2,1,0:T(8,128)(2,1)S(1)}, bf16[1,1,128,512]{3,2,1,0:T(8,128)(2,1)}, u32[]{:S(2)}) %copy-start.12) | copy-done | bytes 131096
  32.3 0.9 %copy-done.14 = bf16[128,512]{1,0:T(8,128)(2,1)S(1)} copy-done((bf16[128,512]{1,0:T(8,128)(2,1)S(1)}, bf16[128,512]{1,0:T(8,128)(2,1)}, u32[]{:S(2)}) %copy-start.14) | copy-done | bytes 131096
  33.2 2.5 %base.1 = (f32[1024,512]{1,0:T(8,128)S(1)}, f32[128,512]{1,0:T(8,128)S(1)}, f32[128,512]{1,0:T(8,128)S(1)}, bf16[512,512]{1,0:T(8,128)(2,1)S(1)}) custom-call(f32[128,512]{1,0:T(8,128)S(1)} %bitcast.18, bf16[128,512]{1,0:T(8,128)(2,1)S(1)} %send_term.1.own, bf16[128,512]{1,0:T(8,128)(2,1)} %collective-permute-done.6.north, bf16[128,512]{1,0:T(8,128)(2,1)S(1)} %copy-done.14, ...), custom_call_target="tpu_custom_call" | custom-call | tf_op jit(solution)/shard_map/base/pallas_call | solution.py:189
  35.8 0.0 collective-permute-done.5.se
  35.8 0.0 collective-permute-done.3.ne
  35.8 0.0 collective-permute-done.4.sw
  35.8 0.0 collective-permute-done.1.nw
  35.8 0.0 copy-done.8
  35.8 3.8 %main.1 = (bf16[384,512]{1,0:T(8,128)(2,1)S(1)}, bf16[384,512]{1,0:T(8,128)(2,1)S(1)}, bf16[1024,512]{1,0:T(8,128)(2,1)S(1)}, bf16[128,512]{1,0:T(8,128)(2,1)S(1)}, f32[128,512]{1,0:T(8,128)S(1)}) custom-call(bf16[128,512]{1,0:T(8,128)(2,1)} %collective-permute-done.1.nw, bf16[128,512]{1,0:T(8,128)(2,1)S(1)} %collective-permute-done.3.ne, ...), custom_call_target="tpu_custom_call" | custom-call | tf_op jit(solution)/shard_map/main/pallas_call | solution.py:206
  39.6 0.5 collective-permute-start.8
  40.1 0.0 collective-permute-start.9
  40.1 1.1 %rest.1 = (f32[384,512]{1,0:T(8,128)S(1)}, f32[128,512]{1,0:T(8,128)S(1)}) custom-call(bf16[1024,512]{1,0:T(8,128)(2,1)S(1)} %get-tuple-element.32.edge_grad, bf16[1280,1024]{1,0:T(8,128)(2,1)S(1)} %get-tuple-element.28.pick_t, bf16[128,512]{1,0:T(8,128)(2,1)S(1)} %get-tuple-element.33.node_grad, f32[128,512]{1,0:T(8,128)S(1)} %get-tuple-element.34.observed, ...), custom_call_target="tpu_custom_call" | custom-call | tf_op jit(solution)/shard_map/rest/pallas_call | solution.py:29
  41.2 0.0 copy-start.11
  41.2 3.6 %collective-permute-done.8.from_north = bf16[384,512]{1,0:T(8,128)(2,1)S(1)} collective-permute-done((bf16[384,512]{1,0:T(8,128)(2,1)S(1)}, bf16[384,512]{1,0:T(8,128)(2,1)S(1)}, u32[]{:S(2)}, u32[]{:S(2)}) %collective-permute-start.8) | collective-permute-done | bytes 393248 | tf_op jit(solution)/shard_map/ppermute | solution.py:151
  44.8 2.6 %collective-permute-done.9.from_south = bf16[384,512]{1,0:T(8,128)(2,1)S(1)} collective-permute-done((bf16[384,512]{1,0:T(8,128)(2,1)S(1)}, bf16[384,512]{1,0:T(8,128)(2,1)S(1)}, u32[]{:S(2)}, u32[]{:S(2)}) %collective-permute-start.9) | collective-permute-done | bytes 393248 | tf_op jit(solution)/shard_map/ppermute | solution.py:151
  47.4 0.1 merge.1
  47.6 0.1 collective-permute-start.10
  47.7 4.8 %collective-permute-start.11 = (bf16[128,512]{1,0:T(8,128)(2,1)S(1)}, bf16[128,512]{1,0:T(8,128)(2,1)S(1)}, u32[]{:S(2)}, u32[]{:S(2)}) collective-permute-start(bf16[128,512]{1,0:T(8,128)(2,1)S(1)} %get-tuple-element.40), channel_id=1, source_target_pairs={{0,31},{1,0},{2,1},{3,2},{4,3},{5,4},{6,5},{7,6},{8,7},{9,8},{10,9... | collective-permute-start | bytes 393224 | tf_op jit(solution)/shard_map/ppermute | solution.py:151
  52.4 3.2 %collective-permute-done.10.from_west = bf16[128,512]{1,0:T(8,128)(2,1)S(1)} collective-permute-done((bf16[128,512]{1,0:T(8,128)(2,1)S(1)}, bf16[128,512]{1,0:T(8,128)(2,1)S(1)}, u32[]{:S(2)}, u32[]{:S(2)}) %collective-permute-start.10) | collective-permute-done | bytes 131104 | tf_op jit(solution)/shard_map/ppermute | solution.py:151
  55.6 0.0 collective-permute-done.11.from_east
  55.6 0.0 copy-done.3
  55.6 0.0 copy-done.7
  55.7 0.5 product.1
  56.1 8.9 %all_to_all.17 = f32[8,1,128]{2,1,0:T(1,128)S(1)} all-to-all(f32[8,1,128]{2,1,0:T(1,128)S(1)} %bitcast.33), channel_id=1, replica_groups=mesh['lat'=8,'lon'=32] {'lat'}, dimensions={0} | all-to-all | bytes 8192 | tf_op jit(solution)/shard_map/all_to_all | solution.py:155
  65.0 15.4 %all_to_all.18 = f32[32,1,128]{2,1,0:T(1,128)S(1)} all-to-all(f32[32,1,128]{2,1,0:T(1,128)S(1)} %broadcast_in_dim.2), channel_id=1, replica_groups=mesh['lat'=8,'lon'=32] {'lon'}, dimensions={0} | all-to-all | bytes 32768 | tf_op jit(solution)/shard_map/all_to_all | solution.py:155
  80.4 0.0 copy-done.11
  80.4 1.0 %final.1 = (f32[128,512]{1,0:T(8,128)}, f32[128,512]{1,0:T(8,128)}, f32[128,512]{1,0:T(8,128)}) custom-call(f32[32,128]{1,0:T(8,128)S(1)} %bitcast.28, f32[128,512]{1,0:T(8,128)S(1)} %bitcast.26, f32[128,512]{1,0:T(8,128)S(1)} %bitcast.25, f32[128,512]{1,0:T(8,128)S(1)} %bitcast.22, f32[128,512]{1,0:T(8,128)S(1)} %get-tuple-element.43.product), custom_call_target="tpu_custom_call" | custom-call | tf_op jit(solution)/shard_map/final/pallas_call | solution.py:29
  (9 shorter events, 0.1 us)
Async XLA Ops:
  0.6 1.0 %copy-start = (f32[1,1,128,512]{3,2,1,0:T(8,128)S(1)}, f32[1,1,128,512]{3,2,1,0:T(8,128)}, u32[]{:S(2)}) copy-start(f32[1,1,128,512]{3,2,1,0:T(8,128)} %param.16) | copy-start | bytes 786436
  1.6 1.0 %copy-start.2 = (bf16[512,512]{1,0:T(8,128)(2,1)S(1)}, bf16[512,512]{1,0:T(8,128)(2,1)}, u32[]{:S(2)}) copy-start(bf16[512,512]{1,0:T(8,128)(2,1)} %w_send.1) | copy-start | bytes 1572868
  2.6 27.7 %copy-start.1 = (f32[1,1,128,512]{3,2,1,0:T(8,128)S(1)}, f32[1,1,128,512]{3,2,1,0:T(8,128)}, u32[]{:S(2)}) copy-start(f32[1,1,128,512]{3,2,1,0:T(8,128)} %param.16) | copy-start | bytes 786436
  2.6 27.7 %copy-start.4 = (bf16[512,512]{1,0:T(8,128)(2,1)S(1)}, bf16[512,512]{1,0:T(8,128)(2,1)}, u32[]{:S(2)}) copy-start(bf16[512,512]{1,0:T(8,128)(2,1)} %w_recv.3) | copy-start | bytes 1572868
  2.6 27.7 %copy-start.5 = (bf16[512,512]{1,0:T(8,128)(2,1)S(1)}, bf16[512,512]{1,0:T(8,128)(2,1)}, u32[]{:S(2)}) copy-start(bf16[512,512]{1,0:T(8,128)(2,1)} %w_self.3) | copy-start | bytes 1572868
  2.6 27.7 %copy-start.9 = (bf16[512,512]{1,0:T(8,128)(2,1)S(1)}, bf16[512,512]{1,0:T(8,128)(2,1)}, u32[]{:S(2)}) copy-start(bf16[512,512]{1,0:T(8,128)(2,1)} %w_edge.1) | copy-start | bytes 1572868
  2.9 10.8 %collective-permute-start.2 = (bf16[128,512]{1,0:T(8,128)(2,1)S(1)}, bf16[128,512]{1,0:T(8,128)(2,1)}, u32[]{:S(2)}, u32[]{:S(2)}) collective-permute-start(bf16[128,512]{1,0:T(8,128)(2,1)S(1)} %send_term.1.own), channel_id=1, source_target_pairs={{0,31},{1,0},{2,1},{3,2},{4,3},{5,4},{6,5},{7,6},{8,7},{9,8},{10,9... | collective-permute-start | bytes 393224 | tf_op jit(solution)/shard_map/ppermute | solution.py:151
  11.5 7.2 %collective-permute-start = (bf16[128,512]{1,0:T(8,128)(2,1)S(1)}, bf16[128,512]{1,0:T(8,128)(2,1)}, u32[]{:S(2)}, u32[]{:S(2)}) collective-permute-start(bf16[128,512]{1,0:T(8,128)(2,1)S(1)} %send_term.1.own), channel_id=1, source_target_pairs={{0,1},{1,2},{2,3},{3,4},{4,5},{5,6},{6,7},{7,8},{8,9},{9,10},{10,1... | collective-permute-start | bytes 393224 | tf_op jit(solution)/shard_map/ppermute | solution.py:151
  11.6 9.3 %collective-permute-start.7 = (bf16[128,512]{1,0:T(8,128)(2,1)S(1)}, bf16[128,512]{1,0:T(8,128)(2,1)S(1)}, u32[]{:S(2)}, u32[]{:S(2)}) collective-permute-start(bf16[128,512]{1,0:T(8,128)(2,1)S(1)} %send_term.1.own), channel_id=1, source_target_pairs={{0,224},{32,0},{64,32},{96,64},{128,96},{160,128},{192,160},{224,1... | collective-permute-start | bytes 393224 | tf_op jit(solution)/shard_map/ppermute | solution.py:151
  12.5 17.8 %collective-permute-start.6 = (bf16[128,512]{1,0:T(8,128)(2,1)S(1)}, bf16[128,512]{1,0:T(8,128)(2,1)}, u32[]{:S(2)}, u32[]{:S(2)}) collective-permute-start(bf16[128,512]{1,0:T(8,128)(2,1)S(1)} %send_term.1.own), channel_id=1, source_target_pairs={{0,32},{32,64},{64,96},{96,128},{128,160},{160,192},{192,224},{224... | collective-permute-start | bytes 393224 | tf_op jit(solution)/shard_map/ppermute | solution.py:151
  13.7 22.0 %collective-permute-start.5 = (bf16[128,512]{1,0:T(8,128)(2,1)}, bf16[128,512]{1,0:T(8,128)(2,1)S(1)}, u32[]{:S(2)}, u32[]{:S(2)}) collective-permute-start(bf16[128,512]{1,0:T(8,128)(2,1)} %collective-permute-done.2.east), channel_id=1, source_target_pairs={{0,224},{32,0},{64,32},{96,64},{128,96},{160,128},{192,160},{224,1... | collective-permute-start | bytes 393224 | tf_op jit(solution)/shard_map/ppermute | solution.py:151
  15.3 20.5 %collective-permute-start.3 = (bf16[128,512]{1,0:T(8,128)(2,1)}, bf16[128,512]{1,0:T(8,128)(2,1)S(1)}, u32[]{:S(2)}, u32[]{:S(2)}) collective-permute-start(bf16[128,512]{1,0:T(8,128)(2,1)} %collective-permute-done.2.east), channel_id=1, source_target_pairs={{0,32},{32,64},{64,96},{96,128},{128,160},{160,192},{192,224},{224... | collective-permute-start | bytes 393224 | tf_op jit(solution)/shard_map/ppermute | solution.py:151
  18.8 17.0 %collective-permute-start.4 = (bf16[128,512]{1,0:T(8,128)(2,1)}, bf16[128,512]{1,0:T(8,128)(2,1)S(1)}, u32[]{:S(2)}, u32[]{:S(2)}) collective-permute-start(bf16[128,512]{1,0:T(8,128)(2,1)} %collective-permute-done.west), channel_id=1, source_target_pairs={{0,224},{32,0},{64,32},{96,64},{128,96},{160,128},{192,160},{224,1... | collective-permute-start | bytes 393224 | tf_op jit(solution)/shard_map/ppermute | solution.py:151
  20.9 0.7 copy-start.13
  21.6 14.2 %collective-permute-start.1 = (bf16[128,512]{1,0:T(8,128)(2,1)}, bf16[128,512]{1,0:T(8,128)(2,1)}, u32[]{:S(2)}, u32[]{:S(2)}) collective-permute-start(bf16[128,512]{1,0:T(8,128)(2,1)} %collective-permute-done.west), channel_id=1, source_target_pairs={{0,32},{32,64},{64,96},{96,128},{128,160},{160,192},{192,224},{224... | collective-permute-start | bytes 393224 | tf_op jit(solution)/shard_map/ppermute | solution.py:151
  25.3 1.2 %copy-start.6 = (bf16[1,1,1024,512]{3,2,1,0:T(8,128)(2,1)S(1)}, bf16[1,1,1024,512]{3,2,1,0:T(8,128)(2,1)}, u32[]{:S(2)}) copy-start(bf16[1,1,1024,512]{3,2,1,0:T(8,128)(2,1)} %param.18) | copy-start | bytes 3145732
  26.6 0.7 copy-start.15
  27.2 0.7 copy-start.16
  30.3 1.0 %copy-start.10 = (bf16[512,512]{1,0:T(8,128)(2,1)S(1)}, bf16[512,512]{1,0:T(8,128)(2,1)}, u32[]{:S(2)}) copy-start(bf16[512,512]{1,0:T(8,128)(2,1)} %w_msg.1) | copy-start | bytes 1572868
  31.4 0.9 %copy-start.12 = (bf16[1,1,128,512]{3,2,1,0:T(8,128)(2,1)S(1)}, bf16[1,1,128,512]{3,2,1,0:T(8,128)(2,1)}, u32[]{:S(2)}) copy-start(bf16[1,1,128,512]{3,2,1,0:T(8,128)(2,1)} %param.17) | copy-start | bytes 393220
  32.3 0.9 %copy-start.14 = (bf16[128,512]{1,0:T(8,128)(2,1)S(1)}, bf16[128,512]{1,0:T(8,128)(2,1)}, u32[]{:S(2)}) copy-start(bf16[128,512]{1,0:T(8,128)(2,1)} %copy-done.13) | copy-start | bytes 393220
  33.2 2.6 %copy-start.8 = (bf16[512,512]{1,0:T(8,128)(2,1)S(1)}, bf16[512,512]{1,0:T(8,128)(2,1)}, u32[]{:S(2)}) copy-start(bf16[512,512]{1,0:T(8,128)(2,1)} %w_out.1) | copy-start | bytes 1572868
  39.6 5.2 %collective-permute-start.8 = (bf16[384,512]{1,0:T(8,128)(2,1)S(1)}, bf16[384,512]{1,0:T(8,128)(2,1)S(1)}, u32[]{:S(2)}, u32[]{:S(2)}) collective-permute-start(bf16[384,512]{1,0:T(8,128)(2,1)S(1)} %get-tuple-element.36), channel_id=1, source_target_pairs={{0,32},{32,64},{64,96},{96,128},{128,160},{160,192},{192,224},{224... | collective-permute-start | bytes 1179656 | tf_op jit(solution)/shard_map/ppermute | solution.py:151
  40.1 7.4 %collective-permute-start.9 = (bf16[384,512]{1,0:T(8,128)(2,1)S(1)}, bf16[384,512]{1,0:T(8,128)(2,1)S(1)}, u32[]{:S(2)}, u32[]{:S(2)}) collective-permute-start(bf16[384,512]{1,0:T(8,128)(2,1)S(1)} %get-tuple-element.37), channel_id=1, source_target_pairs={{0,224},{32,0},{64,32},{96,64},{128,96},{160,128},{192,160},{224,1... | collective-permute-start | bytes 1179656 | tf_op jit(solution)/shard_map/ppermute | solution.py:151
  40.1 15.5 %copy-start.3 = (bf16[512,512]{1,0:T(8,128)(2,1)S(1)}, bf16[512,512]{1,0:T(8,128)(2,1)}, u32[]{:S(2)}) copy-start(bf16[512,512]{1,0:T(8,128)(2,1)} %w_send.1) | copy-start | bytes 1572868
  40.1 15.5 %copy-start.7 = (f32[1,1,128,512]{3,2,1,0:T(8,128)S(1)}, f32[1,1,128,512]{3,2,1,0:T(8,128)}, u32[]{:S(2)}) copy-start(f32[1,1,128,512]{3,2,1,0:T(8,128)} %param.15) | copy-start | bytes 786436
  41.2 39.2 %copy-start.11 = (f32[1,1,128,512]{3,2,1,0:T(8,128)S(1)}, f32[1,1,128,512]{3,2,1,0:T(8,128)}, u32[]{:S(2)}) copy-start(f32[1,1,128,512]{3,2,1,0:T(8,128)} %param.14) | copy-start | bytes 786436
  47.6 8.1 %collective-permute-start.10 = (bf16[128,512]{1,0:T(8,128)(2,1)S(1)}, bf16[128,512]{1,0:T(8,128)(2,1)S(1)}, u32[]{:S(2)}, u32[]{:S(2)}) collective-permute-start(bf16[128,512]{1,0:T(8,128)(2,1)S(1)} %get-tuple-element.39), channel_id=1, source_target_pairs={{0,1},{1,2},{2,3},{3,4},{4,5},{5,6},{6,7},{7,8},{8,9},{9,10},{10,1... | collective-permute-start | bytes 393224 | tf_op jit(solution)/shard_map/ppermute | solution.py:151
  47.7 8.0 %collective-permute-start.11 = (bf16[128,512]{1,0:T(8,128)(2,1)S(1)}, bf16[128,512]{1,0:T(8,128)(2,1)S(1)}, u32[]{:S(2)}, u32[]{:S(2)}) collective-permute-start(bf16[128,512]{1,0:T(8,128)(2,1)S(1)} %get-tuple-element.40), channel_id=1, source_target_pairs={{0,31},{1,0},{2,1},{3,2},{4,3},{5,4},{6,5},{7,6},{8,7},{9,8},{10,9... | collective-permute-start | bytes 393224 | tf_op jit(solution)/shard_map/ppermute | solution.py:151

commit v2 on v1

v2 whole, which is shorter than its diff:
```python
import jax
import jax.numpy as jnp
from jax import lax
from jax.experimental import pallas as pl
from jax.experimental.pallas import tpu as pltpu
from jax.sharding import PartitionSpec as P

BF = jnp.bfloat16
F32 = jnp.float32
ORDER = (0, 2, 6, 8, 1, 7, 3, 5, 4)
VMEM_LIMIT = 12 * 1024 * 1024


def dot(left, right):
    return jnp.dot(left, right, preferred_element_type=F32)


def dot_back(left, weight):
    return lax.dot_general(left, weight, (((1,), (1,)), ((), ())), preferred_element_type=F32)


def silu_slope(value):
    sig = 0.5 * jnp.tanh(0.5 * value) + 0.5
    return sig * (1.0 + value * (1.0 - sig))


def call(kernel, name, out_shape, args, scratch=(), hbm=False):
    here = pl.BlockSpec(memory_space=pltpu.VMEM)
    there = pl.BlockSpec(memory_space=pltpu.HBM)
    if hbm:
        args = [pltpu.with_memory_space_constraint(arg, pltpu.HBM) for arg in args]
    return pl.pallas_call(
        kernel,
        out_shape=out_shape,
        in_specs=[there if hbm else here] * len(args),
        out_specs=jax.tree.map(lambda _: here, out_shape),
        scratch_shapes=scratch,
        compiler_params=pltpu.CompilerParams(vmem_limit_bytes=VMEM_LIMIT),
        name=name,
    )(*args)


def shape(rows, cols, kind):
    return jax.ShapeDtypeStruct((rows, cols), kind)


def send_kernel(d_hbm, w_hbm, out_ref, d, w, sems):
    copies = [pltpu.make_async_copy(d_hbm, d, sems.at[0]), pltpu.make_async_copy(w_hbm, w, sems.at[1])]
    for copy in copies:
        copy.start()
    for copy in copies:
        copy.wait()
    out_ref[...] = dot(d[...].astype(BF), w[...]).astype(BF)


def prepare_kernel(
    senders, receivers, act, d_hbm, a_node_hbm, w_recv_hbm, w_self_hbm, w_edge_hbm, w_msg_hbm, w_out_hbm,
    slope, pick, pick_t, d, a_node, w_recv, w_self, w_edge, w_msg, w_out,
    send_row, recv_row, act_here, sems,
):
    pairs = (
        (senders, send_row), (receivers, recv_row), (act, act_here), (d_hbm, d), (a_node_hbm, a_node),
        (w_recv_hbm, w_recv), (w_self_hbm, w_self), (w_edge_hbm, w_edge), (w_msg_hbm, w_msg), (w_out_hbm, w_out),
    )
    copies = [pltpu.make_async_copy(a, b, sems.at[k]) for k, (a, b) in enumerate(pairs)]
    for copy in copies:
        copy.start()
    edges = act_here.shape[0]
    nodes = 128
    copies[0].wait()
    copies[1].wait()
    rows = lax.broadcasted_iota(jnp.int32, (nodes, edges), 0)
    lanes = lax.broadcasted_iota(jnp.int32, (edges, nodes), 1)
    sends = jnp.broadcast_to(send_row[...], (nodes, edges))
    recvs = jnp.broadcast_to(recv_row[...], (nodes, edges))
    s_row = sends - rows
    s_col = jnp.transpose(sends) - lanes
    r_col = jnp.transpose(recvs)
    for k, b in enumerate(ORDER):
        pick[:, k * nodes : (k + 1) * nodes] = jnp.where(s_col == b * nodes, 1.0, 0.0).astype(BF)
        pick_t[k * nodes : (k + 1) * nodes, :] = jnp.where(s_row == b * nodes, 1.0, 0.0).astype(BF)
    k = len(ORDER)
    pick[:, k * nodes :] = jnp.where(r_col == lanes, 1.0, 0.0).astype(BF)
    pick_t[k * nodes :, :] = jnp.where(recvs == rows, 1.0, 0.0).astype(BF)
    copies[2].wait()
    slope[...] = silu_slope(act_here[...].astype(F32))
    for copy in copies[3:]:
        copy.wait()


def stack_kernel(north, south, west, east, after, out):
    out[0:128, :] = west[...]
    out[128:256, :] = east[...]


def base_kernel(
    d, own, north, south, west, east, pick, a_node, w_recv, w_self, w_edge, w_msg, w_out,
    base, node_slope, self_pre, fold, gram, d_back, table,
):
    d_bf = d[...].astype(BF)
    for k, part in enumerate((north, south, west, east, own)):
        table[k * 128 : (k + 1) * 128, :] = part[...]
    table[5 * 128 :, :] = dot(d_bf, w_recv[...]).astype(BF)
    base[...] = dot(pick[:, 512:], table[...])
    node_slope[...] = silu_slope(a_node[...].astype(F32))
    self_pre[...] = dot(d_bf, w_self[...])
    fold[...] = dot(w_edge[...], w_msg[...]).astype(BF)
    gram[...] = dot_back(w_out[...], w_out[...]).astype(BF)
    d_back[...] = dot_back(d_bf, w_out[...])


def lanes_of(row, width):
    nodes = row.shape[1]
    column = jnp.transpose(jnp.broadcast_to(row, (nodes, nodes)))
    return jnp.concatenate([column] * (width // nodes), axis=1)


def main_kernel(
    from_n, from_s, base, slope, pick, pick_t, node_slope, self_pre, fold, gram, d_back, obs,
    corner_n, corner_s, edge_grad, node_grad, node_hidden, table,
):
    table[0:256, :] = from_n[...]
    table[256:512, :] = from_s[...]
    gathered = base[...] + dot(pick[:, :512], table[...])
    hidden = (slope[...] * gathered).astype(BF)
    hidden_sum = dot(pick_t[1152:, :], hidden).astype(BF)
    pre_node = self_pre[...] + dot(hidden_sum, fold[...])
    inner = (node_slope[...] * pre_node).astype(BF)
    node_hidden[...] = inner
    back = lanes_of(obs[...], inner.shape[1]) * (d_back[...] + dot(inner, gram[...]))
    grad = (back * node_slope[...]).astype(BF)
    node_grad[...] = grad
    edge_back = dot_back(grad, fold[...]).astype(BF)
    e_grad = (dot(pick[:, 1152:], edge_back) * slope[...]).astype(BF)
    edge_grad[...] = e_grad
    corner_n[...] = dot(pick_t[0:256, :], e_grad).astype(BF)
    corner_s[...] = dot(pick_t[256:512, :], e_grad).astype(BF)


def rest_kernel(
    edge_grad, pick_t, node_grad, node_hidden, obs, d, w_recv, w_self, w_out,
    middle_n, middle_s, mid, partial,
):
    sums = dot(pick_t[512:, :], edge_grad[...])
    middle_n[...] = sums[:128, :].astype(BF)
    middle_s[...] = sums[128:256, :].astype(BF)
    mid[...] = sums[256:640, :]
    search = d[...]
    changed = search + dot(node_hidden[...], w_out[...])
    observed = lanes_of(obs[...], search.shape[1]) * changed
    back = dot_back(node_grad[...], w_self[...]) + dot_back(sums[640:, :].astype(BF), w_recv[...])
    partial[...] = search + observed + back


def merge_kernel(mid, from_n, from_s, to_west, to_east):
    west, east = slice(0, 128), slice(128, 256)
    for side, out in ((west, to_west), (east, to_east)):
        out[...] = (mid[side, :] + from_n[side, :].astype(F32) + from_s[side, :].astype(F32)).astype(BF)


def product_kernel(
    mid, from_n, from_s, from_w, from_e, partial, w_send, d, r, product, sums
):
    total = mid[256:384, :]
    for part in (from_n, from_s, from_w, from_e):
        total = total + part[...].astype(F32)
    prod = partial[...] + dot_back(total.astype(BF), w_send[...])
    product[...] = prod
    res = r[...]
    lane = lax.broadcasted_iota(jnp.int32, sums.shape, 1)
    out = jnp.zeros(sums.shape, F32)
    for k, value in enumerate((res * res, d[...] * prod, res * prod, prod * prod)):
        out = jnp.where(lane == k, jnp.sum(value), out)
    sums[...] = out


def final_kernel(sums, x, r, d, product, new_x, new_r, new_d):
    total = jnp.sum(sums[...], axis=0, keepdims=True)
    norm_now, curvature = total[:, 0:1], total[:, 1:2]
    cross, square = total[:, 2:3], total[:, 3:4]
    alpha = norm_now / curvature
    norm_next = jnp.maximum(norm_now + alpha * (alpha * square - 2.0 * cross), 0.0)
    beta = norm_next / norm_now
    search = d[...]
    new_x[...] = x[...] + alpha * search
    left = r[...] - alpha * product[...]
    new_r[...] = left
    new_d[...] = left + beta * search


def shifted(value, axis, step):
    count = lax.axis_size(axis)
    return lax.ppermute(value, axis, [(i, (i + step) % count) for i in range(count)])


def sums_everywhere(value):
    n_lat, n_lon = lax.axis_size("lat"), lax.axis_size("lon")
    near = n_lon // 4
    first = [
        [(2 * y + c) * n_lon + x * near + z for c in range(2) for z in range(near)]
        for y in range(n_lat // 2)
        for x in range(4)
    ]
    second = [
        [(2 * y + c) * n_lon + x * near + z for y in range(n_lat // 2) for x in range(4)]
        for c in range(2)
        for z in range(near)
    ]
    value = lax.all_to_all(value, ("lat", "lon"), 0, 0, tiled=True, axis_index_groups=first)
    value = jnp.sum(value, axis=0, keepdims=True)
    value = jnp.broadcast_to(value, (len(second[0]), value.shape[1]))
    return lax.all_to_all(value, ("lat", "lon"), 0, 0, tiled=True, axis_index_groups=second)


def body(
    x_field, residual, direction, a_node, a_edge, senders, receivers, obs_weight,
    w_send, w_recv, w_edge_out, w_node_self, w_node_msg, w_node_out,
):
    nodes, width = x_field.shape[2:]
    edges = a_edge.shape[2]
    x = x_field.reshape(nodes, width)
    r = residual.reshape(nodes, width)
    d_hbm = direction.reshape(nodes, width)
    obs = obs_weight.reshape(1, nodes)
    field = shape(nodes, width, F32)
    block = shape(nodes, width, BF)
    weight = shape(width, width, BF)
    own = call(
        send_kernel, "send_term", block, (d_hbm, w_send), hbm=True,
        scratch=(pltpu.VMEM((nodes, width), F32), pltpu.VMEM((width, width), BF), pltpu.SemaphoreType.DMA((2,))),
    )
    north = shifted(own, "lat", 1)
    south = shifted(own, "lat", -1)
    west = shifted(own, "lon", 1)
    east = shifted(own, "lon", -1)
    slope, pick, pick_t, d, node_act, w_recv, w_self, w_edge, w_msg, w_out = call(
        prepare_kernel,
        "prepare",
        (
            shape(edges, width, F32),
            shape(edges, 10 * nodes, BF),
            shape(10 * nodes, edges, BF),
            field,
            block,
        )
        + (weight,) * 5,
        (
            senders.reshape(1, edges), receivers.reshape(1, edges), a_edge.reshape(edges, width), d_hbm,
            a_node.reshape(nodes, width), w_recv, w_node_self, w_edge_out, w_node_msg, w_node_out,
        ),
        hbm=True,
        scratch=(
            pltpu.VMEM((1, edges), jnp.int32),
            pltpu.VMEM((1, edges), jnp.int32),
            pltpu.VMEM((edges, width), BF),
            pltpu.SemaphoreType.DMA((10,)),
        ),
    )
    beside = call(stack_kernel, "stack", shape(2 * nodes, width, BF), (north, south, west, east, node_act))
    from_n = shifted(beside, "lat", 1)
    from_s = shifted(beside, "lat", -1)
    base, node_slope, self_pre, fold, gram, d_back = call(
        base_kernel,
        "base",
        (shape(edges, width, F32), field, field, weight, weight, field),
        (d, own, north, south, west, east, pick, node_act, w_recv, w_self, w_edge, w_msg, w_out),
        scratch=(pltpu.VMEM((6 * nodes, width), BF),),
    )
    corner_n, corner_s, edge_grad, node_grad, node_hidden = call(
        main_kernel,
        "main",
        (shape(2 * nodes, width, BF),) * 2 + (shape(edges, width, BF), block, block),
        (from_n, from_s, base, slope, pick, pick_t, node_slope, self_pre, fold, gram, d_back, obs),
        scratch=(pltpu.VMEM((4 * nodes, width), BF),),
    )
    from_s = shifted(corner_n, "lat", -1)
    from_n = shifted(corner_s, "lat", 1)
    middle_n, middle_s, mid, partial = call(
        rest_kernel,
        "rest",
        (block, block, shape(3 * nodes, width, F32), field),
        (edge_grad, pick_t, node_grad, node_hidden, obs, d, w_recv, w_self, w_out),
    )
    to_west, to_east = call(merge_kernel, "merge", (block,) * 2, (mid, from_n, from_s))
    from_e = shifted(to_west, "lon", -1)
    from_w = shifted(to_east, "lon", 1)
    from_s = shifted(middle_n, "lat", -1)
    from_n = shifted(middle_s, "lat", 1)
    product, sums = call(
        product_kernel,
        "product",
        (field, shape(16, 128, F32)),
        (mid, from_n, from_s, from_w, from_e, partial, w_send, d, r),
    )
    sums = sums_everywhere(sums)
    outs = call(final_kernel, "final", (field,) * 3, (sums, x, r, d, product))
    return tuple(out.reshape(x_field.shape) for out in outs)


def solution(mesh):
    field = P("lat", "lon", None, None)
    flat = P("lat", "lon", None)
    return jax.shard_map(
        body,
        mesh=mesh,
        in_specs=(field,) * 5 + (flat,) * 3 + (P(),) * 6,
        out_specs=(field,) * 3,
        check_vma=False,
    )
```

time: 82 us -> 69.9 us (0.85)
  local copies, waits for them, and re-layouts: 10.7 us -> 0.03 us
  waiting for transfers between devices: 11.8 us -> 7.84 us
  starting transfers between devices: 22.2 us -> 24.5 us
  blocking collectives: 24.2 us -> 25.3 us
    unnamed x34 -> x8, local copies, waits for them, and re-layouts: 8.11 us -> 0.02 us
    ppermute x12, waiting for transfers between devices: 11.8 us -> 7.84 us  [shifted(): lax.ppermute(value, axis, [(i, (i + step) % count) for i in range(count)])]
    reshape x3 -> x0, local copies, waits for them, and re-layouts: 2.57 us -> none  [the longest x1 0.91 us: body(): senders.reshape(edges, 1)]
    ppermute x12, starting transfers between devices: 22.2 us -> 24.5 us  [shifted(): lax.ppermute(value, axis, [(i, (i + step) % count) for i in range(count)])]
    all_to_all x2, blocking collectives: 24.2 us -> 25.3 us  [sums_everywhere(): lax.all_to_all(value, ('lat', 'lon'), 0, 0, tiled=True, axis_index_groups...]
    pallas_call x8 -> x9, Pallas kernels: 11.6 us -> 11.3 us  [call(): pl.pallas_call(kernel, out_shape=out_shape, in_specs=[there if hbm else h...]
  transfers between devices with their start and end apart: 12 -> 12, of which waited for: 4 -> 4; matrix products, arithmetic and copies ran while one was open for 3% -> 0% of each run, Pallas kernels for 7% -> 9%
where the time goes in v2:
time: 69.9 us; the launch traced here: 69.7 us
  blocking collectives  25.3 us (36%)
  starting transfers between devices  24.5 us (35%)
  Pallas kernels  11.3 us (16%)
  waiting for transfers between devices  7.84 us (11%)
  between operations  0.73 us (1%)
    all_to_all x2, blocking collectives, sums_everywhere(): lax.all_to_all(value, ('lat', 'lon'), 0, 0, tiled=True, axis_index_groups...  25.3 us
    ppermute x12, starting transfers between devices, shifted(): lax.ppermute(value, axis, [(i, (i + step) % count) for i in range(count)])  24.5 us
    pallas_call x9, Pallas kernels, call(): pl.pallas_call(kernel, out_shape=out_shape, in_specs=[there if hbm else h...  11.3 us
    ppermute x12, waiting for transfers between devices, shifted(): lax.ppermute(value, axis, [(i, (i + step) % count) for i in range(count)])  7.84 us
  transfers between devices with their start and end apart: 12, of which 4 were waited for; matrix products, arithmetic and copies ran while one was open for 0% of the time, Pallas kernels for 9%

profile of v2, /device:TPU:1, one launch (start us, length us, event | category | flops | bytes accessed | tf_op | source)
XLA Modules:
  0.0 69.7 jit_solution(11643053712895504467)
XLA Ops:
  0.6 1.4 %send_term.1.own = bf16[128,512]{1,0:T(8,128)(2,1)S(1)} custom-call(f32[128,512]{1,0:T(8,128)} %bitcast.22, bf16[512,512]{1,0:T(8,128)(2,1)} %w_send.1), custom_call_target="tpu_custom_call" | custom-call | tf_op jit(solution)/shard_map/send_term/pallas_call | solution.py:32
  2.0 8.7 %collective-permute-start.3 = (bf16[128,512]{1,0:T(8,128)(2,1)S(1)}, bf16[128,512]{1,0:T(8,128)(2,1)S(1)}, u32[]{:S(2)}, u32[]{:S(2)}) collective-permute-start(bf16[128,512]{1,0:T(8,128)(2,1)S(1)} %send_term.1.own), channel_id=1, source_target_pairs={{0,31},{1,0},{2,1},{3,2},{4,3},{5,4},{6,5},{7,6},{8,7},{9,8},{10,9... | collective-permute-start | bytes 393224 | tf_op jit(solution)/shard_map/ppermute | solution.py:193
  10.7 0.0 collective-permute-start.2
  10.7 1.0 %collective-permute-start.1 = (bf16[128,512]{1,0:T(8,128)(2,1)S(1)}, bf16[128,512]{1,0:T(8,128)(2,1)S(1)}, u32[]{:S(2)}, u32[]{:S(2)}) collective-permute-start(bf16[128,512]{1,0:T(8,128)(2,1)S(1)} %send_term.1.own), channel_id=1, source_target_pairs={{0,224},{32,0},{64,32},{96,64},{128,96},{160,128},{192,160},{224,1... | collective-permute-start | bytes 393224 | tf_op jit(solution)/shard_map/ppermute | solution.py:193
  11.7 1.2 %collective-permute-start = (bf16[128,512]{1,0:T(8,128)(2,1)S(1)}, bf16[128,512]{1,0:T(8,128)(2,1)S(1)}, u32[]{:S(2)}, u32[]{:S(2)}) collective-permute-start(bf16[128,512]{1,0:T(8,128)(2,1)S(1)} %send_term.1.own), channel_id=1, source_target_pairs={{0,32},{32,64},{64,96},{96,128},{128,160},{160,192},{192,224},{224... | collective-permute-start | bytes 393224 | tf_op jit(solution)/shard_map/ppermute | solution.py:193
  12.8 2.6 %prepare.1 = (f32[1024,512]{1,0:T(8,128)S(1)}, bf16[1024,1280]{1,0:T(8,128)(2,1)S(1)}, bf16[1280,1024]{1,0:T(8,128)(2,1)S(1)}, f32[128,512]{1,0:T(8,128)S(1)}, b...) custom-call(s32[1,1024]{1,0:T(1,128)} %bitcast.26, ...), custom_call_target="tpu_custom_call" | custom-call | tf_op jit(solution)/shard_map/prepare/pallas_call | solution.py:32
  15.5 0.0 collective-permute-done.3.east
  15.5 2.3 %collective-permute-done.2.west = bf16[128,512]{1,0:T(8,128)(2,1)S(1)} collective-permute-done((bf16[128,512]{1,0:T(8,128)(2,1)S(1)}, bf16[128,512]{1,0:T(8,128)(2,1)S(1)}, u32[]{:S(2)}, u32[]{:S(2)}) %collective-permute-start.2) | collective-permute-done | bytes 131104 | tf_op jit(solution)/shard_map/ppermute | solution.py:193
  17.8 0.0 collective-permute-done.1.south
  17.8 0.0 collective-permute-done.north
  17.9 2.1 %collective-permute-start.5 = (bf16[256,512]{1,0:T(8,128)(2,1)S(1)}, bf16[256,512]{1,0:T(8,128)(2,1)S(1)}, u32[]{:S(2)}, u32[]{:S(2)}) collective-permute-start(bf16[256,512]{1,0:T(8,128)(2,1)S(1)} %stack.1), channel_id=1, source_target_pairs={{0,224},{32,0},{64,32},{96,64},{128,96},{160,128},{192,160},{224,1... | collective-permute-start | bytes 786440 | tf_op jit(solution)/shard_map/ppermute | solution.py:193
  20.0 1.2 %collective-permute-start.4 = (bf16[256,512]{1,0:T(8,128)(2,1)S(1)}, bf16[256,512]{1,0:T(8,128)(2,1)S(1)}, u32[]{:S(2)}, u32[]{:S(2)}) collective-permute-start(bf16[256,512]{1,0:T(8,128)(2,1)S(1)} %stack.1), channel_id=1, source_target_pairs={{0,32},{32,64},{64,96},{96,128},{128,160},{160,192},{192,224},{224... | collective-permute-start | bytes 786440 | tf_op jit(solution)/shard_map/ppermute | solution.py:193
  21.2 0.0 copy-start.3
  21.2 1.8 %base.1 = (f32[1024,512]{1,0:T(8,128)S(1)}, f32[128,512]{1,0:T(8,128)S(1)}, f32[128,512]{1,0:T(8,128)S(1)}, bf16[512,512]{1,0:T(8,128)(2,1)S(1)}, bf16[512,512]{1,0:T(8,128)(2,1)S(1)}, /*index=5*/f32[128,512]{1,0:T(8,128)S(1)}) custom-call(f32[128,512]{1,0:T(8,128)S(1)} %get-tuple-element.36.d, bf16[128,512]{1,0:T(8,128)(2,1)S(1)} %send_term.1.own, ...), custom_call_target="tpu_custom_call" | custom-call | tf_op jit(solution)/shard_map/base/pallas_call | solution.py:32
  23.0 2.5 %collective-permute-done.5.from_s = bf16[256,512]{1,0:T(8,128)(2,1)S(1)} collective-permute-done((bf16[256,512]{1,0:T(8,128)(2,1)S(1)}, bf16[256,512]{1,0:T(8,128)(2,1)S(1)}, u32[]{:S(2)}, u32[]{:S(2)}) %collective-permute-start.5) | collective-permute-done | bytes 262176 | tf_op jit(solution)/shard_map/ppermute | solution.py:193
  25.5 0.0 collective-permute-done.4.from_n
  25.5 0.0 copy-done.3
  25.5 2.4 %main.1 = (bf16[256,512]{1,0:T(8,128)(2,1)S(1)}, bf16[256,512]{1,0:T(8,128)(2,1)S(1)}, bf16[1024,512]{1,0:T(8,128)(2,1)S(1)}, bf16[128,512]{1,0:T(8,128)(2,1)S(1)}, bf16[128,512]{1,0:T(8,128)(2,1)S(1)}) custom-call(bf16[256,512]{1,0:T(8,128)(2,1)S(1)} %collective-permute-done.4.from_n, bf16[256,512]{1,0:T(8,128)(2,1)S(1)} %collective-permute-done.5.from_s, ...), custom_call_target="tpu_custom_call" | custom-call | tf_op jit(solution)/shard_map/main/pallas_call | solution.py:32
  28.0 1.5 %collective-permute-start.8 = (bf16[256,512]{1,0:T(8,128)(2,1)S(1)}, bf16[256,512]{1,0:T(8,128)(2,1)S(1)}, u32[]{:S(2)}, u32[]{:S(2)}) collective-permute-start(bf16[256,512]{1,0:T(8,128)(2,1)S(1)} %get-tuple-element.57), channel_id=1, source_target_pairs={{0,32},{32,64},{64,96},{96,128},{128,160},{160,192},{192,224},{224... | collective-permute-start | bytes 786440 | tf_op jit(solution)/shard_map/ppermute | solution.py:193
  29.4 1.1 %collective-permute-start.9 = (bf16[256,512]{1,0:T(8,128)(2,1)S(1)}, bf16[256,512]{1,0:T(8,128)(2,1)S(1)}, u32[]{:S(2)}, u32[]{:S(2)}) collective-permute-start(bf16[256,512]{1,0:T(8,128)(2,1)S(1)} %get-tuple-element.58), channel_id=1, source_target_pairs={{0,224},{32,0},{64,32},{96,64},{128,96},{160,128},{192,160},{224,1... | collective-permute-start | bytes 786440 | tf_op jit(solution)/shard_map/ppermute | solution.py:193
  30.5 0.0 copy-start
  30.5 0.0 copy-start.1
  30.5 1.4 %rest.1 = (bf16[128,512]{1,0:T(8,128)(2,1)S(1)}, bf16[128,512]{1,0:T(8,128)(2,1)S(1)}, f32[384,512]{1,0:T(8,128)S(1)}, f32[128,512]{1,0:T(8,128)S(1)}) custom-call(bf16[1024,512]{1,0:T(8,128)(2,1)S(1)} %get-tuple-element.51.edge_grad, bf16[1280,1024]{1,0:T(8,128)(2,1)S(1)} %get-tuple-element.45.pick_t, bf16[128,512]{1,0:T(8,128)(2,1)S(1)} %get-tuple-element.52.node_grad, ...), custom_call_target="tpu_custom_call" | custom-call | tf_op jit(solution)/shard_map/rest/pallas_call | solution.py:32
  31.9 0.0 copy-start.2
  31.9 0.7 collective-permute-start.6
  32.6 2.3 %collective-permute-start.7 = (bf16[128,512]{1,0:T(8,128)(2,1)S(1)}, bf16[128,512]{1,0:T(8,128)(2,1)S(1)}, u32[]{:S(2)}, u32[]{:S(2)}) collective-permute-start(bf16[128,512]{1,0:T(8,128)(2,1)S(1)} %get-tuple-element.56), channel_id=1, source_target_pairs={{0,224},{32,0},{64,32},{96,64},{128,96},{160,128},{192,160},{224,1... | collective-permute-start | bytes 393224 | tf_op jit(solution)/shard_map/ppermute | solution.py:193
  34.9 0.0 collective-permute-done.8.from_n
  34.9 0.6 collective-permute-done.9.from_s
  35.5 0.1 merge.1
  35.6 0.1 collective-permute-start.10
  35.7 4.8 %collective-permute-start.11 = (bf16[128,512]{1,0:T(8,128)(2,1)S(1)}, bf16[128,512]{1,0:T(8,128)(2,1)S(1)}, u32[]{:S(2)}, u32[]{:S(2)}) collective-permute-start(bf16[128,512]{1,0:T(8,128)(2,1)S(1)} %get-tuple-element.60), channel_id=1, source_target_pairs={{0,31},{1,0},{2,1},{3,2},{4,3},{5,4},{6,5},{7,6},{8,7},{9,8},{10,9... | collective-permute-start | bytes 393224 | tf_op jit(solution)/shard_map/ppermute | solution.py:193
  40.5 0.0 collective-permute-done.6.from_n
  40.5 0.0 collective-permute-done.7.from_s
  40.5 2.3 %collective-permute-done.10.from_w = bf16[128,512]{1,0:T(8,128)(2,1)S(1)} collective-permute-done((bf16[128,512]{1,0:T(8,128)(2,1)S(1)}, bf16[128,512]{1,0:T(8,128)(2,1)S(1)}, u32[]{:S(2)}, u32[]{:S(2)}) %collective-permute-start.10) | collective-permute-done | bytes 131104 | tf_op jit(solution)/shard_map/ppermute | solution.py:193
  42.8 0.0 collective-permute-done.11.from_e
  42.8 0.0 copy-done
  42.8 0.0 copy-done.1
  42.9 0.5 product.1
  43.3 12.8 %all_to_all.17 = f32[16,1,128]{2,1,0:T(1,128)S(1)} all-to-all(f32[16,1,128]{2,1,0:T(1,128)S(1)} %bitcast.19), channel_id=1, replica_groups={{0,1,2,3,4,5,6,7,32,33,34,35,36,37,38,39},{8,9,10,11,12,13,14,15,40,41,..., dimensions={0} | all-to-all | bytes 16384 | tf_op jit(solution)/shard_map/all_to_all | solution.py:209
  56.2 12.5 %all_to_all.18 = f32[16,1,128]{2,1,0:T(1,128)S(1)} all-to-all(f32[16,1,128]{2,1,0:T(1,128)S(1)} %broadcast_in_dim.2), channel_id=1, replica_groups={{0,8,16,24,64,72,80,88,128,136,144,152,192,200,208,216},{1,9,17,25,65,7..., dimensions={0} | all-to-all | bytes 16384 | tf_op jit(solution)/shard_map/all_to_all | solution.py:212
  68.7 0.0 copy-done.2
  68.7 1.0 %final.1 = (f32[128,512]{1,0:T(8,128)}, f32[128,512]{1,0:T(8,128)}, f32[128,512]{1,0:T(8,128)}) custom-call(f32[16,128]{1,0:T(8,128)S(1)} %bitcast.18, f32[128,512]{1,0:T(8,128)S(1)} %bitcast.17, f32[128,512]{1,0:T(8,128)S(1)} %bitcast.16, f32[128,512]{1,0:T(8,128)S(1)} %get-tuple-element.36.d, f32[128,512]{1,0:T(8,128)S(1)} %get-tuple-element.63.product), custom_call_target="tpu_custom_call" | custom-call | tf_op jit(solution)/shard_map/final/pallas_call | solution.py:32
  (3 shorter events, 0.1 us)
Async XLA Ops:
  2.0 13.5 %collective-permute-start.3 = (bf16[128,512]{1,0:T(8,128)(2,1)S(1)}, bf16[128,512]{1,0:T(8,128)(2,1)S(1)}, u32[]{:S(2)}, u32[]{:S(2)}) collective-permute-start(bf16[128,512]{1,0:T(8,128)(2,1)S(1)} %send_term.1.own), channel_id=1, source_target_pairs={{0,31},{1,0},{2,1},{3,2},{4,3},{5,4},{6,5},{7,6},{8,7},{9,8},{10,9... | collective-permute-start | bytes 393224 | tf_op jit(solution)/shard_map/ppermute | solution.py:193
  10.7 7.1 %collective-permute-start.2 = (bf16[128,512]{1,0:T(8,128)(2,1)S(1)}, bf16[128,512]{1,0:T(8,128)(2,1)S(1)}, u32[]{:S(2)}, u32[]{:S(2)}) collective-permute-start(bf16[128,512]{1,0:T(8,128)(2,1)S(1)} %send_term.1.own), channel_id=1, source_target_pairs={{0,1},{1,2},{2,3},{3,4},{4,5},{5,6},{6,7},{7,8},{8,9},{9,10},{10,1... | collective-permute-start | bytes 393224 | tf_op jit(solution)/shard_map/ppermute | solution.py:193
  10.7 7.1 %collective-permute-start.1 = (bf16[128,512]{1,0:T(8,128)(2,1)S(1)}, bf16[128,512]{1,0:T(8,128)(2,1)S(1)}, u32[]{:S(2)}, u32[]{:S(2)}) collective-permute-start(bf16[128,512]{1,0:T(8,128)(2,1)S(1)} %send_term.1.own), channel_id=1, source_target_pairs={{0,224},{32,0},{64,32},{96,64},{128,96},{160,128},{192,160},{224,1... | collective-permute-start | bytes 393224 | tf_op jit(solution)/shard_map/ppermute | solution.py:193
  11.7 6.2 %collective-permute-start = (bf16[128,512]{1,0:T(8,128)(2,1)S(1)}, bf16[128,512]{1,0:T(8,128)(2,1)S(1)}, u32[]{:S(2)}, u32[]{:S(2)}) collective-permute-start(bf16[128,512]{1,0:T(8,128)(2,1)S(1)} %send_term.1.own), channel_id=1, source_target_pairs={{0,32},{32,64},{64,96},{96,128},{128,160},{160,192},{192,224},{224... | collective-permute-start | bytes 393224 | tf_op jit(solution)/shard_map/ppermute | solution.py:193
  17.9 7.7 %collective-permute-start.5 = (bf16[256,512]{1,0:T(8,128)(2,1)S(1)}, bf16[256,512]{1,0:T(8,128)(2,1)S(1)}, u32[]{:S(2)}, u32[]{:S(2)}) collective-permute-start(bf16[256,512]{1,0:T(8,128)(2,1)S(1)} %stack.1), channel_id=1, source_target_pairs={{0,224},{32,0},{64,32},{96,64},{128,96},{160,128},{192,160},{224,1... | collective-permute-start | bytes 786440 | tf_op jit(solution)/shard_map/ppermute | solution.py:193
  20.0 5.5 %collective-permute-start.4 = (bf16[256,512]{1,0:T(8,128)(2,1)S(1)}, bf16[256,512]{1,0:T(8,128)(2,1)S(1)}, u32[]{:S(2)}, u32[]{:S(2)}) collective-permute-start(bf16[256,512]{1,0:T(8,128)(2,1)S(1)} %stack.1), channel_id=1, source_target_pairs={{0,32},{32,64},{64,96},{96,128},{128,160},{160,192},{192,224},{224... | collective-permute-start | bytes 786440 | tf_op jit(solution)/shard_map/ppermute | solution.py:193
  21.2 4.3 %copy-start.3 = (f32[1,1,128]{2,1,0:T(1,128)S(1)}, f32[1,1,128]{2,1,0:T(1,128)}, u32[]{:S(2)}) copy-start(f32[1,1,128]{2,1,0:T(1,128)} %param.21) | copy-start | bytes 1540
  28.0 6.9 %collective-permute-start.8 = (bf16[256,512]{1,0:T(8,128)(2,1)S(1)}, bf16[256,512]{1,0:T(8,128)(2,1)S(1)}, u32[]{:S(2)}, u32[]{:S(2)}) collective-permute-start(bf16[256,512]{1,0:T(8,128)(2,1)S(1)} %get-tuple-element.57), channel_id=1, source_target_pairs={{0,32},{32,64},{64,96},{96,128},{128,160},{160,192},{192,224},{224... | collective-permute-start | bytes 786440 | tf_op jit(solution)/shard_map/ppermute | solution.py:193
  29.4 6.1 %collective-permute-start.9 = (bf16[256,512]{1,0:T(8,128)(2,1)S(1)}, bf16[256,512]{1,0:T(8,128)(2,1)S(1)}, u32[]{:S(2)}, u32[]{:S(2)}) collective-permute-start(bf16[256,512]{1,0:T(8,128)(2,1)S(1)} %get-tuple-element.58), channel_id=1, source_target_pairs={{0,224},{32,0},{64,32},{96,64},{128,96},{160,128},{192,160},{224,1... | collective-permute-start | bytes 786440 | tf_op jit(solution)/shard_map/ppermute | solution.py:193
  30.5 12.3 %copy-start = (bf16[512,512]{1,0:T(8,128)(2,1)S(1)}, bf16[512,512]{1,0:T(8,128)(2,1)}, u32[]{:S(2)}) copy-start(bf16[512,512]{1,0:T(8,128)(2,1)} %w_send.1) | copy-start | bytes 1572868
  30.5 12.3 %copy-start.1 = (f32[1,1,128,512]{3,2,1,0:T(8,128)S(1)}, f32[1,1,128,512]{3,2,1,0:T(8,128)}, u32[]{:S(2)}) copy-start(f32[1,1,128,512]{3,2,1,0:T(8,128)} %param.15) | copy-start | bytes 786436
  31.9 36.8 %copy-start.2 = (f32[1,1,128,512]{3,2,1,0:T(8,128)S(1)}, f32[1,1,128,512]{3,2,1,0:T(8,128)}, u32[]{:S(2)}) copy-start(f32[1,1,128,512]{3,2,1,0:T(8,128)} %param.14) | copy-start | bytes 786436
  31.9 8.6 %collective-permute-start.6 = (bf16[128,512]{1,0:T(8,128)(2,1)S(1)}, bf16[128,512]{1,0:T(8,128)(2,1)S(1)}, u32[]{:S(2)}, u32[]{:S(2)}) collective-permute-start(bf16[128,512]{1,0:T(8,128)(2,1)S(1)} %get-tuple-element.55), channel_id=1, source_target_pairs={{0,32},{32,64},{64,96},{96,128},{128,160},{160,192},{192,224},{224... | collective-permute-start | bytes 393224 | tf_op jit(solution)/shard_map/ppermute | solution.py:193
  32.6 7.9 %collective-permute-start.7 = (bf16[128,512]{1,0:T(8,128)(2,1)S(1)}, bf16[128,512]{1,0:T(8,128)(2,1)S(1)}, u32[]{:S(2)}, u32[]{:S(2)}) collective-permute-start(bf16[128,512]{1,0:T(8,128)(2,1)S(1)} %get-tuple-element.56), channel_id=1, source_target_pairs={{0,224},{32,0},{64,32},{96,64},{128,96},{160,128},{192,160},{224,1... | collective-permute-start | bytes 393224 | tf_op jit(solution)/shard_map/ppermute | solution.py:193
  35.6 7.2 %collective-permute-start.10 = (bf16[128,512]{1,0:T(8,128)(2,1)S(1)}, bf16[128,512]{1,0:T(8,128)(2,1)S(1)}, u32[]{:S(2)}, u32[]{:S(2)}) collective-permute-start(bf16[128,512]{1,0:T(8,128)(2,1)S(1)} %get-tuple-element.59), channel_id=1, source_target_pairs={{0,1},{1,2},{2,3},{3,4},{4,5},{5,6},{6,7},{7,8},{8,9},{9,10},{10,1... | collective-permute-start | bytes 393224 | tf_op jit(solution)/shard_map/ppermute | solution.py:193
  35.7 7.1 %collective-permute-start.11 = (bf16[128,512]{1,0:T(8,128)(2,1)S(1)}, bf16[128,512]{1,0:T(8,128)(2,1)S(1)}, u32[]{:S(2)}, u32[]{:S(2)}) collective-permute-start(bf16[128,512]{1,0:T(8,128)(2,1)S(1)} %get-tuple-element.60), channel_id=1, source_target_pairs={{0,31},{1,0},{2,1},{3,2},{4,3},{5,4},{6,5},{7,6},{8,7},{9,8},{10,9... | collective-permute-start | bytes 393224 | tf_op jit(solution)/shard_map/ppermute | solution.py:193

commit v3 on v2

v3 whole, which is shorter than its diff:
```python
import jax
import jax.numpy as jnp
from jax import lax
from jax.experimental import pallas as pl
from jax.experimental.pallas import tpu as pltpu
from jax.sharding import PartitionSpec as P

BF = jnp.bfloat16
F32 = jnp.float32
VMEM_LIMIT = 12 * 1024 * 1024


def dot(left, right):
    return jnp.dot(left, right, preferred_element_type=F32)


def dot_back(left, weight):
    return lax.dot_general(left, weight, (((1,), (1,)), ((), ())), preferred_element_type=F32)


def silu_slope(value):
    sig = 0.5 * jnp.tanh(0.5 * value) + 0.5
    return sig * (1.0 + value * (1.0 - sig))


def call(kernel, name, out_shape, args, scratch=(), hbm=None):
    here = pl.BlockSpec(memory_space=pltpu.VMEM)
    there = pl.BlockSpec(memory_space=pltpu.HBM)
    first = len(args) if hbm is None else hbm
    away = [pltpu.with_memory_space_constraint(arg, pltpu.HBM) for arg in args[first:]]
    return pl.pallas_call(
        kernel,
        out_shape=out_shape,
        in_specs=[here] * first + [there] * len(away),
        out_specs=jax.tree.map(lambda _: here, out_shape),
        scratch_shapes=scratch,
        compiler_params=pltpu.CompilerParams(vmem_limit_bytes=VMEM_LIMIT),
        name=name,
    )(*args[:first], *away)


def shape(rows, cols, kind):
    return jax.ShapeDtypeStruct((rows, cols), kind)


def start_all(pairs, sems):
    copies = [pltpu.make_async_copy(a, b, sems.at[k]) for k, (a, b) in enumerate(pairs)]
    for copy in copies:
        copy.start()
    return copies


def slot_blocks():
    near = 6 - 6 * lax.rem(lax.axis_index("lat"), 2)
    far = 6 - near
    return (near, near + 2, far, far + 2, near + 1, far + 1, 3, 5, 4)


def send_kernel(senders, receivers, obs_hbm, d_hbm, w_hbm, own, send_row, recv_row, obs, d, w, sems):
    pairs = ((d_hbm, d), (w_hbm, w), (senders, send_row), (receivers, recv_row), (obs_hbm, obs))
    for copy in start_all(pairs, sems):
        copy.wait()
    own[...] = dot(d[...].astype(BF), w[...]).astype(BF)


def prepare_kernel(
    send_row, recv_row, act_hbm, a_node_hbm, w_recv_hbm, w_self_hbm, w_edge_hbm, w_msg_hbm, w_out_hbm,
    pick, pick_t, act, a_node, w_recv, w_self, w_edge, w_msg, w_out, sems,
):
    pairs = (
        (act_hbm, act), (a_node_hbm, a_node), (w_recv_hbm, w_recv), (w_self_hbm, w_self),
        (w_edge_hbm, w_edge), (w_msg_hbm, w_msg), (w_out_hbm, w_out),
    )
    copies = start_all(pairs, sems)
    edges = act.shape[0]
    nodes = 128
    rows = lax.broadcasted_iota(jnp.int32, (nodes, edges), 0)
    lanes = lax.broadcasted_iota(jnp.int32, (edges, nodes), 1)
    sends = jnp.broadcast_to(send_row[...], (nodes, edges))
    recvs = jnp.broadcast_to(recv_row[...], (nodes, edges))
    s_row = sends - rows
    s_col = jnp.transpose(sends) - lanes
    r_col = jnp.transpose(recvs)
    blocks = slot_blocks()
    for k, b in enumerate(blocks):
        pick[:, k * nodes : (k + 1) * nodes] = jnp.where(s_col == b * nodes, 1.0, 0.0).astype(BF)
        pick_t[k * nodes : (k + 1) * nodes, :] = jnp.where(s_row == b * nodes, 1.0, 0.0).astype(BF)
    k = len(blocks)
    pick[:, k * nodes :] = jnp.where(r_col == lanes, 1.0, 0.0).astype(BF)
    pick_t[k * nodes :, :] = jnp.where(recvs == rows, 1.0, 0.0).astype(BF)
    for copy in copies:
        copy.wait()


def stack_kernel(west, east, near, far, after, beside, across):
    beside[0:128, :] = west[...]
    beside[128:256, :] = east[...]
    across[0:128, :] = near[...]
    across[128:256, :] = far[...]


def base_kernel(
    d, own, across, beside, pick, act, a_node, w_recv, w_self, w_edge, w_msg, w_out,
    base, slope, node_slope, self_pre, fold, gram, d_back, table,
):
    d_bf = d[...].astype(BF)
    table[0:128, :] = own[...]
    table[128:256, :] = dot(d_bf, w_recv[...]).astype(BF)
    base[...] = (
        dot(pick[:, 512:768], across[...])
        + dot(pick[:, 768:1024], beside[...])
        + dot(pick[:, 1024:1280], table[...])
    )
    slope[...] = silu_slope(act[...].astype(F32))
    node_slope[...] = silu_slope(a_node[...].astype(F32))
    self_pre[...] = dot(d_bf, w_self[...])
    fold[...] = dot(w_edge[...], w_msg[...]).astype(BF)
    gram[...] = dot_back(w_out[...], w_out[...]).astype(BF)
    d_back[...] = dot_back(d_bf, w_out[...])


def lanes_of(row, width):
    nodes = row.shape[1]
    column = jnp.transpose(jnp.broadcast_to(row, (nodes, nodes)))
    return jnp.concatenate([column] * (width // nodes), axis=1)


def main_kernel(
    from_near, from_far, base, slope, pick, pick_t, node_slope, self_pre, fold, gram, d_back, obs,
    corner_near, corner_far, edge_grad, node_grad, node_hidden,
):
    gathered = (
        base[...] + dot(pick[:, 0:256], from_near[...]) + dot(pick[:, 256:512], from_far[...])
    )
    hidden = (slope[...] * gathered).astype(BF)
    hidden_sum = dot(pick_t[1152:, :], hidden).astype(BF)
    pre_node = self_pre[...] + dot(hidden_sum, fold[...])
    inner = (node_slope[...] * pre_node).astype(BF)
    node_hidden[...] = inner
    back = lanes_of(obs[...], inner.shape[1]) * (d_back[...] + dot(inner, gram[...]))
    grad = (back * node_slope[...]).astype(BF)
    node_grad[...] = grad
    edge_back = dot_back(grad, fold[...]).astype(BF)
    e_grad = (dot(pick[:, 1152:], edge_back) * slope[...]).astype(BF)
    edge_grad[...] = e_grad
    corner_near[...] = dot(pick_t[0:256, :], e_grad).astype(BF)
    corner_far[...] = dot(pick_t[256:512, :], e_grad).astype(BF)


def rest_kernel(
    edge_grad, pick_t, node_grad, node_hidden, obs, d, w_recv, w_self, w_out,
    middle_near, middle_far, mid, partial,
):
    sums = dot(pick_t[512:, :], edge_grad[...])
    middle_near[...] = sums[:128, :].astype(BF)
    middle_far[...] = sums[128:256, :].astype(BF)
    mid[...] = sums[256:640, :]
    search = d[...]
    changed = search + dot(node_hidden[...], w_out[...])
    observed = lanes_of(obs[...], search.shape[1]) * changed
    back = dot_back(node_grad[...], w_self[...]) + dot_back(sums[640:, :].astype(BF), w_recv[...])
    partial[...] = search + observed + back


def merge_kernel(mid, from_near, from_far, to_west, to_east):
    west, east = slice(0, 128), slice(128, 256)
    for side, out in ((west, to_west), (east, to_east)):
        out[...] = (
            mid[side, :] + from_near[side, :].astype(F32) + from_far[side, :].astype(F32)
        ).astype(BF)


def product_kernel(
    mid, from_near, from_far, from_w, from_e, partial, w_send, d, r, product, sums
):
    total = mid[256:384, :]
    for part in (from_near, from_far, from_w, from_e):
        total = total + part[...].astype(F32)
    prod = partial[...] + dot_back(total.astype(BF), w_send[...])
    product[...] = prod
    res = r[...]
    lane = lax.broadcasted_iota(jnp.int32, sums.shape, 1)
    out = jnp.zeros(sums.shape, F32)
    for k, value in enumerate((res * res, d[...] * prod, res * prod, prod * prod)):
        out = jnp.where(lane == k, jnp.sum(value), out)
    sums[...] = out


def final_kernel(sums, x, r, d, product, new_x, new_r, new_d):
    total = jnp.sum(sums[...], axis=0, keepdims=True)
    norm_now, curvature = total[:, 0:1], total[:, 1:2]
    cross, square = total[:, 2:3], total[:, 3:4]
    alpha = norm_now / curvature
    norm_next = jnp.maximum(norm_now + alpha * (alpha * square - 2.0 * cross), 0.0)
    beta = norm_next / norm_now
    search = d[...]
    new_x[...] = x[...] + alpha * search
    left = r[...] - alpha * product[...]
    new_r[...] = left
    new_d[...] = left + beta * search


def shifted(value, axis, step):
    count = lax.axis_size(axis)
    return lax.ppermute(value, axis, [(i, (i + step) % count) for i in range(count)])


def swapped(value, far):
    count = lax.axis_size("lat")
    step = -1 if far else 1
    pairs = [(i, (i + (step if i % 2 == 0 else -step)) % count) for i in range(count)]
    return lax.ppermute(value, "lat", pairs)


def sums_everywhere(value):
    n_lat, n_lon = lax.axis_size("lat"), lax.axis_size("lon")
    near = n_lon // 4
    first = [
        [(2 * y + c) * n_lon + x * near + z for c in range(2) for z in range(near)]
        for y in range(n_lat // 2)
        for x in range(4)
    ]
    second = [
        [(2 * y + c) * n_lon + x * near + z for y in range(n_lat // 2) for x in range(4)]
        for c in range(2)
        for z in range(near)
    ]
    value = lax.all_to_all(value, ("lat", "lon"), 0, 0, tiled=True, axis_index_groups=first)
    value = jnp.sum(value, axis=0, keepdims=True)
    value = jnp.broadcast_to(value, (len(second[0]), value.shape[1]))
    return lax.all_to_all(value, ("lat", "lon"), 0, 0, tiled=True, axis_index_groups=second)


def body(
    x_field, residual, direction, a_node, a_edge, senders, receivers, obs_weight,
    w_send, w_recv, w_edge_out, w_node_self, w_node_msg, w_node_out,
):
    nodes, width = x_field.shape[2:]
    edges = a_edge.shape[2]
    x = x_field.reshape(nodes, width)
    r = residual.reshape(nodes, width)
    d_hbm = direction.reshape(nodes, width)
    field = shape(nodes, width, F32)
    block = shape(nodes, width, BF)
    weight = shape(width, width, BF)
    own, send_row, recv_row, obs, d = call(
        send_kernel,
        "send_term",
        (
            block,
            shape(1, edges, jnp.int32),
            shape(1, edges, jnp.int32),
            shape(1, nodes, F32),
            field,
        ),
        (senders.reshape(1, edges), receivers.reshape(1, edges), obs_weight.reshape(1, nodes), d_hbm, w_send),
        hbm=0,
        scratch=(pltpu.VMEM((width, width), BF), pltpu.SemaphoreType.DMA((5,))),
    )
    near = swapped(own, False)
    far = swapped(own, True)
    west = shifted(own, "lon", 1)
    east = shifted(own, "lon", -1)
    pick, pick_t, act, node_act, w_recv, w_self, w_edge, w_msg, w_out = call(
        prepare_kernel,
        "prepare",
        (
            shape(edges, 10 * nodes, BF),
            shape(10 * nodes, edges, BF),
            shape(edges, width, BF),
            block,
        )
        + (weight,) * 5,
        (
            send_row, recv_row, a_edge.reshape(edges, width), a_node.reshape(nodes, width),
            w_recv, w_node_self, w_edge_out, w_node_msg, w_node_out,
        ),
        hbm=2,
        scratch=(pltpu.SemaphoreType.DMA((7,)),),
    )
    pair = shape(2 * nodes, width, BF)
    beside, across = call(stack_kernel, "stack", (pair, pair), (west, east, near, far, node_act))
    from_near = swapped(beside, False)
    from_far = swapped(beside, True)
    base, slope, node_slope, self_pre, fold, gram, d_back = call(
        base_kernel,
        "base",
        (shape(edges, width, F32),) * 2 + (field, field, weight, weight, field),
        (d, own, across, beside, pick, act, node_act, w_recv, w_self, w_edge, w_msg, w_out),
        scratch=(pltpu.VMEM((2 * nodes, width), BF),),
    )
    corner_near, corner_far, edge_grad, node_grad, node_hidden = call(
        main_kernel,
        "main",
        (pair, pair, shape(edges, width, BF), block, block),
        (
            from_near, from_far, base, slope, pick, pick_t, node_slope, self_pre, fold, gram, d_back, obs,
        ),
    )
    from_near = swapped(corner_near, False)
    from_far = swapped(corner_far, True)
    middle_near, middle_far, mid, partial = call(
        rest_kernel,
        "rest",
        (block, block, shape(3 * nodes, width, F32), field),
        (edge_grad, pick_t, node_grad, node_hidden, obs, d, w_recv, w_self, w_out),
    )
    to_west, to_east = call(merge_kernel, "merge", (block, block), (mid, from_near, from_far))
    from_e = shifted(to_west, "lon", -1)
    from_w = shifted(to_east, "lon", 1)
    from_near = swapped(middle_near, False)
    from_far = swapped(middle_far, True)
    product, sums = call(
        product_kernel,
        "product",
        (field, shape(16, 128, F32)),
        (mid, from_near, from_far, from_w, from_e, partial, w_send, d, r),
    )
    sums = sums_everywhere(sums)
    outs = call(final_kernel, "final", (field,) * 3, (sums, x, r, d, product))
    return tuple(out.reshape(x_field.shape) for out in outs)


def solution(mesh):
    field = P("lat", "lon", None, None)
    flat = P("lat", "lon", None)
    return jax.shard_map(
        body,
        mesh=mesh,
        in_specs=(field,) * 5 + (flat,) * 3 + (P(),) * 6,
        out_specs=(field,) * 3,
        check_vma=False,
    )
```

time: 69.9 us -> 68.8 us (0.984)
  starting transfers between devices: 24.5 us -> 21.5 us
  blocking collectives: 25.3 us -> 26.2 us
    ppermute x12 -> x4, starting transfers between devices: 24.5 us -> 13.6 us  [shifted(): lax.ppermute(value, axis, [(i, (i + step) % count) for i in range(count)])]
    ppermute x0 -> x8, starting transfers between devices: none -> 7.87 us  [swapped(): return lax.ppermute(value, 'lat', pairs)]
    ppermute x0 -> x8, waiting for transfers between devices: none -> 6.02 us  [swapped(): return lax.ppermute(value, 'lat', pairs)]
    ppermute x12 -> x4, waiting for transfers between devices: 7.84 us -> 2.35 us  [shifted(): lax.ppermute(value, axis, [(i, (i + step) % count) for i in range(count)])]
    all_to_all x2, blocking collectives: 25.3 us -> 26.2 us  [sums_everywhere(): lax.all_to_all(value, ('lat', 'lon'), 0, 0, tiled=True, axis_index_groups...]
where the time goes in v3:
time: 68.8 us; the launch traced here: 68.6 us
  blocking collectives  26.2 us (38%)
  starting transfers between devices  21.5 us (31%)
  Pallas kernels  11.7 us (17%)
  waiting for transfers between devices  8.37 us (12%)
  between operations  0.75 us (1%)
    all_to_all x2, blocking collectives, sums_everywhere(): lax.all_to_all(value, ('lat', 'lon'), 0, 0, tiled=True, axis_index_groups...  26.2 us
    ppermute x4, starting transfers between devices, shifted(): lax.ppermute(value, axis, [(i, (i + step) % count) for i in range(count)])  13.6 us
    pallas_call x9, Pallas kernels, call(): pl.pallas_call(kernel, out_shape=out_shape, in_specs=[here] * first + [th...  11.7 us
    ppermute x8, starting transfers between devices, swapped(): return lax.ppermute(value, 'lat', pairs)  7.87 us
    ppermute x8, waiting for transfers between devices, swapped(): return lax.ppermute(value, 'lat', pairs)  6.02 us
    ppermute x4, waiting for transfers between devices, shifted(): lax.ppermute(value, axis, [(i, (i + step) % count) for i in range(count)])  2.35 us
  transfers between devices with their start and end apart: 12, of which 4 were waited for; matrix products, arithmetic and copies ran while one was open for 0% of the time, Pallas kernels for 9%

profile of v3, /device:TPU:1, one launch (start us, length us, event | category | flops | bytes accessed | tf_op | source)
XLA Modules:
  0.0 68.6 jit_solution(4650205691911364113)
XLA Ops:
  0.6 1.4 %send_term.1 = (bf16[128,512]{1,0:T(8,128)(2,1)S(1)}, s32[1,1024]{1,0:T(1,128)S(1)}, s32[1,1024]{1,0:T(1,128)S(1)}, f32[1,128]{1,0:T(1,128)S(1)}, f32[128,512]{1,0:T(8,128)S(1)}) custom-call(s32[1,1024]{1,0:T(1,128)} %bitcast.23, s32[1,1024]{1,0:T(1,128)} %bitcast.24, f32[1,128]{1,0:T(1,128)} %bitcast.25, f32[128,512]{1,0:T(8,128)} %bitcast.21, ...), custom_call_target="tpu_custom_call" | custom-call | tf_op jit(solution)/shard_map/send_term/pallas_call | solution.py:31
  2.0 2.5 %collective-permute-start = (bf16[128,512]{1,0:T(8,128)(2,1)S(1)}, bf16[128,512]{1,0:T(8,128)(2,1)S(1)}, u32[]{:S(2)}, u32[]{:S(2)}) collective-permute-start(bf16[128,512]{1,0:T(8,128)(2,1)S(1)} %get-tuple-element.42.own), channel_id=1, source_target_pairs={{0,1},{1,2},{2,3},{3,4},{4,5},{5,6},{6,7},{7,8},{8,9},{9,10},{10,1... | collective-permute-start | bytes 393224 | tf_op jit(solution)/shard_map/ppermute | solution.py:205
  4.6 6.2 %collective-permute-start.1 = (bf16[128,512]{1,0:T(8,128)(2,1)S(1)}, bf16[128,512]{1,0:T(8,128)(2,1)S(1)}, u32[]{:S(2)}, u32[]{:S(2)}) collective-permute-start(bf16[128,512]{1,0:T(8,128)(2,1)S(1)} %get-tuple-element.42.own), channel_id=1, source_target_pairs={{0,31},{1,0},{2,1},{3,2},{4,3},{5,4},{6,5},{7,6},{8,7},{9,8},{10,9... | collective-permute-start | bytes 393224 | tf_op jit(solution)/shard_map/ppermute | solution.py:205
  10.8 1.0 %collective-permute-start.2 = (bf16[128,512]{1,0:T(8,128)(2,1)S(1)}, bf16[128,512]{1,0:T(8,128)(2,1)S(1)}, u32[]{:S(2)}, u32[]{:S(2)}) collective-permute-start(bf16[128,512]{1,0:T(8,128)(2,1)S(1)} %get-tuple-element.42.own), channel_id=1, source_target_pairs={{0,32},{32,0},{64,96},{96,64},{128,160},{160,128},{192,224},{224,1... | collective-permute-start | bytes 393224 | tf_op jit(solution)/shard_map/ppermute | solution.py:212
  11.8 1.2 %collective-permute-start.3 = (bf16[128,512]{1,0:T(8,128)(2,1)S(1)}, bf16[128,512]{1,0:T(8,128)(2,1)S(1)}, u32[]{:S(2)}, u32[]{:S(2)}) collective-permute-start(bf16[128,512]{1,0:T(8,128)(2,1)S(1)} %get-tuple-element.42.own), channel_id=1, source_target_pairs={{0,224},{32,64},{64,32},{96,128},{128,96},{160,192},{192,160},{224... | collective-permute-start | bytes 393224 | tf_op jit(solution)/shard_map/ppermute | solution.py:212
  13.0 2.2 %prepare.1 = (bf16[1024,1280]{1,0:T(8,128)(2,1)S(1)}, bf16[1280,1024]{1,0:T(8,128)(2,1)S(1)}, bf16[1024,512]{1,0:T(8,128)(2,1)S(1)}, bf16[128,512]{1,0:T(8,128)(...) custom-call(s32[1,1024]{1,0:T(1,128)S(1)} %get-tuple-element.43.send, ...), custom_call_target="tpu_custom_call" | custom-call | tf_op jit(solution)/shard_map/prepare/pallas_call | solution.py:31
  15.2 0.0 collective-permute-done.west
  15.2 0.0 collective-permute-done.1.east
  15.2 0.0 collective-permute-done.2.near
  15.2 1.2 %collective-permute-done.3.far = bf16[128,512]{1,0:T(8,128)(2,1)S(1)} collective-permute-done((bf16[128,512]{1,0:T(8,128)(2,1)S(1)}, bf16[128,512]{1,0:T(8,128)(2,1)S(1)}, u32[]{:S(2)}, u32[]{:S(2)}) %collective-permute-start.3) | collective-permute-done | bytes 131104 | tf_op jit(solution)/shard_map/ppermute | solution.py:212
  16.5 1.2 %collective-permute-start.4 = (bf16[256,512]{1,0:T(8,128)(2,1)S(1)}, bf16[256,512]{1,0:T(8,128)(2,1)S(1)}, u32[]{:S(2)}, u32[]{:S(2)}) collective-permute-start(bf16[256,512]{1,0:T(8,128)(2,1)S(1)} %get-tuple-element.46.beside), channel_id=1, source_target_pairs={{0,32},{32,0},{64,96},{96,64},{128,160},{160,128},{192,224},{224,1... | collective-permute-start | bytes 786440 | tf_op jit(solution)/shard_map/ppermute | solution.py:212
  17.7 0.3 collective-permute-start.5
  18.0 2.5 %base.1 = (f32[1024,512]{1,0:T(8,128)S(1)}, f32[1024,512]{1,0:T(8,128)S(1)}, f32[128,512]{1,0:T(8,128)S(1)}, f32[128,512]{1,0:T(8,128)S(1)}, bf16[512,512]{1,0:T...) custom-call(f32[128,512]{1,0:T(8,128)S(1)} %get-tuple-element.47.d, ...), custom_call_target="tpu_custom_call" | custom-call | tf_op jit(solution)/shard_map/base/pallas_call | solution.py:31
  20.5 0.0 collective-permute-done.4.from_near
  20.5 3.2 %collective-permute-done.5.from_far = bf16[256,512]{1,0:T(8,128)(2,1)S(1)} collective-permute-done((bf16[256,512]{1,0:T(8,128)(2,1)S(1)}, bf16[256,512]{1,0:T(8,128)(2,1)S(1)}, u32[]{:S(2)}, u32[]{:S(2)}) %collective-permute-start.5) | collective-permute-done | bytes 262176 | tf_op jit(solution)/shard_map/ppermute | solution.py:212
  23.8 2.5 %main.1 = (bf16[256,512]{1,0:T(8,128)(2,1)S(1)}, bf16[256,512]{1,0:T(8,128)(2,1)S(1)}, bf16[1024,512]{1,0:T(8,128)(2,1)S(1)}, bf16[128,512]{1,0:T(8,128)(2,1)S(1)}, bf16[128,512]{1,0:T(8,128)(2,1)S(1)}) custom-call(bf16[256,512]{1,0:T(8,128)(2,1)S(1)} %collective-permute-done.4.from_near, bf16[256,512]{1,0:T(8,128)(2,1)S(1)} %collective-permute-done.5.from_far, ...), custom_call_target="tpu_custom_call" | custom-call | tf_op jit(solution)/shard_map/main/pallas_call | solution.py:31
  26.3 1.1 %collective-permute-start.8 = (bf16[256,512]{1,0:T(8,128)(2,1)S(1)}, bf16[256,512]{1,0:T(8,128)(2,1)S(1)}, u32[]{:S(2)}, u32[]{:S(2)}) collective-permute-start(bf16[256,512]{1,0:T(8,128)(2,1)S(1)} %get-tuple-element.71), channel_id=1, source_target_pairs={{0,32},{32,0},{64,96},{96,64},{128,160},{160,128},{192,224},{224,1... | collective-permute-start | bytes 786440 | tf_op jit(solution)/shard_map/ppermute | solution.py:212
  27.4 0.0 collective-permute-start.9
  27.4 0.0 copy-start
  27.4 0.0 copy-start.1
  27.4 1.4 %rest.1 = (bf16[128,512]{1,0:T(8,128)(2,1)S(1)}, bf16[128,512]{1,0:T(8,128)(2,1)S(1)}, f32[384,512]{1,0:T(8,128)S(1)}, f32[128,512]{1,0:T(8,128)S(1)}) custom-call(bf16[1024,512]{1,0:T(8,128)(2,1)S(1)} %get-tuple-element.65.edge_grad, bf16[1280,1024]{1,0:T(8,128)(2,1)S(1)} %get-tuple-element.58.pick_t, bf16[128,512]{1,0:T(8,128)(2,1)S(1)} %get-tuple-element.66.node_grad, ...), custom_call_target="tpu_custom_call" | custom-call | tf_op jit(solution)/shard_map/rest/pallas_call | solution.py:31
  28.7 0.0 copy-start.2
  28.8 3.1 %collective-permute-start.6 = (bf16[128,512]{1,0:T(8,128)(2,1)S(1)}, bf16[128,512]{1,0:T(8,128)(2,1)S(1)}, u32[]{:S(2)}, u32[]{:S(2)}) collective-permute-start(bf16[128,512]{1,0:T(8,128)(2,1)S(1)} %get-tuple-element.69), channel_id=1, source_target_pairs={{0,32},{32,0},{64,96},{96,64},{128,160},{160,128},{192,224},{224,1... | collective-permute-start | bytes 393224 | tf_op jit(solution)/shard_map/ppermute | solution.py:212
  31.9 0.0 collective-permute-start.7
  31.9 0.0 collective-permute-done.8.from_near
  31.9 1.5 %collective-permute-done.9.from_far = bf16[256,512]{1,0:T(8,128)(2,1)S(1)} collective-permute-done((bf16[256,512]{1,0:T(8,128)(2,1)S(1)}, bf16[256,512]{1,0:T(8,128)(2,1)S(1)}, u32[]{:S(2)}, u32[]{:S(2)}) %collective-permute-start.9) | collective-permute-done | bytes 262176 | tf_op jit(solution)/shard_map/ppermute | solution.py:212
  33.5 0.1 merge.1
  33.5 0.1 collective-permute-start.10
  33.6 4.8 %collective-permute-start.11 = (bf16[128,512]{1,0:T(8,128)(2,1)S(1)}, bf16[128,512]{1,0:T(8,128)(2,1)S(1)}, u32[]{:S(2)}, u32[]{:S(2)}) collective-permute-start(bf16[128,512]{1,0:T(8,128)(2,1)S(1)} %get-tuple-element.74), channel_id=1, source_target_pairs={{0,31},{1,0},{2,1},{3,2},{4,3},{5,4},{6,5},{7,6},{8,7},{9,8},{10,9... | collective-permute-start | bytes 393224 | tf_op jit(solution)/shard_map/ppermute | solution.py:205
  38.4 0.0 collective-permute-done.6.from_near
  38.4 0.0 collective-permute-done.7.from_far
  38.4 2.3 %collective-permute-done.10.from_w = bf16[128,512]{1,0:T(8,128)(2,1)S(1)} collective-permute-done((bf16[128,512]{1,0:T(8,128)(2,1)S(1)}, bf16[128,512]{1,0:T(8,128)(2,1)S(1)}, u32[]{:S(2)}, u32[]{:S(2)}) %collective-permute-start.10) | collective-permute-done | bytes 131104 | tf_op jit(solution)/shard_map/ppermute | solution.py:205
  40.8 0.0 collective-permute-done.11.from_e
  40.8 0.0 copy-done
  40.8 0.0 copy-done.1
  40.8 0.5 product.1
  41.3 11.5 %all_to_all.17 = f32[16,1,128]{2,1,0:T(1,128)S(1)} all-to-all(f32[16,1,128]{2,1,0:T(1,128)S(1)} %bitcast.19), channel_id=1, replica_groups={{0,1,2,3,4,5,6,7,32,33,34,35,36,37,38,39},{8,9,10,11,12,13,14,15,40,41,..., dimensions={0} | all-to-all | bytes 16384 | tf_op jit(solution)/shard_map/all_to_all | solution.py:228
  52.8 14.7 %all_to_all.18 = f32[16,1,128]{2,1,0:T(1,128)S(1)} all-to-all(f32[16,1,128]{2,1,0:T(1,128)S(1)} %broadcast_in_dim.2), channel_id=1, replica_groups={{0,8,16,24,64,72,80,88,128,136,144,152,192,200,208,216},{1,9,17,25,65,7..., dimensions={0} | all-to-all | bytes 16384 | tf_op jit(solution)/shard_map/all_to_all | solution.py:231
  67.5 0.0 copy-done.2
  67.5 1.0 %final.1 = (f32[128,512]{1,0:T(8,128)}, f32[128,512]{1,0:T(8,128)}, f32[128,512]{1,0:T(8,128)}) custom-call(f32[16,128]{1,0:T(8,128)S(1)} %bitcast.18, f32[128,512]{1,0:T(8,128)S(1)} %bitcast.17, f32[128,512]{1,0:T(8,128)S(1)} %bitcast.16, f32[128,512]{1,0:T(8,128)S(1)} %get-tuple-element.47.d, f32[128,512]{1,0:T(8,128)S(1)} %get-tuple-element.77.product), custom_call_target="tpu_custom_call" | custom-call | tf_op jit(solution)/shard_map/final/pallas_call | solution.py:31
  (3 shorter events, 0.1 us)
Async XLA Ops:
  2.0 13.2 %collective-permute-start = (bf16[128,512]{1,0:T(8,128)(2,1)S(1)}, bf16[128,512]{1,0:T(8,128)(2,1)S(1)}, u32[]{:S(2)}, u32[]{:S(2)}) collective-permute-start(bf16[128,512]{1,0:T(8,128)(2,1)S(1)} %get-tuple-element.42.own), channel_id=1, source_target_pairs={{0,1},{1,2},{2,3},{3,4},{4,5},{5,6},{6,7},{7,8},{8,9},{9,10},{10,1... | collective-permute-start | bytes 393224 | tf_op jit(solution)/shard_map/ppermute | solution.py:205
  4.6 10.6 %collective-permute-start.1 = (bf16[128,512]{1,0:T(8,128)(2,1)S(1)}, bf16[128,512]{1,0:T(8,128)(2,1)S(1)}, u32[]{:S(2)}, u32[]{:S(2)}) collective-permute-start(bf16[128,512]{1,0:T(8,128)(2,1)S(1)} %get-tuple-element.42.own), channel_id=1, source_target_pairs={{0,31},{1,0},{2,1},{3,2},{4,3},{5,4},{6,5},{7,6},{8,7},{9,8},{10,9... | collective-permute-start | bytes 393224 | tf_op jit(solution)/shard_map/ppermute | solution.py:205
  10.8 4.4 %collective-permute-start.2 = (bf16[128,512]{1,0:T(8,128)(2,1)S(1)}, bf16[128,512]{1,0:T(8,128)(2,1)S(1)}, u32[]{:S(2)}, u32[]{:S(2)}) collective-permute-start(bf16[128,512]{1,0:T(8,128)(2,1)S(1)} %get-tuple-element.42.own), channel_id=1, source_target_pairs={{0,32},{32,0},{64,96},{96,64},{128,160},{160,128},{192,224},{224,1... | collective-permute-start | bytes 393224 | tf_op jit(solution)/shard_map/ppermute | solution.py:212
  11.8 4.7 %collective-permute-start.3 = (bf16[128,512]{1,0:T(8,128)(2,1)S(1)}, bf16[128,512]{1,0:T(8,128)(2,1)S(1)}, u32[]{:S(2)}, u32[]{:S(2)}) collective-permute-start(bf16[128,512]{1,0:T(8,128)(2,1)S(1)} %get-tuple-element.42.own), channel_id=1, source_target_pairs={{0,224},{32,64},{64,32},{96,128},{128,96},{160,192},{192,160},{224... | collective-permute-start | bytes 393224 | tf_op jit(solution)/shard_map/ppermute | solution.py:212
  16.5 4.0 %collective-permute-start.4 = (bf16[256,512]{1,0:T(8,128)(2,1)S(1)}, bf16[256,512]{1,0:T(8,128)(2,1)S(1)}, u32[]{:S(2)}, u32[]{:S(2)}) collective-permute-start(bf16[256,512]{1,0:T(8,128)(2,1)S(1)} %get-tuple-element.46.beside), channel_id=1, source_target_pairs={{0,32},{32,0},{64,96},{96,64},{128,160},{160,128},{192,224},{224,1... | collective-permute-start | bytes 786440 | tf_op jit(solution)/shard_map/ppermute | solution.py:212
  17.7 6.1 %collective-permute-start.5 = (bf16[256,512]{1,0:T(8,128)(2,1)S(1)}, bf16[256,512]{1,0:T(8,128)(2,1)S(1)}, u32[]{:S(2)}, u32[]{:S(2)}) collective-permute-start(bf16[256,512]{1,0:T(8,128)(2,1)S(1)} %get-tuple-element.46.beside), channel_id=1, source_target_pairs={{0,224},{32,64},{64,32},{96,128},{128,96},{160,192},{192,160},{224... | collective-permute-start | bytes 786440 | tf_op jit(solution)/shard_map/ppermute | solution.py:212
  26.3 5.7 %collective-permute-start.8 = (bf16[256,512]{1,0:T(8,128)(2,1)S(1)}, bf16[256,512]{1,0:T(8,128)(2,1)S(1)}, u32[]{:S(2)}, u32[]{:S(2)}) collective-permute-start(bf16[256,512]{1,0:T(8,128)(2,1)S(1)} %get-tuple-element.71), channel_id=1, source_target_pairs={{0,32},{32,0},{64,96},{96,64},{128,160},{160,128},{192,224},{224,1... | collective-permute-start | bytes 786440 | tf_op jit(solution)/shard_map/ppermute | solution.py:212
  27.4 6.1 %collective-permute-start.9 = (bf16[256,512]{1,0:T(8,128)(2,1)S(1)}, bf16[256,512]{1,0:T(8,128)(2,1)S(1)}, u32[]{:S(2)}, u32[]{:S(2)}) collective-permute-start(bf16[256,512]{1,0:T(8,128)(2,1)S(1)} %get-tuple-element.72), channel_id=1, source_target_pairs={{0,224},{32,64},{64,32},{96,128},{128,96},{160,192},{192,160},{224... | collective-permute-start | bytes 786440 | tf_op jit(solution)/shard_map/ppermute | solution.py:212
  27.4 13.4 %copy-start = (bf16[512,512]{1,0:T(8,128)(2,1)S(1)}, bf16[512,512]{1,0:T(8,128)(2,1)}, u32[]{:S(2)}) copy-start(bf16[512,512]{1,0:T(8,128)(2,1)} %w_send.1) | copy-start | bytes 1572868
  27.4 13.4 %copy-start.1 = (f32[1,1,128,512]{3,2,1,0:T(8,128)S(1)}, f32[1,1,128,512]{3,2,1,0:T(8,128)}, u32[]{:S(2)}) copy-start(f32[1,1,128,512]{3,2,1,0:T(8,128)} %param.15) | copy-start | bytes 786436
  28.7 38.8 %copy-start.2 = (f32[1,1,128,512]{3,2,1,0:T(8,128)S(1)}, f32[1,1,128,512]{3,2,1,0:T(8,128)}, u32[]{:S(2)}) copy-start(f32[1,1,128,512]{3,2,1,0:T(8,128)} %param.14) | copy-start | bytes 786436
  28.8 9.6 %collective-permute-start.6 = (bf16[128,512]{1,0:T(8,128)(2,1)S(1)}, bf16[128,512]{1,0:T(8,128)(2,1)S(1)}, u32[]{:S(2)}, u32[]{:S(2)}) collective-permute-start(bf16[128,512]{1,0:T(8,128)(2,1)S(1)} %get-tuple-element.69), channel_id=1, source_target_pairs={{0,32},{32,0},{64,96},{96,64},{128,160},{160,128},{192,224},{224,1... | collective-permute-start | bytes 393224 | tf_op jit(solution)/shard_map/ppermute | solution.py:212
  31.9 6.5 %collective-permute-start.7 = (bf16[128,512]{1,0:T(8,128)(2,1)S(1)}, bf16[128,512]{1,0:T(8,128)(2,1)S(1)}, u32[]{:S(2)}, u32[]{:S(2)}) collective-permute-start(bf16[128,512]{1,0:T(8,128)(2,1)S(1)} %get-tuple-element.70), channel_id=1, source_target_pairs={{0,224},{32,64},{64,32},{96,128},{128,96},{160,192},{192,160},{224... | collective-permute-start | bytes 393224 | tf_op jit(solution)/shard_map/ppermute | solution.py:212
  33.5 7.2 %collective-permute-start.10 = (bf16[128,512]{1,0:T(8,128)(2,1)S(1)}, bf16[128,512]{1,0:T(8,128)(2,1)S(1)}, u32[]{:S(2)}, u32[]{:S(2)}) collective-permute-start(bf16[128,512]{1,0:T(8,128)(2,1)S(1)} %get-tuple-element.73), channel_id=1, source_target_pairs={{0,1},{1,2},{2,3},{3,4},{4,5},{5,6},{6,7},{7,8},{8,9},{9,10},{10,1... | collective-permute-start | bytes 393224 | tf_op jit(solution)/shard_map/ppermute | solution.py:205
  33.6 7.1 %collective-permute-start.11 = (bf16[128,512]{1,0:T(8,128)(2,1)S(1)}, bf16[128,512]{1,0:T(8,128)(2,1)S(1)}, u32[]{:S(2)}, u32[]{:S(2)}) collective-permute-start(bf16[128,512]{1,0:T(8,128)(2,1)S(1)} %get-tuple-element.74), channel_id=1, source_target_pairs={{0,31},{1,0},{2,1},{3,2},{4,3},{5,4},{6,5},{7,6},{8,7},{9,8},{10,9... | collective-permute-start | bytes 393224 | tf_op jit(solution)/shard_map/ppermute | solution.py:205

commit v4 on v3

--- a/solution.py
+++ b/solution.py
@@ -23,7 +23,7 @@
     return sig * (1.0 + value * (1.0 - sig))
 
 
-def call(kernel, name, out_shape, args, scratch=(), hbm=None):
+def call(kernel, name, out_shape, args, scratch=(), hbm=None, cost=None):
     here = pl.BlockSpec(memory_space=pltpu.VMEM)
     there = pl.BlockSpec(memory_space=pltpu.HBM)
     first = len(args) if hbm is None else hbm
@@ -35,6 +35,7 @@
         out_specs=jax.tree.map(lambda _: here, out_shape),
         scratch_shapes=scratch,
         compiler_params=pltpu.CompilerParams(vmem_limit_bytes=VMEM_LIMIT),
+        cost_estimate=cost,
         name=name,
     )(*args[:first], *away)
 
@@ -51,9 +52,13 @@
 
 
 def slot_blocks():
-    near = 6 - 6 * lax.rem(lax.axis_index("lat"), 2)
-    far = 6 - near
-    return (near, near + 2, far, far + 2, near + 1, far + 1, 3, 5, 4)
+    near = 1 - 2 * lax.rem(lax.axis_index("lat"), 2)
+    inner = 1 - 2 * lax.rem(lax.axis_index("lon"), 2)
+    places = (
+        (-near, -inner), (-near, inner), (near, -inner), (near, inner), (near, 0), (-near, 0),
+        (0, -inner), (0, inner), (0, 0),
+    )
+    return [(lat + 1) * 3 + lon + 1 for lat, lon in places]
 
 
 def send_kernel(senders, receivers, obs_hbm, d_hbm, w_hbm, own, send_row, recv_row, obs, d, w, sems):
@@ -92,24 +97,24 @@
         copy.wait()
 
 
-def stack_kernel(west, east, near, far, after, beside, across):
-    beside[0:128, :] = west[...]
-    beside[128:256, :] = east[...]
-    across[0:128, :] = near[...]
-    across[128:256, :] = far[...]
+def stack_kernel(outer, inner, after, beside):
+    beside[0:128, :] = outer[...]
+    beside[128:256, :] = inner[...]
 
 
 def base_kernel(
-    d, own, across, beside, pick, act, a_node, w_recv, w_self, w_edge, w_msg, w_out,
+    d, own, far, near, beside, pick, act, a_node, w_recv, w_self, w_edge, w_msg, w_out,
     base, slope, node_slope, self_pre, fold, gram, d_back, table,
 ):
     d_bf = d[...].astype(BF)
-    table[0:128, :] = own[...]
-    table[128:256, :] = dot(d_bf, w_recv[...]).astype(BF)
+    table[0:128, :] = near[...]
+    table[128:256, :] = far[...]
+    table[256:384, :] = own[...]
+    table[384:512, :] = dot(d_bf, w_recv[...]).astype(BF)
     base[...] = (
-        dot(pick[:, 512:768], across[...])
+        dot(pick[:, 512:768], table[:256, :])
         + dot(pick[:, 768:1024], beside[...])
-        + dot(pick[:, 1024:1280], table[...])
+        + dot(pick[:, 1024:1280], table[256:, :])
     )
     slope[...] = silu_slope(act[...].astype(F32))
     node_slope[...] = silu_slope(a_node[...].astype(F32))
@@ -126,11 +131,11 @@
 
 
 def main_kernel(
-    from_near, from_far, base, slope, pick, pick_t, node_slope, self_pre, fold, gram, d_back, obs,
-    corner_near, corner_far, edge_grad, node_grad, node_hidden,
+    from_far, from_near, base, slope, pick, pick_t, node_slope, self_pre, fold, gram, d_back, obs,
+    corner_far, corner_near, edge_grad, node_grad, node_hidden,
 ):
     gathered = (
-        base[...] + dot(pick[:, 0:256], from_near[...]) + dot(pick[:, 256:512], from_far[...])
+        base[...] + dot(pick[:, 0:256], from_far[...]) + dot(pick[:, 256:512], from_near[...])
     )
     hidden = (slope[...] * gathered).astype(BF)
     hidden_sum = dot(pick_t[1152:, :], hidden).astype(BF)
@@ -143,13 +148,13 @@
     edge_back = dot_back(grad, fold[...]).astype(BF)
     e_grad = (dot(pick[:, 1152:], edge_back) * slope[...]).astype(BF)
     edge_grad[...] = e_grad
-    corner_near[...] = dot(pick_t[0:256, :], e_grad).astype(BF)
-    corner_far[...] = dot(pick_t[256:512, :], e_grad).astype(BF)
+    corner_far[...] = dot(pick_t[0:256, :], e_grad).astype(BF)
+    corner_near[...] = dot(pick_t[256:512, :], e_grad).astype(BF)
 
 
 def rest_kernel(
     edge_grad, pick_t, node_grad, node_hidden, obs, d, w_recv, w_self, w_out,
-    middle_near, middle_far, mid, partial,
+    middle_far, middle_near, mid, partial,
 ):
     sums = dot(pick_t[512:, :], edge_grad[...])
     middle_near[...] = sums[:128, :].astype(BF)
@@ -162,19 +167,18 @@
     partial[...] = search + observed + back
 
 
-def merge_kernel(mid, from_near, from_far, to_west, to_east):
-    west, east = slice(0, 128), slice(128, 256)
-    for side, out in ((west, to_west), (east, to_east)):
+def merge_kernel(mid, from_far, from_near, to_outer, to_inner):
+    for rows, out in ((slice(0, 128), to_outer), (slice(128, 256), to_inner)):
         out[...] = (
-            mid[side, :] + from_near[side, :].astype(F32) + from_far[side, :].astype(F32)
+            mid[rows, :] + from_near[rows, :].astype(F32) + from_far[rows, :].astype(F32)
         ).astype(BF)
 
 
 def product_kernel(
-    mid, from_near, from_far, from_w, from_e, partial, w_send, d, r, product, sums
+    mid, from_near, from_far, from_outer, from_inner, partial, w_send, d, r, product, sums
 ):
     total = mid[256:384, :]
-    for part in (from_near, from_far, from_w, from_e):
+    for part in (from_near, from_far, from_inner, from_outer):
         total = total + part[...].astype(F32)
     prod = partial[...] + dot_back(total.astype(BF), w_send[...])
     product[...] = prod
@@ -200,16 +204,12 @@
     new_d[...] = left + beta * search
 
 
-def shifted(value, axis, step):
+def swapped(value, axis, across):
     count = lax.axis_size(axis)
-    return lax.ppermute(value, axis, [(i, (i + step) % count) for i in range(count)])
-
-
-def swapped(value, far):
-    count = lax.axis_size("lat")
-    step = -1 if far else 1
-    pairs = [(i, (i + (step if i % 2 == 0 else -step)) % count) for i in range(count)]
-    return lax.ppermute(value, "lat", pairs)
+    first = 1 if across else 0
+    last = count - 1 if axis == "lat" else count
+    pairs = [(i, (i + 1) % count) for i in range(first, last, 2)]
+    return lax.ppermute(value, axis, pairs + [(b, a) for a, b in pairs])
 
 
 def sums_everywhere(value):
@@ -257,10 +257,10 @@
         hbm=0,
         scratch=(pltpu.VMEM((width, width), BF), pltpu.SemaphoreType.DMA((5,))),
     )
-    near = swapped(own, False)
-    far = swapped(own, True)
-    west = shifted(own, "lon", 1)
-    east = shifted(own, "lon", -1)
+    outer = swapped(own, "lon", True)
+    inner = swapped(own, "lon", False)
+    far = swapped(own, "lat", True)
+    near = swapped(own, "lat", False)
     pick, pick_t, act, node_act, w_recv, w_self, w_edge, w_msg, w_out = call(
         prepare_kernel,
         "prepare",
@@ -279,42 +279,44 @@
         scratch=(pltpu.SemaphoreType.DMA((7,)),),
     )
     pair = shape(2 * nodes, width, BF)
-    beside, across = call(stack_kernel, "stack", (pair, pair), (west, east, near, far, node_act))
-    from_near = swapped(beside, False)
-    from_far = swapped(beside, True)
+    beside = call(stack_kernel, "stack", pair, (outer, inner, node_act))
+    from_far = swapped(beside, "lat", True)
+    from_near = swapped(beside, "lat", False)
     base, slope, node_slope, self_pre, fold, gram, d_back = call(
         base_kernel,
         "base",
         (shape(edges, width, F32),) * 2 + (field, field, weight, weight, field),
-        (d, own, across, beside, pick, act, node_act, w_recv, w_self, w_edge, w_msg, w_out),
-        scratch=(pltpu.VMEM((2 * nodes, width), BF),),
-    )
-    corner_near, corner_far, edge_grad, node_grad, node_hidden = call(
+        (d, own, far, near, beside, pick, act, node_act, w_recv, w_self, w_edge, w_msg, w_out),
+        scratch=(pltpu.VMEM((4 * nodes, width), BF),),
+        cost=pl.CostEstimate(flops=5 * 10**9, bytes_accessed=5 * 10**7, transcendentals=0),
+    )
+    corner_far, corner_near, edge_grad, node_grad, node_hidden = call(
         main_kernel,
         "main",
         (pair, pair, shape(edges, width, BF), block, block),
         (
-            from_near, from_far, base, slope, pick, pick_t, node_slope, self_pre, fold, gram, d_back, obs,
+            from_far, from_near, base, slope, pick, pick_t, node_slope, self_pre, fold, gram, d_back, obs,
         ),
     )
-    from_near = swapped(corner_near, False)
-    from_far = swapped(corner_far, True)
-    middle_near, middle_far, mid, partial = call(
+    from_far = swapped(corner_far, "lat", True)
+    from_near = swapped(corner_near, "lat", False)
+    middle_far, middle_near, mid, partial = call(
         rest_kernel,
         "rest",
         (block, block, shape(3 * nodes, width, F32), field),
         (edge_grad, pick_t, node_grad, node_hidden, obs, d, w_recv, w_self, w_out),
-    )
-    to_west, to_east = call(merge_kernel, "merge", (block, block), (mid, from_near, from_far))
-    from_e = shifted(to_west, "lon", -1)
-    from_w = shifted(to_east, "lon", 1)
-    from_near = swapped(middle_near, False)
-    from_far = swapped(middle_far, True)
+        cost=pl.CostEstimate(flops=5 * 10**9, bytes_accessed=5 * 10**7, transcendentals=0),
+    )
+    to_outer, to_inner = call(merge_kernel, "merge", (block, block), (mid, from_far, from_near))
+    from_outer = swapped(to_outer, "lon", True)
+    from_inner = swapped(to_inner, "lon", False)
+    from_far = swapped(middle_far, "lat", True)
+    from_near = swapped(middle_near, "lat", False)
     product, sums = call(
         product_kernel,
         "product",
         (field, shape(16, 128, F32)),
-        (mid, from_near, from_far, from_w, from_e, partial, w_send, d, r),
+        (mid, from_near, from_far, from_outer, from_inner, partial, w_send, d, r),
     )
     sums = sums_everywhere(sums)
     outs = call(final_kernel, "final", (field,) * 3, (sums, x, r, d, product))

time: 68.8 us -> 67.5 us (0.981)
  starting transfers between devices: 21.5 us -> 26 us
  blocking collectives: 26.2 us -> 22.3 us
  waiting for transfers between devices: 8.37 us -> 6.1 us
    ppermute x12, starting transfers between devices: 21.5 us -> 26 us  [swapped(): return lax.ppermute(value, axis, pairs + [(b, a) for a, b in pairs])]
    all_to_all x2, blocking collectives: 26.2 us -> 22.3 us  [sums_everywhere(): lax.all_to_all(value, ('lat', 'lon'), 0, 0, tiled=True, axis_index_groups...]
    ppermute x12, waiting for transfers between devices: 8.37 us -> 6.1 us  [swapped(): return lax.ppermute(value, axis, pairs + [(b, a) for a, b in pairs])]
  transfers between devices with their start and end apart: 12 -> 12, of which waited for: 4 -> 3; matrix products, arithmetic and copies ran while one was open for 0% -> 0% of each run, Pallas kernels for 9% -> 10%
where the time goes in v4:
time: 67.5 us; the launch traced here: 67.2 us
  starting transfers between devices  26 us (39%)
  blocking collectives  22.3 us (33%)
  Pallas kernels  11.9 us (18%)
  waiting for transfers between devices  6.1 us (9%)
  between operations  0.83 us (1%)
    ppermute x12, starting transfers between devices, swapped(): return lax.ppermute(value, axis, pairs + [(b, a) for a, b in pairs])  26 us
    all_to_all x2, blocking collectives, sums_everywhere(): lax.all_to_all(value, ('lat', 'lon'), 0, 0, tiled=True, axis_index_groups...  22.3 us
    pallas_call x9, Pallas kernels, call(): pl.pallas_call(kernel, out_shape=out_shape, in_specs=[here] * first + [th...  11.9 us
    ppermute x12, waiting for transfers between devices, swapped(): return lax.ppermute(value, axis, pairs + [(b, a) for a, b in pairs])  6.1 us
  transfers between devices with their start and end apart: 12, of which 3 were waited for; matrix products, arithmetic and copies ran while one was open for 0% of the time, Pallas kernels for 10%

profile of v4, /device:TPU:1, one launch (start us, length us, event | category | flops | bytes accessed | tf_op | source)
XLA Modules:
  0.0 67.2 jit_solution(8491296602749261694)
XLA Ops:
  0.6 1.4 %send_term.1 = (bf16[128,512]{1,0:T(8,128)(2,1)S(1)}, s32[1,1024]{1,0:T(1,128)S(1)}, s32[1,1024]{1,0:T(1,128)S(1)}, f32[1,128]{1,0:T(1,128)S(1)}, f32[128,512]{1,0:T(8,128)S(1)}) custom-call(s32[1,1024]{1,0:T(1,128)} %bitcast.23, s32[1,1024]{1,0:T(1,128)} %bitcast.24, f32[1,128]{1,0:T(1,128)} %bitcast.25, f32[128,512]{1,0:T(8,128)} %bitcast.21, ...), custom_call_target="tpu_custom_call" | custom-call | tf_op jit(solution)/shard_map/send_term/pallas_call | solution.py:31
  2.0 8.7 %collective-permute-start = (bf16[128,512]{1,0:T(8,128)(2,1)S(1)}, bf16[128,512]{1,0:T(8,128)(2,1)S(1)}, u32[]{:S(2)}, u32[]{:S(2)}) collective-permute-start(bf16[128,512]{1,0:T(8,128)(2,1)S(1)} %get-tuple-element.40.own), channel_id=1, source_target_pairs={{1,2},{3,4},{5,6},{7,8},{9,10},{11,12},{13,14},{15,16},{17,18},{19... | collective-permute-start | bytes 393224 | tf_op jit(solution)/shard_map/ppermute | solution.py:212
  10.7 0.0 collective-permute-start.1
  10.7 4.0 %collective-permute-start.4 = (bf16[128,512]{1,0:T(8,128)(2,1)S(1)}, bf16[128,512]{1,0:T(8,128)(2,1)S(1)}, u32[]{:S(2)}, u32[]{:S(2)}) collective-permute-start(bf16[128,512]{1,0:T(8,128)(2,1)S(1)} %get-tuple-element.40.own), channel_id=1, source_target_pairs={{32,64},{96,128},{160,192},{64,32},{128,96},{192,160},{33,65},{97,... | collective-permute-start | bytes 393224 | tf_op jit(solution)/shard_map/ppermute | solution.py:212
  14.8 0.1 collective-permute-start.5
  14.9 2.4 %prepare.1 = (bf16[1024,1280]{1,0:T(8,128)(2,1)S(1)}, bf16[1280,1024]{1,0:T(8,128)(2,1)S(1)}, bf16[1024,512]{1,0:T(8,128)(2,1)S(1)}, bf16[128,512]{1,0:T(8,128)(...) custom-call(s32[1,1024]{1,0:T(1,128)S(1)} %get-tuple-element.41.send, ...), custom_call_target="tpu_custom_call" | custom-call | tf_op jit(solution)/shard_map/prepare/pallas_call | solution.py:31
  17.3 0.0 collective-permute-done.outer
  17.3 0.0 collective-permute-done.1.inner
  17.4 3.6 %collective-permute-start.2 = (bf16[256,512]{1,0:T(8,128)(2,1)S(1)}, bf16[256,512]{1,0:T(8,128)(2,1)S(1)}, u32[]{:S(2)}, u32[]{:S(2)}) collective-permute-start(bf16[256,512]{1,0:T(8,128)(2,1)S(1)} %stack.1.beside), channel_id=1, source_target_pairs={{32,64},{96,128},{160,192},{64,32},{128,96},{192,160},{33,65},{97,... | collective-permute-start | bytes 786440 | tf_op jit(solution)/shard_map/ppermute | solution.py:212
  21.0 0.1 collective-permute-start.3
  21.1 0.0 collective-permute-done.4.far
  21.1 0.0 collective-permute-done.5.near
  21.1 2.6 %base.1 = (f32[1024,512]{1,0:T(8,128)S(1)}, f32[1024,512]{1,0:T(8,128)S(1)}, f32[128,512]{1,0:T(8,128)S(1)}, f32[128,512]{1,0:T(8,128)S(1)}, bf16[512,512]{1,0:T...) custom-call(f32[128,512]{1,0:T(8,128)S(1)} %get-tuple-element.44.d, ...), custom_call_target="tpu_custom_call" | custom-call | flops 5000000000 | bytes 50000000 | tf_op jit(solution)/shard_map/base/pallas_call | solution.py:31
  23.7 1.4 %collective-permute-done.2.from_far = bf16[256,512]{1,0:T(8,128)(2,1)S(1)} collective-permute-done((bf16[256,512]{1,0:T(8,128)(2,1)S(1)}, bf16[256,512]{1,0:T(8,128)(2,1)S(1)}, u32[]{:S(2)}, u32[]{:S(2)}) %collective-permute-start.2) | collective-permute-done | bytes 262176 | tf_op jit(solution)/shard_map/ppermute | solution.py:212
  25.1 0.0 collective-permute-done.3.from_near
  25.1 2.4 %main.1 = (bf16[256,512]{1,0:T(8,128)(2,1)S(1)}, bf16[256,512]{1,0:T(8,128)(2,1)S(1)}, bf16[1024,512]{1,0:T(8,128)(2,1)S(1)}, bf16[128,512]{1,0:T(8,128)(2,1)S(1)}, bf16[128,512]{1,0:T(8,128)(2,1)S(1)}) custom-call(bf16[256,512]{1,0:T(8,128)(2,1)S(1)} %collective-permute-done.2.from_far, bf16[256,512]{1,0:T(8,128)(2,1)S(1)} %collective-permute-done.3.from_near, ...), custom_call_target="tpu_custom_call" | custom-call | tf_op jit(solution)/shard_map/main/pallas_call | solution.py:31
  27.5 3.6 %collective-permute-start.8 = (bf16[256,512]{1,0:T(8,128)(2,1)S(1)}, bf16[256,512]{1,0:T(8,128)(2,1)S(1)}, u32[]{:S(2)}, u32[]{:S(2)}) collective-permute-start(bf16[256,512]{1,0:T(8,128)(2,1)S(1)} %get-tuple-element.67), channel_id=1, source_target_pairs={{32,64},{96,128},{160,192},{64,32},{128,96},{192,160},{33,65},{97,... | collective-permute-start | bytes 786440 | tf_op jit(solution)/shard_map/ppermute | solution.py:212
  31.1 0.1 collective-permute-start.9
  31.2 0.0 copy-start
  31.2 0.0 copy-start.1
  31.2 1.4 %rest.1 = (bf16[128,512]{1,0:T(8,128)(2,1)S(1)}, bf16[128,512]{1,0:T(8,128)(2,1)S(1)}, f32[384,512]{1,0:T(8,128)S(1)}, f32[128,512]{1,0:T(8,128)S(1)}) custom-call(bf16[1024,512]{1,0:T(8,128)(2,1)S(1)} %get-tuple-element.61.edge_grad, bf16[1280,1024]{1,0:T(8,128)(2,1)S(1)} %get-tuple-element.54.pick_t, bf16[128,512]{1,0:T(8,128)(2,1)S(1)} %get-tuple-element.62.node_grad, ...), custom_call_target="tpu_custom_call" | custom-call | flops 5000000000 | bytes 50000000 | tf_op jit(solution)/shard_map/rest/pallas_call | solution.py:31
  32.6 0.0 copy-start.2
  32.6 0.6 collective-permute-start.6
  33.2 2.8 %collective-permute-start.7 = (bf16[128,512]{1,0:T(8,128)(2,1)S(1)}, bf16[128,512]{1,0:T(8,128)(2,1)S(1)}, u32[]{:S(2)}, u32[]{:S(2)}) collective-permute-start(bf16[128,512]{1,0:T(8,128)(2,1)S(1)} %get-tuple-element.66), channel_id=1, source_target_pairs={{32,64},{96,128},{160,192},{64,32},{128,96},{192,160},{33,65},{97,... | collective-permute-start | bytes 393224 | tf_op jit(solution)/shard_map/ppermute | solution.py:212
  36.0 0.0 collective-permute-done.8.from_far
  36.0 0.0 collective-permute-done.9.from_near
  36.0 0.1 merge.1
  36.1 2.5 %collective-permute-start.10 = (bf16[128,512]{1,0:T(8,128)(2,1)S(1)}, bf16[128,512]{1,0:T(8,128)(2,1)S(1)}, u32[]{:S(2)}, u32[]{:S(2)}) collective-permute-start(bf16[128,512]{1,0:T(8,128)(2,1)S(1)} %get-tuple-element.69), channel_id=1, source_target_pairs={{1,2},{3,4},{5,6},{7,8},{9,10},{11,12},{13,14},{15,16},{17,18},{19... | collective-permute-start | bytes 393224 | tf_op jit(solution)/shard_map/ppermute | solution.py:212
  38.6 0.0 collective-permute-start.11
  38.6 0.0 collective-permute-done.6.from_near
  38.6 1.1 %collective-permute-done.7.from_far = bf16[128,512]{1,0:T(8,128)(2,1)S(1)} collective-permute-done((bf16[128,512]{1,0:T(8,128)(2,1)S(1)}, bf16[128,512]{1,0:T(8,128)(2,1)S(1)}, u32[]{:S(2)}, u32[]{:S(2)}) %collective-permute-start.7) | collective-permute-done | bytes 131104 | tf_op jit(solution)/shard_map/ppermute | solution.py:212
  39.7 3.6 %collective-permute-done.10.from_outer = bf16[128,512]{1,0:T(8,128)(2,1)S(1)} collective-permute-done((bf16[128,512]{1,0:T(8,128)(2,1)S(1)}, bf16[128,512]{1,0:T(8,128)(2,1)S(1)}, u32[]{:S(2)}, u32[]{:S(2)}) %collective-permute-start.10) | collective-permute-done | bytes 131104 | tf_op jit(solution)/shard_map/ppermute | solution.py:212
  43.3 0.0 collective-permute-done.11.from_inner
  43.3 0.0 copy-done
  43.4 0.0 copy-done.1
  43.4 0.5 product.1
  43.8 8.6 %all_to_all.17 = f32[16,1,128]{2,1,0:T(1,128)S(1)} all-to-all(f32[16,1,128]{2,1,0:T(1,128)S(1)} %bitcast.19), channel_id=1, replica_groups={{0,1,2,3,4,5,6,7,32,33,34,35,36,37,38,39},{8,9,10,11,12,13,14,15,40,41,..., dimensions={0} | all-to-all | bytes 16384 | tf_op jit(solution)/shard_map/all_to_all | solution.py:228
  52.4 13.8 %all_to_all.18 = f32[16,1,128]{2,1,0:T(1,128)S(1)} all-to-all(f32[16,1,128]{2,1,0:T(1,128)S(1)} %broadcast_in_dim.2), channel_id=1, replica_groups={{0,8,16,24,64,72,80,88,128,136,144,152,192,200,208,216},{1,9,17,25,65,7..., dimensions={0} | all-to-all | bytes 16384 | tf_op jit(solution)/shard_map/all_to_all | solution.py:231
  66.2 0.0 copy-done.2
  66.2 1.0 %final.1 = (f32[128,512]{1,0:T(8,128)}, f32[128,512]{1,0:T(8,128)}, f32[128,512]{1,0:T(8,128)}) custom-call(f32[16,128]{1,0:T(8,128)S(1)} %bitcast.18, f32[128,512]{1,0:T(8,128)S(1)} %bitcast.17, f32[128,512]{1,0:T(8,128)S(1)} %bitcast.16, f32[128,512]{1,0:T(8,128)S(1)} %get-tuple-element.44.d, f32[128,512]{1,0:T(8,128)S(1)} %get-tuple-element.73.product), custom_call_target="tpu_custom_call" | custom-call | tf_op jit(solution)/shard_map/final/pallas_call | solution.py:31
  (3 shorter events, 0.1 us)
Async XLA Ops:
  2.0 15.3 %collective-permute-start = (bf16[128,512]{1,0:T(8,128)(2,1)S(1)}, bf16[128,512]{1,0:T(8,128)(2,1)S(1)}, u32[]{:S(2)}, u32[]{:S(2)}) collective-permute-start(bf16[128,512]{1,0:T(8,128)(2,1)S(1)} %get-tuple-element.40.own), channel_id=1, source_target_pairs={{1,2},{3,4},{5,6},{7,8},{9,10},{11,12},{13,14},{15,16},{17,18},{19... | collective-permute-start | bytes 393224 | tf_op jit(solution)/shard_map/ppermute | solution.py:212
  10.7 6.6 %collective-permute-start.1 = (bf16[128,512]{1,0:T(8,128)(2,1)S(1)}, bf16[128,512]{1,0:T(8,128)(2,1)S(1)}, u32[]{:S(2)}, u32[]{:S(2)}) collective-permute-start(bf16[128,512]{1,0:T(8,128)(2,1)S(1)} %get-tuple-element.40.own), channel_id=1, source_target_pairs={{0,1},{2,3},{4,5},{6,7},{8,9},{10,11},{12,13},{14,15},{16,17},{18,... | collective-permute-start | bytes 393224 | tf_op jit(solution)/shard_map/ppermute | solution.py:212
  10.7 10.3 %collective-permute-start.4 = (bf16[128,512]{1,0:T(8,128)(2,1)S(1)}, bf16[128,512]{1,0:T(8,128)(2,1)S(1)}, u32[]{:S(2)}, u32[]{:S(2)}) collective-permute-start(bf16[128,512]{1,0:T(8,128)(2,1)S(1)} %get-tuple-element.40.own), channel_id=1, source_target_pairs={{32,64},{96,128},{160,192},{64,32},{128,96},{192,160},{33,65},{97,... | collective-permute-start | bytes 393224 | tf_op jit(solution)/shard_map/ppermute | solution.py:212
  14.8 6.3 %collective-permute-start.5 = (bf16[128,512]{1,0:T(8,128)(2,1)S(1)}, bf16[128,512]{1,0:T(8,128)(2,1)S(1)}, u32[]{:S(2)}, u32[]{:S(2)}) collective-permute-start(bf16[128,512]{1,0:T(8,128)(2,1)S(1)} %get-tuple-element.40.own), channel_id=1, source_target_pairs={{0,32},{64,96},{128,160},{192,224},{32,0},{96,64},{160,128},{224,1... | collective-permute-start | bytes 393224 | tf_op jit(solution)/shard_map/ppermute | solution.py:212
  17.4 7.7 %collective-permute-start.2 = (bf16[256,512]{1,0:T(8,128)(2,1)S(1)}, bf16[256,512]{1,0:T(8,128)(2,1)S(1)}, u32[]{:S(2)}, u32[]{:S(2)}) collective-permute-start(bf16[256,512]{1,0:T(8,128)(2,1)S(1)} %stack.1.beside), channel_id=1, source_target_pairs={{32,64},{96,128},{160,192},{64,32},{128,96},{192,160},{33,65},{97,... | collective-permute-start | bytes 786440 | tf_op jit(solution)/shard_map/ppermute | solution.py:212
  21.0 4.1 %collective-permute-start.3 = (bf16[256,512]{1,0:T(8,128)(2,1)S(1)}, bf16[256,512]{1,0:T(8,128)(2,1)S(1)}, u32[]{:S(2)}, u32[]{:S(2)}) collective-permute-start(bf16[256,512]{1,0:T(8,128)(2,1)S(1)} %stack.1.beside), channel_id=1, source_target_pairs={{0,32},{64,96},{128,160},{192,224},{32,0},{96,64},{160,128},{224,1... | collective-permute-start | bytes 786440 | tf_op jit(solution)/shard_map/ppermute | solution.py:212
  27.5 8.5 %collective-permute-start.8 = (bf16[256,512]{1,0:T(8,128)(2,1)S(1)}, bf16[256,512]{1,0:T(8,128)(2,1)S(1)}, u32[]{:S(2)}, u32[]{:S(2)}) collective-permute-start(bf16[256,512]{1,0:T(8,128)(2,1)S(1)} %get-tuple-element.67), channel_id=1, source_target_pairs={{32,64},{96,128},{160,192},{64,32},{128,96},{192,160},{33,65},{97,... | collective-permute-start | bytes 786440 | tf_op jit(solution)/shard_map/ppermute | solution.py:212
  31.1 4.9 %collective-permute-start.9 = (bf16[256,512]{1,0:T(8,128)(2,1)S(1)}, bf16[256,512]{1,0:T(8,128)(2,1)S(1)}, u32[]{:S(2)}, u32[]{:S(2)}) collective-permute-start(bf16[256,512]{1,0:T(8,128)(2,1)S(1)} %get-tuple-element.68), channel_id=1, source_target_pairs={{0,32},{64,96},{128,160},{192,224},{32,0},{96,64},{160,128},{224,1... | collective-permute-start | bytes 786440 | tf_op jit(solution)/shard_map/ppermute | solution.py:212
  31.2 12.2 %copy-start = (bf16[512,512]{1,0:T(8,128)(2,1)S(1)}, bf16[512,512]{1,0:T(8,128)(2,1)}, u32[]{:S(2)}) copy-start(bf16[512,512]{1,0:T(8,128)(2,1)} %w_send.1) | copy-start | bytes 1572868
  31.2 12.1 %copy-start.1 = (f32[1,1,128,512]{3,2,1,0:T(8,128)S(1)}, f32[1,1,128,512]{3,2,1,0:T(8,128)}, u32[]{:S(2)}) copy-start(f32[1,1,128,512]{3,2,1,0:T(8,128)} %param.15) | copy-start | bytes 786436
  32.6 33.6 %copy-start.2 = (f32[1,1,128,512]{3,2,1,0:T(8,128)S(1)}, f32[1,1,128,512]{3,2,1,0:T(8,128)}, u32[]{:S(2)}) copy-start(f32[1,1,128,512]{3,2,1,0:T(8,128)} %param.14) | copy-start | bytes 786436
  32.6 6.0 %collective-permute-start.6 = (bf16[128,512]{1,0:T(8,128)(2,1)S(1)}, bf16[128,512]{1,0:T(8,128)(2,1)S(1)}, u32[]{:S(2)}, u32[]{:S(2)}) collective-permute-start(bf16[128,512]{1,0:T(8,128)(2,1)S(1)} %get-tuple-element.65), channel_id=1, source_target_pairs={{0,32},{64,96},{128,160},{192,224},{32,0},{96,64},{160,128},{224,1... | collective-permute-start | bytes 393224 | tf_op jit(solution)/shard_map/ppermute | solution.py:212
  33.2 6.6 %collective-permute-start.7 = (bf16[128,512]{1,0:T(8,128)(2,1)S(1)}, bf16[128,512]{1,0:T(8,128)(2,1)S(1)}, u32[]{:S(2)}, u32[]{:S(2)}) collective-permute-start(bf16[128,512]{1,0:T(8,128)(2,1)S(1)} %get-tuple-element.66), channel_id=1, source_target_pairs={{32,64},{96,128},{160,192},{64,32},{128,96},{192,160},{33,65},{97,... | collective-permute-start | bytes 393224 | tf_op jit(solution)/shard_map/ppermute | solution.py:212
  36.1 7.2 %collective-permute-start.10 = (bf16[128,512]{1,0:T(8,128)(2,1)S(1)}, bf16[128,512]{1,0:T(8,128)(2,1)S(1)}, u32[]{:S(2)}, u32[]{:S(2)}) collective-permute-start(bf16[128,512]{1,0:T(8,128)(2,1)S(1)} %get-tuple-element.69), channel_id=1, source_target_pairs={{1,2},{3,4},{5,6},{7,8},{9,10},{11,12},{13,14},{15,16},{17,18},{19... | collective-permute-start | bytes 393224 | tf_op jit(solution)/shard_map/ppermute | solution.py:212
  38.6 4.7 %collective-permute-start.11 = (bf16[128,512]{1,0:T(8,128)(2,1)S(1)}, bf16[128,512]{1,0:T(8,128)(2,1)S(1)}, u32[]{:S(2)}, u32[]{:S(2)}) collective-permute-start(bf16[128,512]{1,0:T(8,128)(2,1)S(1)} %get-tuple-element.70), channel_id=1, source_target_pairs={{0,1},{2,3},{4,5},{6,7},{8,9},{10,11},{12,13},{14,15},{16,17},{18,... | collective-permute-start | bytes 393224 | tf_op jit(solution)/shard_map/ppermute | solution.py:212

commit v5 on v4

--- a/solution.py
+++ b/solution.py
@@ -1,3 +1,5 @@
+import functools
+
 import jax
 import jax.numpy as jnp
 from jax import lax
@@ -7,6 +9,8 @@
 
 BF = jnp.bfloat16
 F32 = jnp.float32
+LIGHT = 10**9
+HEAVY = 5 * 10**9
 VMEM_LIMIT = 12 * 1024 * 1024
 
 
@@ -40,6 +44,10 @@
     )(*args[:first], *away)
 
 
+def cost(flops):
+    return pl.CostEstimate(flops=flops, bytes_accessed=flops // 100, transcendentals=0)
+
+
 def shape(rows, cols, kind):
     return jax.ShapeDtypeStruct((rows, cols), kind)
 
@@ -69,12 +77,12 @@
 
 
 def prepare_kernel(
-    send_row, recv_row, act_hbm, a_node_hbm, w_recv_hbm, w_self_hbm, w_edge_hbm, w_msg_hbm, w_out_hbm,
-    pick, pick_t, act, a_node, w_recv, w_self, w_edge, w_msg, w_out, sems,
+    send_row, recv_row, d, act_hbm, a_node_hbm, w_recv_hbm, w_self_hbm, w_edge_hbm, w_msg_hbm, w_out_hbm,
+    pick, pick_t, act, a_node, recv_term, w_recv, w_self, w_edge, w_msg, w_out, sems,
 ):
     pairs = (
-        (act_hbm, act), (a_node_hbm, a_node), (w_recv_hbm, w_recv), (w_self_hbm, w_self),
-        (w_edge_hbm, w_edge), (w_msg_hbm, w_msg), (w_out_hbm, w_out),
+        (w_recv_hbm, w_recv), (w_self_hbm, w_self), (w_out_hbm, w_out), (w_edge_hbm, w_edge),
+        (w_msg_hbm, w_msg), (a_node_hbm, a_node), (act_hbm, act),
     )
     copies = start_all(pairs, sems)
     edges = act.shape[0]
@@ -95,33 +103,44 @@
     pick_t[k * nodes :, :] = jnp.where(recvs == rows, 1.0, 0.0).astype(BF)
     for copy in copies:
         copy.wait()
-
-
-def stack_kernel(outer, inner, after, beside):
-    beside[0:128, :] = outer[...]
-    beside[128:256, :] = inner[...]
+    d_bf = d[...].astype(BF)
+    recv_term[...] = dot(d_bf, w_recv[...]).astype(BF)
+
+
+def pass_kernel(block, after, out):
+    out[...] = block[...]
+
+
+def stack_kernel(outer, inner, outer_out, pair):
+    outer_out[...] = outer[...]
+    pair[0:128, :] = outer[...]
+    pair[128:256, :] = inner[...]
+
+
+def gathered(pick, first, parts, table):
+    row = 0
+    for part in parts:
+        table[row : row + part.shape[0], :] = part[...]
+        row += part.shape[0]
+    return dot(pick[:, first : first + row], table[...])
 
 
 def base_kernel(
-    d, own, far, near, beside, pick, act, a_node, w_recv, w_self, w_edge, w_msg, w_out,
-    base, slope, node_slope, self_pre, fold, gram, d_back, table,
+    far, near, outer, inner, own, recv_term, pick, act, a_node, d, w_self, w_edge, w_msg, w_out,
+    base, slope, node_slope, self_pre, d_back, fold, gram, table,
 ):
     d_bf = d[...].astype(BF)
-    table[0:128, :] = near[...]
-    table[128:256, :] = far[...]
-    table[256:384, :] = own[...]
-    table[384:512, :] = dot(d_bf, w_recv[...]).astype(BF)
-    base[...] = (
-        dot(pick[:, 512:768], table[:256, :])
-        + dot(pick[:, 768:1024], beside[...])
-        + dot(pick[:, 1024:1280], table[256:, :])
-    )
+    self_pre[...] = dot(d_bf, w_self[...])
+    d_back[...] = dot_back(d_bf, w_out[...])
+    fold[...] = dot(w_edge[...], w_msg[...]).astype(BF)
+    gram[...] = dot_back(w_out[...], w_out[...]).astype(BF)
     slope[...] = silu_slope(act[...].astype(F32))
     node_slope[...] = silu_slope(a_node[...].astype(F32))
-    self_pre[...] = dot(d_bf, w_self[...])
-    fold[...] = dot(w_edge[...], w_msg[...]).astype(BF)
-    gram[...] = dot_back(w_out[...], w_out[...]).astype(BF)
-    d_back[...] = dot_back(d_bf, w_out[...])
+    base[...] = gathered(pick, 512, (near, far, outer, inner, own, recv_term), table)
+
+
+def more_kernel(first, part, base, pick, more):
+    more[...] = base[...] + dot(pick[:, first : first + part.shape[0]], part[...])
 
 
 def lanes_of(row, width):
@@ -131,13 +150,11 @@
 
 
 def main_kernel(
-    from_far, from_near, base, slope, pick, pick_t, node_slope, self_pre, fold, gram, d_back, obs,
-    corner_far, corner_near, edge_grad, node_grad, node_hidden,
-):
-    gathered = (
-        base[...] + dot(pick[:, 0:256], from_far[...]) + dot(pick[:, 256:512], from_near[...])
-    )
-    hidden = (slope[...] * gathered).astype(BF)
+    far_outer, base, slope, pick, pick_t, node_slope, self_pre, fold, gram, d_back, obs,
+    corner_outer, corner_inner, all_near, edge_grad, node_grad, node_hidden,
+):
+    edge_input = base[...] + dot(pick[:, 0:128], far_outer[...])
+    hidden = (slope[...] * edge_input).astype(BF)
     hidden_sum = dot(pick_t[1152:, :], hidden).astype(BF)
     pre_node = self_pre[...] + dot(hidden_sum, fold[...])
     inner = (node_slope[...] * pre_node).astype(BF)
@@ -148,37 +165,41 @@
     edge_back = dot_back(grad, fold[...]).astype(BF)
     e_grad = (dot(pick[:, 1152:], edge_back) * slope[...]).astype(BF)
     edge_grad[...] = e_grad
-    corner_far[...] = dot(pick_t[0:256, :], e_grad).astype(BF)
-    corner_near[...] = dot(pick_t[256:512, :], e_grad).astype(BF)
+    sums = dot(pick_t[0:640, :], e_grad).astype(BF)
+    corner_outer[...] = sums[0:128, :]
+    corner_inner[...] = sums[128:256, :]
+    all_near[...] = sums[256:640, :]
 
 
 def rest_kernel(
     edge_grad, pick_t, node_grad, node_hidden, obs, d, w_recv, w_self, w_out,
-    middle_far, middle_near, mid, partial,
-):
-    sums = dot(pick_t[512:, :], edge_grad[...])
-    middle_near[...] = sums[:128, :].astype(BF)
-    middle_far[...] = sums[128:256, :].astype(BF)
-    mid[...] = sums[256:640, :]
+    middle_far, mid, partial,
+):
+    sums = dot(pick_t[640:, :], edge_grad[...])
+    middle_far[...] = sums[:128, :].astype(BF)
+    mid[...] = sums[128:512, :]
     search = d[...]
     changed = search + dot(node_hidden[...], w_out[...])
     observed = lanes_of(obs[...], search.shape[1]) * changed
-    back = dot_back(node_grad[...], w_self[...]) + dot_back(sums[640:, :].astype(BF), w_recv[...])
+    back = dot_back(node_grad[...], w_self[...]) + dot_back(sums[512:, :].astype(BF), w_recv[...])
     partial[...] = search + observed + back
 
 
-def merge_kernel(mid, from_far, from_near, to_outer, to_inner):
-    for rows, out in ((slice(0, 128), to_outer), (slice(128, 256), to_inner)):
-        out[...] = (
-            mid[rows, :] + from_near[rows, :].astype(F32) + from_far[rows, :].astype(F32)
-        ).astype(BF)
+def merge_kernel(first, mid, from_far, from_near, *refs):
+    rows = slice(first, first + 128)
+    total = mid[rows, :] + from_far[...].astype(F32) + from_near[rows, :].astype(F32)
+    refs[-1][...] = total.astype(BF)
+
+
+def center_kernel(mid, from_outer, center):
+    center[...] = mid[256:384, :] + from_outer[...].astype(F32)
 
 
 def product_kernel(
-    mid, from_near, from_far, from_outer, from_inner, partial, w_send, d, r, product, sums
-):
-    total = mid[256:384, :]
-    for part in (from_near, from_far, from_inner, from_outer):
+    center, from_near, from_far, from_inner, partial, w_send, d, r, product, sums
+):
+    total = center[...] + from_near[256:384, :].astype(F32)
+    for part in (from_far, from_inner):
         total = total + part[...].astype(F32)
     prod = partial[...] + dot_back(total.astype(BF), w_send[...])
     product[...] = prod
@@ -205,11 +226,21 @@
 
 
 def swapped(value, axis, across):
-    count = lax.axis_size(axis)
-    first = 1 if across else 0
-    last = count - 1 if axis == "lat" else count
-    pairs = [(i, (i + 1) % count) for i in range(first, last, 2)]
-    return lax.ppermute(value, axis, pairs + [(b, a) for a, b in pairs])
+    n_lat, n_lon = lax.axis_size("lat"), lax.axis_size("lon")
+
+    def partner(i, j):
+        if axis == "lon":
+            return i, (j - 1 if j % 2 == 0 else j + 1) % n_lon if across else j ^ 1
+        if not across:
+            return i ^ 1, j
+        return (i, j ^ 1) if i in (0, n_lat - 1) else (i - 1 if i % 2 == 0 else i + 1, j)
+
+    pairs = []
+    for i in range(n_lat):
+        for j in range(n_lon):
+            to_lat, to_lon = partner(i, j)
+            pairs.append((i * n_lon + j, to_lat * n_lon + to_lon))
+    return lax.ppermute(value, ("lat", "lon"), pairs)
 
 
 def sums_everywhere(value):
@@ -261,7 +292,7 @@
     inner = swapped(own, "lon", False)
     far = swapped(own, "lat", True)
     near = swapped(own, "lat", False)
-    pick, pick_t, act, node_act, w_recv, w_self, w_edge, w_msg, w_out = call(
+    pick, pick_t, act, node_act, recv_term, w_recv, w_self, w_edge, w_msg, w_out = call(
         prepare_kernel,
         "prepare",
         (
@@ -269,54 +300,79 @@
             shape(10 * nodes, edges, BF),
             shape(edges, width, BF),
             block,
+            block,
         )
         + (weight,) * 5,
         (
-            send_row, recv_row, a_edge.reshape(edges, width), a_node.reshape(nodes, width),
+            send_row, recv_row, d, a_edge.reshape(edges, width), a_node.reshape(nodes, width),
             w_recv, w_node_self, w_edge_out, w_node_msg, w_node_out,
         ),
-        hbm=2,
-        scratch=(pltpu.SemaphoreType.DMA((7,)),),
+        hbm=3,
+        scratch=(
+            pltpu.SemaphoreType.DMA((7,)),
+        ),
     )
     pair = shape(2 * nodes, width, BF)
-    beside = call(stack_kernel, "stack", pair, (outer, inner, node_act))
-    from_far = swapped(beside, "lat", True)
-    from_near = swapped(beside, "lat", False)
-    base, slope, node_slope, self_pre, fold, gram, d_back = call(
+    inner = call(pass_kernel, "pass_inner", block, (inner, recv_term))
+    far_inner = swapped(inner, "lat", True)
+    outer, beside = call(stack_kernel, "stack", (block, pair), (outer, inner))
+    far_outer = swapped(outer, "lat", True)
+    near_pair = swapped(beside, "lat", False)
+    base, slope, node_slope, self_pre, d_back, fold, gram = call(
         base_kernel,
         "base",
-        (shape(edges, width, F32),) * 2 + (field, field, weight, weight, field),
-        (d, own, far, near, beside, pick, act, node_act, w_recv, w_self, w_edge, w_msg, w_out),
-        scratch=(pltpu.VMEM((4 * nodes, width), BF),),
-        cost=pl.CostEstimate(flops=5 * 10**9, bytes_accessed=5 * 10**7, transcendentals=0),
-    )
-    corner_far, corner_near, edge_grad, node_grad, node_hidden = call(
+        (shape(edges, width, F32),) * 2 + (field, field, field, weight, weight),
+        (far, near, outer, inner, own, recv_term, pick, act, node_act, d, w_self, w_edge, w_msg, w_out),
+        scratch=(pltpu.VMEM((6 * nodes, width), BF),),
+        cost=cost(LIGHT),
+    )
+    base = call(
+        functools.partial(more_kernel, 128),
+        "inner",
+        shape(edges, width, F32),
+        (far_inner, base, pick),
+        cost=cost(HEAVY),
+    )
+    base = call(
+        functools.partial(more_kernel, 256), "near", shape(edges, width, F32), (near_pair, base, pick)
+    )
+    corner_outer, corner_inner, all_near, edge_grad, node_grad, node_hidden = call(
         main_kernel,
         "main",
-        (pair, pair, shape(edges, width, BF), block, block),
-        (
-            from_far, from_near, base, slope, pick, pick_t, node_slope, self_pre, fold, gram, d_back, obs,
-        ),
-    )
-    from_far = swapped(corner_far, "lat", True)
-    from_near = swapped(corner_near, "lat", False)
-    middle_far, middle_near, mid, partial = call(
+        (block, block, shape(3 * nodes, width, BF), shape(edges, width, BF), block, block),
+        (far_outer, base, slope, pick, pick_t, node_slope, self_pre, fold, gram, d_back, obs),
+    )
+    far_outer = swapped(corner_outer, "lat", True)
+    far_inner = swapped(corner_inner, "lat", True)
+    from_near = swapped(all_near, "lat", False)
+    middle_far, mid, partial = call(
         rest_kernel,
         "rest",
-        (block, block, shape(3 * nodes, width, F32), field),
+        (block, shape(3 * nodes, width, F32), field),
         (edge_grad, pick_t, node_grad, node_hidden, obs, d, w_recv, w_self, w_out),
-        cost=pl.CostEstimate(flops=5 * 10**9, bytes_accessed=5 * 10**7, transcendentals=0),
-    )
-    to_outer, to_inner = call(merge_kernel, "merge", (block, block), (mid, from_far, from_near))
+        cost=cost(HEAVY),
+    )
+    to_outer = call(
+        functools.partial(merge_kernel, 0), "merge_outer", block, (mid, far_outer, from_near)
+    )
+    to_inner = call(
+        functools.partial(merge_kernel, 128), "merge_inner", block, (mid, far_inner, from_near, to_outer)
+    )
     from_outer = swapped(to_outer, "lon", True)
     from_inner = swapped(to_inner, "lon", False)
     from_far = swapped(middle_far, "lat", True)
-    from_near = swapped(middle_near, "lat", False)
+    center = call(
+        center_kernel,
+        "center",
+        field,
+        (mid, from_outer),
+        cost=cost(HEAVY),
+    )
     product, sums = call(
         product_kernel,
         "product",
         (field, shape(16, 128, F32)),
-        (mid, from_near, from_far, from_outer, from_inner, partial, w_send, d, r),
+        (center, from_near, from_far, from_inner, partial, w_send, d, r),
     )
     sums = sums_everywhere(sums)
     outs = call(final_kernel, "final", (field,) * 3, (sums, x, r, d, product))

time: 67.5 us -> 62.5 us (0.926)
  starting transfers between devices: 26 us -> 21.2 us
  blocking collectives: 22.3 us -> 20.7 us
  waiting for transfers between devices: 6.1 us -> 7.26 us
    ppermute x12 -> x13, starting transfers between devices: 26 us -> 21.2 us  [swapped(): return lax.ppermute(value, ('lat', 'lon'), pairs)]
    all_to_all x2, blocking collectives: 22.3 us -> 20.7 us  [sums_everywhere(): lax.all_to_all(value, ('lat', 'lon'), 0, 0, tiled=True, axis_index_groups...]
    ppermute x12 -> x13, waiting for transfers between devices: 6.1 us -> 7.26 us  [swapped(): return lax.ppermute(value, ('lat', 'lon'), pairs)]
    pallas_call x9 -> x14, Pallas kernels: 11.9 us -> 12.2 us  [call(): pl.pallas_call(kernel, out_shape=out_shape, in_specs=[here] * first + [th...]
  transfers between devices with their start and end apart: 12 -> 13, of which waited for: 3 -> 4; matrix products, arithmetic and copies ran while one was open for 0% -> 0% of each run, Pallas kernels for 10% -> 11%
where the time goes in v5:
time: 62.5 us; the launch traced here: 62.3 us
  starting transfers between devices  21.2 us (34%)
  blocking collectives  20.7 us (33%)
  Pallas kernels  12.2 us (20%)
  waiting for transfers between devices  7.26 us (12%)
  between operations  0.8 us (1%)
    ppermute x13, starting transfers between devices, swapped(): return lax.ppermute(value, ('lat', 'lon'), pairs)  21.2 us
    all_to_all x2, blocking collectives, sums_everywhere(): lax.all_to_all(value, ('lat', 'lon'), 0, 0, tiled=True, axis_index_groups...  20.7 us
    pallas_call x14, Pallas kernels, call(): pl.pallas_call(kernel, out_shape=out_shape, in_specs=[here] * first + [th...  12.2 us
    ppermute x13, waiting for transfers between devices, swapped(): return lax.ppermute(value, ('lat', 'lon'), pairs)  7.26 us
  transfers between devices with their start and end apart: 13, of which 4 were waited for; matrix products, arithmetic and copies ran while one was open for 0% of the time, Pallas kernels for 11%

profile of v5, /device:TPU:1, one launch (start us, length us, event | category | flops | bytes accessed | tf_op | source)
XLA Modules:
  0.0 62.3 jit_solution(12446236146021271584)
XLA Ops:
  0.6 1.4 %send_term.1 = (bf16[128,512]{1,0:T(8,128)(2,1)S(1)}, s32[1,1024]{1,0:T(1,128)S(1)}, s32[1,1024]{1,0:T(1,128)S(1)}, f32[1,128]{1,0:T(1,128)S(1)}, f32[128,512]{1,0:T(8,128)S(1)}) custom-call(s32[1,1024]{1,0:T(1,128)} %bitcast.23, s32[1,1024]{1,0:T(1,128)} %bitcast.24, f32[1,128]{1,0:T(1,128)} %bitcast.25, f32[128,512]{1,0:T(8,128)} %bitcast.21, ...), custom_call_target="tpu_custom_call" | custom-call | tf_op jit(solution)/shard_map/send_term/pallas_call | solution.py:35
  2.0 2.6 %collective-permute-start.1 = (bf16[128,512]{1,0:T(8,128)(2,1)S(1)}, bf16[128,512]{1,0:T(8,128)(2,1)S(1)}, u32[]{:S(2)}, u32[]{:S(2)}) collective-permute-start(bf16[128,512]{1,0:T(8,128)(2,1)S(1)} %get-tuple-element.41.own), channel_id=1, source_target_pairs={{0,1},{1,0},{2,3},{3,2},{4,5},{5,4},{6,7},{7,6},{8,9},{9,8},{10,11... | collective-permute-start | bytes 393224 | tf_op jit(solution)/shard_map/ppermute | solution.py:243
  4.6 6.9 %collective-permute-start = (bf16[128,512]{1,0:T(8,128)(2,1)S(1)}, bf16[128,512]{1,0:T(8,128)(2,1)S(1)}, u32[]{:S(2)}, u32[]{:S(2)}) collective-permute-start(bf16[128,512]{1,0:T(8,128)(2,1)S(1)} %get-tuple-element.41.own), channel_id=1, source_target_pairs={{0,31},{1,2},{2,1},{3,4},{4,3},{5,6},{6,5},{7,8},{8,7},{9,10},{10,... | collective-permute-start | bytes 393224 | tf_op jit(solution)/shard_map/ppermute | solution.py:243
  11.5 2.4 %collective-permute-start.5 = (bf16[128,512]{1,0:T(8,128)(2,1)S(1)}, bf16[128,512]{1,0:T(8,128)(2,1)S(1)}, u32[]{:S(2)}, u32[]{:S(2)}) collective-permute-start(bf16[128,512]{1,0:T(8,128)(2,1)S(1)} %get-tuple-element.41.own), channel_id=1, source_target_pairs={{0,1},{1,0},{2,3},{3,2},{4,5},{5,4},{6,7},{7,6},{8,9},{9,8},{10,11... | collective-permute-start | bytes 393224 | tf_op jit(solution)/shard_map/ppermute | solution.py:243
  13.9 0.0 collective-permute-start.6
  13.9 2.4 %prepare.1 = (bf16[1024,1280]{1,0:T(8,128)(2,1)S(1)}, bf16[1280,1024]{1,0:T(8,128)(2,1)S(1)}, bf16[1024,512]{1,0:T(8,128)(2,1)S(1)}, bf16[128,512]{1,0:T(8,128)(...) custom-call(s32[1,1024]{1,0:T(1,128)S(1)} %get-tuple-element.42.send, ...), custom_call_target="tpu_custom_call" | custom-call | tf_op jit(solution)/shard_map/prepare/pallas_call | solution.py:35
  16.3 0.0 collective-permute-done.1.block
  16.3 1.8 %collective-permute-start.4 = (bf16[128,512]{1,0:T(8,128)(2,1)S(1)}, bf16[128,512]{1,0:T(8,128)(2,1)S(1)}, u32[]{:S(2)}, u32[]{:S(2)}) collective-permute-start(bf16[128,512]{1,0:T(8,128)(2,1)S(1)} %pass_inner.1.inner), channel_id=1, source_target_pairs={{0,1},{1,0},{2,3},{3,2},{4,5},{5,4},{6,7},{7,6},{8,9},{9,8},{10,11... | collective-permute-start | bytes 393224 | tf_op jit(solution)/shard_map/ppermute | solution.py:243
  18.1 0.0 collective-permute-done.outer
  18.1 0.1 collective-permute-start.3
  18.2 1.4 %collective-permute-start.2 = (bf16[128,512]{1,0:T(8,128)(2,1)S(1)}, bf16[128,512]{1,0:T(8,128)(2,1)S(1)}, u32[]{:S(2)}, u32[]{:S(2)}) collective-permute-start(bf16[128,512]{1,0:T(8,128)(2,1)S(1)} %get-tuple-element.46.outer), channel_id=1, source_target_pairs={{0,1},{1,0},{2,3},{3,2},{4,5},{5,4},{6,7},{7,6},{8,9},{9,8},{10,11... | collective-permute-start | bytes 393224 | tf_op jit(solution)/shard_map/ppermute | solution.py:243
  19.6 0.0 collective-permute-done.5.far
  19.6 0.0 collective-permute-done.6.near
  19.6 2.4 %base.1 = (f32[1024,512]{1,0:T(8,128)S(1)}, f32[1024,512]{1,0:T(8,128)S(1)}, f32[128,512]{1,0:T(8,128)S(1)}, f32[128,512]{1,0:T(8,128)S(1)}, f32[128,512]{1,0:T(...) custom-call(bf16[128,512]{1,0:T(8,128)(2,1)S(1)} %collective-permute-done.5.far, ...), custom_call_target="tpu_custom_call" | custom-call | flops 1000000000 | bytes 10000000 | tf_op jit(solution)/shard_map/base/pallas_call | solution.py:35
  22.0 0.0 collective-permute-done.4.part
  22.0 0.4 inner.1.base
  22.4 0.0 collective-permute-done.3.part
  22.5 0.4 near.1.base
  22.9 0.1 collective-permute-done.2.far_outer
  23.0 2.3 %main.1 = (bf16[128,512]{1,0:T(8,128)(2,1)S(1)}, bf16[128,512]{1,0:T(8,128)(2,1)S(1)}, bf16[384,512]{1,0:T(8,128)(2,1)S(1)}, bf16[1024,512]{1,0:T(8,128)(2,1)S(1...) custom-call(bf16[128,512]{1,0:T(8,128)(2,1)S(1)} %collective-permute-done.2.far_outer, ...), custom_call_target="tpu_custom_call" | custom-call | tf_op jit(solution)/shard_map/main/pallas_call | solution.py:35
  25.3 0.8 %collective-permute-start.8 = (bf16[384,512]{1,0:T(8,128)(2,1)S(1)}, bf16[384,512]{1,0:T(8,128)(2,1)S(1)}, u32[]{:S(2)}, u32[]{:S(2)}) collective-permute-start(bf16[384,512]{1,0:T(8,128)(2,1)S(1)} %get-tuple-element.70), channel_id=1, source_target_pairs={{0,32},{1,33},{2,34},{3,35},{4,36},{5,37},{6,38},{7,39},{8,40},{9,... | collective-permute-start | bytes 1179656 | tf_op jit(solution)/shard_map/ppermute | solution.py:243
  26.1 0.4 collective-permute-start.7
  26.5 1.3 %collective-permute-start.11 = (bf16[128,512]{1,0:T(8,128)(2,1)S(1)}, bf16[128,512]{1,0:T(8,128)(2,1)S(1)}, u32[]{:S(2)}, u32[]{:S(2)}) collective-permute-start(bf16[128,512]{1,0:T(8,128)(2,1)S(1)} %get-tuple-element.72), channel_id=1, source_target_pairs={{0,1},{1,0},{2,3},{3,2},{4,5},{5,4},{6,7},{7,6},{8,9},{9,8},{10,11... | collective-permute-start | bytes 393224 | tf_op jit(solution)/shard_map/ppermute | solution.py:243
  27.8 1.2 %rest.1 = (bf16[128,512]{1,0:T(8,128)(2,1)S(1)}, f32[384,512]{1,0:T(8,128)S(1)}, f32[128,512]{1,0:T(8,128)S(1)}) custom-call(bf16[1024,512]{1,0:T(8,128)(2,1)S(1)} %get-tuple-element.64.edge_grad, bf16[1280,1024]{1,0:T(8,128)(2,1)S(1)} %get-tuple-element.57.pick_t, bf16[128,512]{1,0:T(8,128)(2,1)S(1)} %get-tuple-element.65.node_grad, ...), custom_call_target="tpu_custom_call" | custom-call | flops 5000000000 | bytes 50000000 | tf_op jit(solution)/shard_map/rest/pallas_call | solution.py:35
  29.1 1.7 %collective-permute-done.7.from_far = bf16[128,512]{1,0:T(8,128)(2,1)S(1)} collective-permute-done((bf16[128,512]{1,0:T(8,128)(2,1)S(1)}, bf16[128,512]{1,0:T(8,128)(2,1)S(1)}, u32[]{:S(2)}, u32[]{:S(2)}) %collective-permute-start.7) | collective-permute-done | bytes 131104 | tf_op jit(solution)/shard_map/ppermute | solution.py:243
  30.8 0.0 collective-permute-done.8.from_near
  30.8 2.3 %collective-permute-start.9 = (bf16[128,512]{1,0:T(8,128)(2,1)S(1)}, bf16[128,512]{1,0:T(8,128)(2,1)S(1)}, u32[]{:S(2)}, u32[]{:S(2)}) collective-permute-start(bf16[128,512]{1,0:T(8,128)(2,1)S(1)} %merge_outer.1.refs_0_), channel_id=1, source_target_pairs={{0,31},{1,2},{2,1},{3,4},{4,3},{5,6},{6,5},{7,8},{8,7},{9,10},{10,... | collective-permute-start | bytes 393224 | tf_op jit(solution)/shard_map/ppermute | solution.py:243
  33.1 1.2 %collective-permute-start.10 = (bf16[128,512]{1,0:T(8,128)(2,1)S(1)}, bf16[128,512]{1,0:T(8,128)(2,1)S(1)}, u32[]{:S(2)}, u32[]{:S(2)}) collective-permute-start(bf16[128,512]{1,0:T(8,128)(2,1)S(1)} %get-tuple-element.71), channel_id=1, source_target_pairs={{0,1},{1,0},{2,3},{3,2},{4,5},{5,4},{6,7},{7,6},{8,9},{9,8},{10,11... | collective-permute-start | bytes 393224 | tf_op jit(solution)/shard_map/ppermute | solution.py:243
  34.4 0.0 collective-permute-done.11.from_far
  34.4 0.1 merge_inner.1
  34.4 0.0 copy-start
  34.4 0.0 copy-start.1
  34.5 0.1 collective-permute-start.12
  34.6 4.4 %collective-permute-done.9.from_outer = bf16[128,512]{1,0:T(8,128)(2,1)S(1)} collective-permute-done((bf16[128,512]{1,0:T(8,128)(2,1)S(1)}, bf16[128,512]{1,0:T(8,128)(2,1)S(1)}, u32[]{:S(2)}, u32[]{:S(2)}) %collective-permute-start.9) | collective-permute-done | bytes 131104 | tf_op jit(solution)/shard_map/ppermute | solution.py:243
  39.0 0.0 copy-start.2
  39.0 0.0 collective-permute-done.10.from_far
  39.0 1.1 %collective-permute-done.12.from_inner = bf16[128,512]{1,0:T(8,128)(2,1)S(1)} collective-permute-done((bf16[128,512]{1,0:T(8,128)(2,1)S(1)}, bf16[128,512]{1,0:T(8,128)(2,1)S(1)}, u32[]{:S(2)}, u32[]{:S(2)}) %collective-permute-start.12) | collective-permute-done | bytes 131104 | tf_op jit(solution)/shard_map/ppermute | solution.py:243
  40.1 0.0 copy-done
  40.1 0.0 copy-done.1
  40.1 0.5 product.1
  40.5 10.9 %all_to_all.17 = f32[16,1,128]{2,1,0:T(1,128)S(1)} all-to-all(f32[16,1,128]{2,1,0:T(1,128)S(1)} %bitcast.19), channel_id=1, replica_groups={{0,1,2,3,4,5,6,7,32,33,34,35,36,37,38,39},{8,9,10,11,12,13,14,15,40,41,..., dimensions={0} | all-to-all | bytes 16384 | tf_op jit(solution)/shard_map/all_to_all | solution.py:259
  51.5 9.8 %all_to_all.18 = f32[16,1,128]{2,1,0:T(1,128)S(1)} all-to-all(f32[16,1,128]{2,1,0:T(1,128)S(1)} %broadcast_in_dim.2), channel_id=1, replica_groups={{0,8,16,24,64,72,80,88,128,136,144,152,192,200,208,216},{1,9,17,25,65,7..., dimensions={0} | all-to-all | bytes 16384 | tf_op jit(solution)/shard_map/all_to_all | solution.py:262
  61.2 0.0 copy-done.2
  61.2 1.0 %final.1 = (f32[128,512]{1,0:T(8,128)}, f32[128,512]{1,0:T(8,128)}, f32[128,512]{1,0:T(8,128)}) custom-call(f32[16,128]{1,0:T(8,128)S(1)} %bitcast.18, f32[128,512]{1,0:T(8,128)S(1)} %bitcast.17, f32[128,512]{1,0:T(8,128)S(1)} %bitcast.16, f32[128,512]{1,0:T(8,128)S(1)} %get-tuple-element.44.d, f32[128,512]{1,0:T(8,128)S(1)} %get-tuple-element.75.product), custom_call_target="tpu_custom_call" | custom-call | tf_op jit(solution)/shard_map/final/pallas_call | solution.py:35
  (6 shorter events, 0.1 us)
Async XLA Ops:
  2.0 14.2 %collective-permute-start.1 = (bf16[128,512]{1,0:T(8,128)(2,1)S(1)}, bf16[128,512]{1,0:T(8,128)(2,1)S(1)}, u32[]{:S(2)}, u32[]{:S(2)}) collective-permute-start(bf16[128,512]{1,0:T(8,128)(2,1)S(1)} %get-tuple-element.41.own), channel_id=1, source_target_pairs={{0,1},{1,0},{2,3},{3,2},{4,5},{5,4},{6,7},{7,6},{8,9},{9,8},{10,11... | collective-permute-start | bytes 393224 | tf_op jit(solution)/shard_map/ppermute | solution.py:243
  4.6 13.5 %collective-permute-start = (bf16[128,512]{1,0:T(8,128)(2,1)S(1)}, bf16[128,512]{1,0:T(8,128)(2,1)S(1)}, u32[]{:S(2)}, u32[]{:S(2)}) collective-permute-start(bf16[128,512]{1,0:T(8,128)(2,1)S(1)} %get-tuple-element.41.own), channel_id=1, source_target_pairs={{0,31},{1,2},{2,1},{3,4},{4,3},{5,6},{6,5},{7,8},{8,7},{9,10},{10,... | collective-permute-start | bytes 393224 | tf_op jit(solution)/shard_map/ppermute | solution.py:243
  11.5 8.1 %collective-permute-start.5 = (bf16[128,512]{1,0:T(8,128)(2,1)S(1)}, bf16[128,512]{1,0:T(8,128)(2,1)S(1)}, u32[]{:S(2)}, u32[]{:S(2)}) collective-permute-start(bf16[128,512]{1,0:T(8,128)(2,1)S(1)} %get-tuple-element.41.own), channel_id=1, source_target_pairs={{0,1},{1,0},{2,3},{3,2},{4,5},{5,4},{6,7},{7,6},{8,9},{9,8},{10,11... | collective-permute-start | bytes 393224 | tf_op jit(solution)/shard_map/ppermute | solution.py:243
  13.9 5.7 %collective-permute-start.6 = (bf16[128,512]{1,0:T(8,128)(2,1)S(1)}, bf16[128,512]{1,0:T(8,128)(2,1)S(1)}, u32[]{:S(2)}, u32[]{:S(2)}) collective-permute-start(bf16[128,512]{1,0:T(8,128)(2,1)S(1)} %get-tuple-element.41.own), channel_id=1, source_target_pairs={{0,32},{1,33},{2,34},{3,35},{4,36},{5,37},{6,38},{7,39},{8,40},{9,... | collective-permute-start | bytes 393224 | tf_op jit(solution)/shard_map/ppermute | solution.py:243
  16.3 5.7 %collective-permute-start.4 = (bf16[128,512]{1,0:T(8,128)(2,1)S(1)}, bf16[128,512]{1,0:T(8,128)(2,1)S(1)}, u32[]{:S(2)}, u32[]{:S(2)}) collective-permute-start(bf16[128,512]{1,0:T(8,128)(2,1)S(1)} %pass_inner.1.inner), channel_id=1, source_target_pairs={{0,1},{1,0},{2,3},{3,2},{4,5},{5,4},{6,7},{7,6},{8,9},{9,8},{10,11... | collective-permute-start | bytes 393224 | tf_op jit(solution)/shard_map/ppermute | solution.py:243
  18.1 4.3 %collective-permute-start.3 = (bf16[256,512]{1,0:T(8,128)(2,1)S(1)}, bf16[256,512]{1,0:T(8,128)(2,1)S(1)}, u32[]{:S(2)}, u32[]{:S(2)}) collective-permute-start(bf16[256,512]{1,0:T(8,128)(2,1)S(1)} %get-tuple-element.47), channel_id=1, source_target_pairs={{0,32},{1,33},{2,34},{3,35},{4,36},{5,37},{6,38},{7,39},{8,40},{9,... | collective-permute-start | bytes 786440 | tf_op jit(solution)/shard_map/ppermute | solution.py:243
  18.2 4.8 %collective-permute-start.2 = (bf16[128,512]{1,0:T(8,128)(2,1)S(1)}, bf16[128,512]{1,0:T(8,128)(2,1)S(1)}, u32[]{:S(2)}, u32[]{:S(2)}) collective-permute-start(bf16[128,512]{1,0:T(8,128)(2,1)S(1)} %get-tuple-element.46.outer), channel_id=1, source_target_pairs={{0,1},{1,0},{2,3},{3,2},{4,5},{5,4},{6,7},{7,6},{8,9},{9,8},{10,11... | collective-permute-start | bytes 393224 | tf_op jit(solution)/shard_map/ppermute | solution.py:243
  25.3 5.5 %collective-permute-start.8 = (bf16[384,512]{1,0:T(8,128)(2,1)S(1)}, bf16[384,512]{1,0:T(8,128)(2,1)S(1)}, u32[]{:S(2)}, u32[]{:S(2)}) collective-permute-start(bf16[384,512]{1,0:T(8,128)(2,1)S(1)} %get-tuple-element.70), channel_id=1, source_target_pairs={{0,32},{1,33},{2,34},{3,35},{4,36},{5,37},{6,38},{7,39},{8,40},{9,... | collective-permute-start | bytes 1179656 | tf_op jit(solution)/shard_map/ppermute | solution.py:243
  26.1 4.7 %collective-permute-start.7 = (bf16[128,512]{1,0:T(8,128)(2,1)S(1)}, bf16[128,512]{1,0:T(8,128)(2,1)S(1)}, u32[]{:S(2)}, u32[]{:S(2)}) collective-permute-start(bf16[128,512]{1,0:T(8,128)(2,1)S(1)} %get-tuple-element.69), channel_id=1, source_target_pairs={{0,1},{1,0},{2,3},{3,2},{4,5},{5,4},{6,7},{7,6},{8,9},{9,8},{10,11... | collective-permute-start | bytes 393224 | tf_op jit(solution)/shard_map/ppermute | solution.py:243
  26.5 7.9 %collective-permute-start.11 = (bf16[128,512]{1,0:T(8,128)(2,1)S(1)}, bf16[128,512]{1,0:T(8,128)(2,1)S(1)}, u32[]{:S(2)}, u32[]{:S(2)}) collective-permute-start(bf16[128,512]{1,0:T(8,128)(2,1)S(1)} %get-tuple-element.72), channel_id=1, source_target_pairs={{0,1},{1,0},{2,3},{3,2},{4,5},{5,4},{6,7},{7,6},{8,9},{9,8},{10,11... | collective-permute-start | bytes 393224 | tf_op jit(solution)/shard_map/ppermute | solution.py:243
  30.8 8.1 %collective-permute-start.9 = (bf16[128,512]{1,0:T(8,128)(2,1)S(1)}, bf16[128,512]{1,0:T(8,128)(2,1)S(1)}, u32[]{:S(2)}, u32[]{:S(2)}) collective-permute-start(bf16[128,512]{1,0:T(8,128)(2,1)S(1)} %merge_outer.1.refs_0_), channel_id=1, source_target_pairs={{0,31},{1,2},{2,1},{3,4},{4,3},{5,6},{6,5},{7,8},{8,7},{9,10},{10,... | collective-permute-start | bytes 393224 | tf_op jit(solution)/shard_map/ppermute | solution.py:243
  33.1 5.8 %collective-permute-start.10 = (bf16[128,512]{1,0:T(8,128)(2,1)S(1)}, bf16[128,512]{1,0:T(8,128)(2,1)S(1)}, u32[]{:S(2)}, u32[]{:S(2)}) collective-permute-start(bf16[128,512]{1,0:T(8,128)(2,1)S(1)} %get-tuple-element.71), channel_id=1, source_target_pairs={{0,1},{1,0},{2,3},{3,2},{4,5},{5,4},{6,7},{7,6},{8,9},{9,8},{10,11... | collective-permute-start | bytes 393224 | tf_op jit(solution)/shard_map/ppermute | solution.py:243
  34.4 5.6 %copy-start = (bf16[512,512]{1,0:T(8,128)(2,1)S(1)}, bf16[512,512]{1,0:T(8,128)(2,1)}, u32[]{:S(2)}) copy-start(bf16[512,512]{1,0:T(8,128)(2,1)} %w_send.1) | copy-start | bytes 1572868
  34.4 5.6 %copy-start.1 = (f32[1,1,128,512]{3,2,1,0:T(8,128)S(1)}, f32[1,1,128,512]{3,2,1,0:T(8,128)}, u32[]{:S(2)}) copy-start(f32[1,1,128,512]{3,2,1,0:T(8,128)} %param.15) | copy-start | bytes 786436
  34.5 5.6 %collective-permute-start.12 = (bf16[128,512]{1,0:T(8,128)(2,1)S(1)}, bf16[128,512]{1,0:T(8,128)(2,1)S(1)}, u32[]{:S(2)}, u32[]{:S(2)}) collective-permute-start(bf16[128,512]{1,0:T(8,128)(2,1)S(1)} %merge_inner.1), channel_id=1, source_target_pairs={{0,1},{1,0},{2,3},{3,2},{4,5},{5,4},{6,7},{7,6},{8,9},{9,8},{10,11... | collective-permute-start | bytes 393224 | tf_op jit(solution)/shard_map/ppermute | solution.py:243
  39.0 22.3 %copy-start.2 = (f32[1,1,128,512]{3,2,1,0:T(8,128)S(1)}, f32[1,1,128,512]{3,2,1,0:T(8,128)}, u32[]{:S(2)}) copy-start(f32[1,1,128,512]{3,2,1,0:T(8,128)} %param.14) | copy-start | bytes 786436

commit v6 on v5

--- a/solution.py
+++ b/solution.py
@@ -63,7 +63,7 @@
     near = 1 - 2 * lax.rem(lax.axis_index("lat"), 2)
     inner = 1 - 2 * lax.rem(lax.axis_index("lon"), 2)
     places = (
-        (-near, -inner), (-near, inner), (near, -inner), (near, inner), (near, 0), (-near, 0),
+        (-near, -inner), (near, -inner), (-near, inner), (near, inner), (near, 0), (-near, 0),
         (0, -inner), (0, inner), (0, 0),
     )
     return [(lat + 1) * 3 + lon + 1 for lat, lon in places]
@@ -111,12 +111,6 @@
     out[...] = block[...]
 
 
-def stack_kernel(outer, inner, outer_out, pair):
-    outer_out[...] = outer[...]
-    pair[0:128, :] = outer[...]
-    pair[128:256, :] = inner[...]
-
-
 def gathered(pick, first, parts, table):
     row = 0
     for part in parts:
@@ -139,8 +133,8 @@
     base[...] = gathered(pick, 512, (near, far, outer, inner, own, recv_term), table)
 
 
-def more_kernel(first, part, base, pick, more):
-    more[...] = base[...] + dot(pick[:, first : first + part.shape[0]], part[...])
+def inner_kernel(far_inner, near_inner, base, pick, more, table):
+    more[...] = base[...] + gathered(pick, 256, (far_inner, near_inner), table)
 
 
 def lanes_of(row, width):
@@ -150,10 +144,10 @@
 
 
 def main_kernel(
-    far_outer, base, slope, pick, pick_t, node_slope, self_pre, fold, gram, d_back, obs,
-    corner_outer, corner_inner, all_near, edge_grad, node_grad, node_hidden,
-):
-    edge_input = base[...] + dot(pick[:, 0:128], far_outer[...])
+    far_outer, near_outer, base, slope, pick, pick_t, node_slope, self_pre, fold, gram, d_back, obs,
+    corner_outer, edge_grad, node_grad, node_hidden, table,
+):
+    edge_input = base[...] + gathered(pick, 0, (far_outer, near_outer), table)
     hidden = (slope[...] * edge_input).astype(BF)
     hidden_sum = dot(pick_t[1152:, :], hidden).astype(BF)
     pre_node = self_pre[...] + dot(hidden_sum, fold[...])
@@ -165,10 +159,14 @@
     edge_back = dot_back(grad, fold[...]).astype(BF)
     e_grad = (dot(pick[:, 1152:], edge_back) * slope[...]).astype(BF)
     edge_grad[...] = e_grad
-    sums = dot(pick_t[0:640, :], e_grad).astype(BF)
-    corner_outer[...] = sums[0:128, :]
+    corner_outer[...] = dot(pick_t[0:128, :], e_grad).astype(BF)
+
+
+def corner_kernel(edge_grad, pick_t, corner_inner, all_near):
+    sums = dot(pick_t[128:640, :], edge_grad[...]).astype(BF)
     corner_inner[...] = sums[128:256, :]
-    all_near[...] = sums[256:640, :]
+    all_near[0:128, :] = sums[0:128, :]
+    all_near[128:384, :] = sums[256:512, :]
 
 
 def rest_kernel(
@@ -196,7 +194,7 @@
 
 
 def product_kernel(
-    center, from_near, from_far, from_inner, partial, w_send, d, r, product, sums
+    center, from_near, from_inner, from_far, partial, w_send, d, r, product, sums
 ):
     total = center[...] + from_near[256:384, :].astype(F32)
     for part in (from_far, from_inner):
@@ -315,9 +313,10 @@
     pair = shape(2 * nodes, width, BF)
     inner = call(pass_kernel, "pass_inner", block, (inner, recv_term))
     far_inner = swapped(inner, "lat", True)
-    outer, beside = call(stack_kernel, "stack", (block, pair), (outer, inner))
+    near_inner = swapped(inner, "lat", False)
+    outer = call(pass_kernel, "pass_outer", block, (outer, inner))
     far_outer = swapped(outer, "lat", True)
-    near_pair = swapped(beside, "lat", False)
+    near_outer = swapped(outer, "lat", False)
     base, slope, node_slope, self_pre, d_back, fold, gram = call(
         base_kernel,
         "base",
@@ -327,22 +326,27 @@
         cost=cost(LIGHT),
     )
     base = call(
-        functools.partial(more_kernel, 128),
+        inner_kernel,
         "inner",
         shape(edges, width, F32),
-        (far_inner, base, pick),
+        (far_inner, near_inner, base, pick),
+        scratch=(pltpu.VMEM((2 * nodes, width), BF),),
         cost=cost(HEAVY),
     )
-    base = call(
-        functools.partial(more_kernel, 256), "near", shape(edges, width, F32), (near_pair, base, pick)
-    )
-    corner_outer, corner_inner, all_near, edge_grad, node_grad, node_hidden = call(
+    far_outer = call(pass_kernel, "gate", block, (far_outer, base), cost=cost(HEAVY))
+    corner_outer, edge_grad, node_grad, node_hidden = call(
         main_kernel,
         "main",
-        (block, block, shape(3 * nodes, width, BF), shape(edges, width, BF), block, block),
-        (far_outer, base, slope, pick, pick_t, node_slope, self_pre, fold, gram, d_back, obs),
+        (block, shape(edges, width, BF), block, block),
+        (
+            far_outer, near_outer, base, slope, pick, pick_t, node_slope, self_pre, fold, gram, d_back, obs,
+        ),
+        scratch=(pltpu.VMEM((2 * nodes, width), BF),),
     )
     far_outer = swapped(corner_outer, "lat", True)
+    corner_inner, all_near = call(
+        corner_kernel, "corner", (block, shape(3 * nodes, width, BF)), (edge_grad, pick_t)
+    )
     far_inner = swapped(corner_inner, "lat", True)
     from_near = swapped(all_near, "lat", False)
     middle_far, mid, partial = call(
@@ -350,8 +354,9 @@
         "rest",
         (block, shape(3 * nodes, width, F32), field),
         (edge_grad, pick_t, node_grad, node_hidden, obs, d, w_recv, w_self, w_out),
-        cost=cost(HEAVY),
-    )
+        cost=cost(LIGHT // 100),
+    )
+    far_outer = call(pass_kernel, "gate", block, (far_outer, obs), cost=cost(HEAVY))
     to_outer = call(
         functools.partial(merge_kernel, 0), "merge_outer", block, (mid, far_outer, from_near)
     )
@@ -372,7 +377,7 @@
         product_kernel,
         "product",
         (field, shape(16, 128, F32)),
-        (center, from_near, from_far, from_inner, partial, w_send, d, r),
+        (center, from_near, from_inner, from_far, partial, w_send, d, r),
     )
     sums = sums_everywhere(sums)
     outs = call(final_kernel, "final", (field,) * 3, (sums, x, r, d, product))

time: 62.5 us -> 61.2 us (0.979)
  waiting for transfers between devices: 7.26 us -> 6.07 us
    ppermute x13 -> x14, waiting for transfers between devices: 7.26 us -> 6.07 us  [swapped(): return lax.ppermute(value, ('lat', 'lon'), pairs)]
    ppermute x13 -> x14, starting transfers between devices: 21.2 us -> 21.5 us  [swapped(): return lax.ppermute(value, ('lat', 'lon'), pairs)]
    pallas_call x14 -> x16, Pallas kernels: 12.2 us -> 12 us  [call(): pl.pallas_call(kernel, out_shape=out_shape, in_specs=[here] * first + [th...]
  transfers between devices with their start and end apart: 13 -> 14, of which waited for: 4 -> 5; matrix products, arithmetic and copies ran while one was open for 0% -> 0% of each run, Pallas kernels for 11% -> 12%
where the time goes in v6:
time: 61.2 us; the launch traced here: 61 us
  starting transfers between devices  21.5 us (35%)
  blocking collectives  20.5 us (33%)
  Pallas kernels  12 us (20%)
  waiting for transfers between devices  6.07 us (10%)
  between operations  0.81 us (1%)
    ppermute x14, starting transfers between devices, swapped(): return lax.ppermute(value, ('lat', 'lon'), pairs)  21.5 us
    all_to_all x2, blocking collectives, sums_everywhere(): lax.all_to_all(value, ('lat', 'lon'), 0, 0, tiled=True, axis_index_groups...  20.5 us
    pallas_call x16, Pallas kernels, call(): pl.pallas_call(kernel, out_shape=out_shape, in_specs=[here] * first + [th...  12 us
    ppermute x14, waiting for transfers between devices, swapped(): return lax.ppermute(value, ('lat', 'lon'), pairs)  6.07 us
  transfers between devices with their start and end apart: 14, of which 5 were waited for; matrix products, arithmetic and copies ran while one was open for 0% of the time, Pallas kernels for 12%

profile of v6, /device:TPU:1, one launch (start us, length us, event | category | flops | bytes accessed | tf_op | source)
XLA Modules:
  0.0 61.0 jit_solution(8417016121282481249)
XLA Ops:
  0.6 1.4 %send_term.1 = (bf16[128,512]{1,0:T(8,128)(2,1)S(1)}, s32[1,1024]{1,0:T(1,128)S(1)}, s32[1,1024]{1,0:T(1,128)S(1)}, f32[1,128]{1,0:T(1,128)S(1)}, f32[128,512]{1,0:T(8,128)S(1)}) custom-call(s32[1,1024]{1,0:T(1,128)} %bitcast.23, s32[1,1024]{1,0:T(1,128)} %bitcast.24, f32[1,128]{1,0:T(1,128)} %bitcast.25, f32[128,512]{1,0:T(8,128)} %bitcast.21, ...), custom_call_target="tpu_custom_call" | custom-call | tf_op jit(solution)/shard_map/send_term/pallas_call | solution.py:35
  2.0 2.6 %collective-permute-start.1 = (bf16[128,512]{1,0:T(8,128)(2,1)S(1)}, bf16[128,512]{1,0:T(8,128)(2,1)S(1)}, u32[]{:S(2)}, u32[]{:S(2)}) collective-permute-start(bf16[128,512]{1,0:T(8,128)(2,1)S(1)} %get-tuple-element.39.own), channel_id=1, source_target_pairs={{0,1},{1,0},{2,3},{3,2},{4,5},{5,4},{6,7},{7,6},{8,9},{9,8},{10,11... | collective-permute-start | bytes 393224 | tf_op jit(solution)/shard_map/ppermute | solution.py:241
  4.6 6.9 %collective-permute-start = (bf16[128,512]{1,0:T(8,128)(2,1)S(1)}, bf16[128,512]{1,0:T(8,128)(2,1)S(1)}, u32[]{:S(2)}, u32[]{:S(2)}) collective-permute-start(bf16[128,512]{1,0:T(8,128)(2,1)S(1)} %get-tuple-element.39.own), channel_id=1, source_target_pairs={{0,31},{1,2},{2,1},{3,4},{4,3},{5,6},{6,5},{7,8},{8,7},{9,10},{10,... | collective-permute-start | bytes 393224 | tf_op jit(solution)/shard_map/ppermute | solution.py:241
  11.5 2.4 %collective-permute-start.5 = (bf16[128,512]{1,0:T(8,128)(2,1)S(1)}, bf16[128,512]{1,0:T(8,128)(2,1)S(1)}, u32[]{:S(2)}, u32[]{:S(2)}) collective-permute-start(bf16[128,512]{1,0:T(8,128)(2,1)S(1)} %get-tuple-element.39.own), channel_id=1, source_target_pairs={{0,1},{1,0},{2,3},{3,2},{4,5},{5,4},{6,7},{7,6},{8,9},{9,8},{10,11... | collective-permute-start | bytes 393224 | tf_op jit(solution)/shard_map/ppermute | solution.py:241
  13.9 0.0 collective-permute-start.6
  13.9 2.4 %prepare.1 = (bf16[1024,1280]{1,0:T(8,128)(2,1)S(1)}, bf16[1280,1024]{1,0:T(8,128)(2,1)S(1)}, bf16[1024,512]{1,0:T(8,128)(2,1)S(1)}, bf16[128,512]{1,0:T(8,128)(...) custom-call(s32[1,1024]{1,0:T(1,128)S(1)} %get-tuple-element.40.send, ...), custom_call_target="tpu_custom_call" | custom-call | tf_op jit(solution)/shard_map/prepare/pallas_call | solution.py:35
  16.3 0.0 collective-permute-done.1.block
  16.3 1.8 %collective-permute-start.3 = (bf16[128,512]{1,0:T(8,128)(2,1)S(1)}, bf16[128,512]{1,0:T(8,128)(2,1)S(1)}, u32[]{:S(2)}, u32[]{:S(2)}) collective-permute-start(bf16[128,512]{1,0:T(8,128)(2,1)S(1)} %pass_inner.1.after.inner), channel_id=1, source_target_pairs={{0,1},{1,0},{2,3},{3,2},{4,5},{5,4},{6,7},{7,6},{8,9},{9,8},{10,11... | collective-permute-start | bytes 393224 | tf_op jit(solution)/shard_map/ppermute | solution.py:241
  18.1 0.0 collective-permute-start.4
  18.1 0.0 collective-permute-done.block
  18.1 1.5 %collective-permute-start.2 = (bf16[128,512]{1,0:T(8,128)(2,1)S(1)}, bf16[128,512]{1,0:T(8,128)(2,1)S(1)}, u32[]{:S(2)}, u32[]{:S(2)}) collective-permute-start(bf16[128,512]{1,0:T(8,128)(2,1)S(1)} %pass_outer.1.outer), channel_id=1, source_target_pairs={{0,1},{1,0},{2,3},{3,2},{4,5},{5,4},{6,7},{7,6},{8,9},{9,8},{10,11... | collective-permute-start | bytes 393224 | tf_op jit(solution)/shard_map/ppermute | solution.py:241
  19.6 0.0 collective-permute-done.5.far
  19.6 0.0 collective-permute-start.7
  19.6 0.0 collective-permute-done.6.near
  19.6 2.4 %base.1 = (f32[1024,512]{1,0:T(8,128)S(1)}, f32[1024,512]{1,0:T(8,128)S(1)}, f32[128,512]{1,0:T(8,128)S(1)}, f32[128,512]{1,0:T(8,128)S(1)}, f32[128,512]{1,0:T(...) custom-call(bf16[128,512]{1,0:T(8,128)(2,1)S(1)} %collective-permute-done.5.far, ...), custom_call_target="tpu_custom_call" | custom-call | flops 1000000000 | bytes 10000000 | tf_op jit(solution)/shard_map/base/pallas_call | solution.py:35
  22.0 0.0 collective-permute-done.3.far_inner
  22.0 0.0 collective-permute-done.4.near_inner
  22.0 0.4 inner.1.after.base
  22.4 0.4 collective-permute-done.2.block
  22.9 0.0 collective-permute-done.7.near_outer
  22.9 1.8 %main.1 = (bf16[128,512]{1,0:T(8,128)(2,1)S(1)}, bf16[1024,512]{1,0:T(8,128)(2,1)S(1)}, bf16[128,512]{1,0:T(8,128)(2,1)S(1)}, bf16[128,512]{1,0:T(8,128)(2,1)S(1)}) custom-call(bf16[128,512]{1,0:T(8,128)(2,1)S(1)} %gate.2.far_outer, bf16[128,512]{1,0:T(8,128)(2,1)S(1)} %collective-permute-done.7.near_outer, f32[1024,512]{1,0:T(8,128)S(1)} %inner.1.after.base, ...), custom_call_target="tpu_custom_call" | custom-call | tf_op jit(solution)/shard_map/main/pallas_call | solution.py:35
  24.7 1.2 %collective-permute-start.8 = (bf16[128,512]{1,0:T(8,128)(2,1)S(1)}, bf16[128,512]{1,0:T(8,128)(2,1)S(1)}, u32[]{:S(2)}, u32[]{:S(2)}) collective-permute-start(bf16[128,512]{1,0:T(8,128)(2,1)S(1)} %get-tuple-element.65), channel_id=1, source_target_pairs={{0,1},{1,0},{2,3},{3,2},{4,5},{5,4},{6,7},{7,6},{8,9},{9,8},{10,11... | collective-permute-start | bytes 393224 | tf_op jit(solution)/shard_map/ppermute | solution.py:241
  25.9 0.7 %corner.1 = (bf16[128,512]{1,0:T(8,128)(2,1)S(1)}, bf16[384,512]{1,0:T(8,128)(2,1)S(1)}) custom-call(bf16[1024,512]{1,0:T(8,128)(2,1)S(1)} %get-tuple-element.60.edge_grad, bf16[1280,1024]{1,0:T(8,128)(2,1)S(1)} %get-tuple-element.53.pick_t), custom_call_target="tpu_custom_call" | custom-call | tf_op jit(solution)/shard_map/corner/pallas_call | solution.py:35
  26.6 0.1 collective-permute-start.9
  26.7 1.3 %collective-permute-start.11 = (bf16[128,512]{1,0:T(8,128)(2,1)S(1)}, bf16[128,512]{1,0:T(8,128)(2,1)S(1)}, u32[]{:S(2)}, u32[]{:S(2)}) collective-permute-start(bf16[128,512]{1,0:T(8,128)(2,1)S(1)} %get-tuple-element.67), channel_id=1, source_target_pairs={{0,1},{1,0},{2,3},{3,2},{4,5},{5,4},{6,7},{7,6},{8,9},{9,8},{10,11... | collective-permute-start | bytes 393224 | tf_op jit(solution)/shard_map/ppermute | solution.py:241
  28.0 1.2 %rest.1 = (bf16[128,512]{1,0:T(8,128)(2,1)S(1)}, f32[384,512]{1,0:T(8,128)S(1)}, f32[128,512]{1,0:T(8,128)S(1)}) custom-call(bf16[1024,512]{1,0:T(8,128)(2,1)S(1)} %get-tuple-element.60.edge_grad, bf16[1280,1024]{1,0:T(8,128)(2,1)S(1)} %get-tuple-element.53.pick_t, bf16[128,512]{1,0:T(8,128)(2,1)S(1)} %get-tuple-element.61.node_grad, ...), custom_call_target="tpu_custom_call" | custom-call | flops 10000000 | bytes 100000 | tf_op jit(solution)/shard_map/rest/pallas_call | solution.py:35
  29.3 0.2 collective-permute-done.8.block
  29.5 0.0 collective-permute-done.9.from_near
  29.6 2.7 %collective-permute-start.10 = (bf16[128,512]{1,0:T(8,128)(2,1)S(1)}, bf16[128,512]{1,0:T(8,128)(2,1)S(1)}, u32[]{:S(2)}, u32[]{:S(2)}) collective-permute-start(bf16[128,512]{1,0:T(8,128)(2,1)S(1)} %merge_outer.1.refs_0_), channel_id=1, source_target_pairs={{0,31},{1,2},{2,1},{3,4},{4,3},{5,6},{6,5},{7,8},{8,7},{9,10},{10,... | collective-permute-start | bytes 393224 | tf_op jit(solution)/shard_map/ppermute | solution.py:241
  32.3 1.1 %collective-permute-start.13 = (bf16[128,512]{1,0:T(8,128)(2,1)S(1)}, bf16[128,512]{1,0:T(8,128)(2,1)S(1)}, u32[]{:S(2)}, u32[]{:S(2)}) collective-permute-start(bf16[128,512]{1,0:T(8,128)(2,1)S(1)} %get-tuple-element.68), channel_id=1, source_target_pairs={{0,1},{1,0},{2,3},{3,2},{4,5},{5,4},{6,7},{7,6},{8,9},{9,8},{10,11... | collective-permute-start | bytes 393224 | tf_op jit(solution)/shard_map/ppermute | solution.py:241
  33.3 0.0 collective-permute-done.11.from_far
  33.3 0.1 merge_inner.1
  33.4 0.0 copy-start
  33.4 0.0 copy-start.1
  33.4 0.1 collective-permute-start.12
  33.5 3.3 %collective-permute-done.10.from_outer = bf16[128,512]{1,0:T(8,128)(2,1)S(1)} collective-permute-done((bf16[128,512]{1,0:T(8,128)(2,1)S(1)}, bf16[128,512]{1,0:T(8,128)(2,1)S(1)}, u32[]{:S(2)}, u32[]{:S(2)}) %collective-permute-start.10) | collective-permute-done | bytes 131104 | tf_op jit(solution)/shard_map/ppermute | solution.py:241
  36.8 0.0 copy-start.2
  36.9 0.1 collective-permute-done.13.from_far
  36.9 2.0 %collective-permute-done.12.from_inner = bf16[128,512]{1,0:T(8,128)(2,1)S(1)} collective-permute-done((bf16[128,512]{1,0:T(8,128)(2,1)S(1)}, bf16[128,512]{1,0:T(8,128)(2,1)S(1)}, u32[]{:S(2)}, u32[]{:S(2)}) %collective-permute-start.12) | collective-permute-done | bytes 131104 | tf_op jit(solution)/shard_map/ppermute | solution.py:241
  38.9 0.0 copy-done
  38.9 0.0 copy-done.1
  38.9 0.5 product.1
  39.4 11.3 %all_to_all.17 = f32[16,1,128]{2,1,0:T(1,128)S(1)} all-to-all(f32[16,1,128]{2,1,0:T(1,128)S(1)} %bitcast.19), channel_id=1, replica_groups={{0,1,2,3,4,5,6,7,32,33,34,35,36,37,38,39},{8,9,10,11,12,13,14,15,40,41,..., dimensions={0} | all-to-all | bytes 16384 | tf_op jit(solution)/shard_map/all_to_all | solution.py:257
  50.7 9.3 %all_to_all.18 = f32[16,1,128]{2,1,0:T(1,128)S(1)} all-to-all(f32[16,1,128]{2,1,0:T(1,128)S(1)} %broadcast_in_dim.2), channel_id=1, replica_groups={{0,8,16,24,64,72,80,88,128,136,144,152,192,200,208,216},{1,9,17,25,65,7..., dimensions={0} | all-to-all | bytes 16384 | tf_op jit(solution)/shard_map/all_to_all | solution.py:260
  60.0 0.0 copy-done.2
  60.0 1.0 %final.1 = (f32[128,512]{1,0:T(8,128)}, f32[128,512]{1,0:T(8,128)}, f32[128,512]{1,0:T(8,128)}) custom-call(f32[16,128]{1,0:T(8,128)S(1)} %bitcast.18, f32[128,512]{1,0:T(8,128)S(1)} %bitcast.17, f32[128,512]{1,0:T(8,128)S(1)} %bitcast.16, f32[128,512]{1,0:T(8,128)S(1)} %get-tuple-element.42.d, f32[128,512]{1,0:T(8,128)S(1)} %get-tuple-element.71.product), custom_call_target="tpu_custom_call" | custom-call | tf_op jit(solution)/shard_map/final/pallas_call | solution.py:35
  (8 shorter events, 0.2 us)
Async XLA Ops:
  2.0 14.2 %collective-permute-start.1 = (bf16[128,512]{1,0:T(8,128)(2,1)S(1)}, bf16[128,512]{1,0:T(8,128)(2,1)S(1)}, u32[]{:S(2)}, u32[]{:S(2)}) collective-permute-start(bf16[128,512]{1,0:T(8,128)(2,1)S(1)} %get-tuple-element.39.own), channel_id=1, source_target_pairs={{0,1},{1,0},{2,3},{3,2},{4,5},{5,4},{6,7},{7,6},{8,9},{9,8},{10,11... | collective-permute-start | bytes 393224 | tf_op jit(solution)/shard_map/ppermute | solution.py:241
  4.6 13.5 %collective-permute-start = (bf16[128,512]{1,0:T(8,128)(2,1)S(1)}, bf16[128,512]{1,0:T(8,128)(2,1)S(1)}, u32[]{:S(2)}, u32[]{:S(2)}) collective-permute-start(bf16[128,512]{1,0:T(8,128)(2,1)S(1)} %get-tuple-element.39.own), channel_id=1, source_target_pairs={{0,31},{1,2},{2,1},{3,4},{4,3},{5,6},{6,5},{7,8},{8,7},{9,10},{10,... | collective-permute-start | bytes 393224 | tf_op jit(solution)/shard_map/ppermute | solution.py:241
  11.5 8.1 %collective-permute-start.5 = (bf16[128,512]{1,0:T(8,128)(2,1)S(1)}, bf16[128,512]{1,0:T(8,128)(2,1)S(1)}, u32[]{:S(2)}, u32[]{:S(2)}) collective-permute-start(bf16[128,512]{1,0:T(8,128)(2,1)S(1)} %get-tuple-element.39.own), channel_id=1, source_target_pairs={{0,1},{1,0},{2,3},{3,2},{4,5},{5,4},{6,7},{7,6},{8,9},{9,8},{10,11... | collective-permute-start | bytes 393224 | tf_op jit(solution)/shard_map/ppermute | solution.py:241
  13.9 5.7 %collective-permute-start.6 = (bf16[128,512]{1,0:T(8,128)(2,1)S(1)}, bf16[128,512]{1,0:T(8,128)(2,1)S(1)}, u32[]{:S(2)}, u32[]{:S(2)}) collective-permute-start(bf16[128,512]{1,0:T(8,128)(2,1)S(1)} %get-tuple-element.39.own), channel_id=1, source_target_pairs={{0,32},{1,33},{2,34},{3,35},{4,36},{5,37},{6,38},{7,39},{8,40},{9,... | collective-permute-start | bytes 393224 | tf_op jit(solution)/shard_map/ppermute | solution.py:241
  16.3 5.7 %collective-permute-start.3 = (bf16[128,512]{1,0:T(8,128)(2,1)S(1)}, bf16[128,512]{1,0:T(8,128)(2,1)S(1)}, u32[]{:S(2)}, u32[]{:S(2)}) collective-permute-start(bf16[128,512]{1,0:T(8,128)(2,1)S(1)} %pass_inner.1.after.inner), channel_id=1, source_target_pairs={{0,1},{1,0},{2,3},{3,2},{4,5},{5,4},{6,7},{7,6},{8,9},{9,8},{10,11... | collective-permute-start | bytes 393224 | tf_op jit(solution)/shard_map/ppermute | solution.py:241
  18.1 3.9 %collective-permute-start.4 = (bf16[128,512]{1,0:T(8,128)(2,1)S(1)}, bf16[128,512]{1,0:T(8,128)(2,1)S(1)}, u32[]{:S(2)}, u32[]{:S(2)}) collective-permute-start(bf16[128,512]{1,0:T(8,128)(2,1)S(1)} %pass_inner.1.after.inner), channel_id=1, source_target_pairs={{0,32},{1,33},{2,34},{3,35},{4,36},{5,37},{6,38},{7,39},{8,40},{9,... | collective-permute-start | bytes 393224 | tf_op jit(solution)/shard_map/ppermute | solution.py:241
  18.1 4.8 %collective-permute-start.2 = (bf16[128,512]{1,0:T(8,128)(2,1)S(1)}, bf16[128,512]{1,0:T(8,128)(2,1)S(1)}, u32[]{:S(2)}, u32[]{:S(2)}) collective-permute-start(bf16[128,512]{1,0:T(8,128)(2,1)S(1)} %pass_outer.1.outer), channel_id=1, source_target_pairs={{0,1},{1,0},{2,3},{3,2},{4,5},{5,4},{6,7},{7,6},{8,9},{9,8},{10,11... | collective-permute-start | bytes 393224 | tf_op jit(solution)/shard_map/ppermute | solution.py:241
  19.6 3.3 %collective-permute-start.7 = (bf16[128,512]{1,0:T(8,128)(2,1)S(1)}, bf16[128,512]{1,0:T(8,128)(2,1)S(1)}, u32[]{:S(2)}, u32[]{:S(2)}) collective-permute-start(bf16[128,512]{1,0:T(8,128)(2,1)S(1)} %pass_outer.1.outer), channel_id=1, source_target_pairs={{0,32},{1,33},{2,34},{3,35},{4,36},{5,37},{6,38},{7,39},{8,40},{9,... | collective-permute-start | bytes 393224 | tf_op jit(solution)/shard_map/ppermute | solution.py:241
  24.7 4.8 %collective-permute-start.8 = (bf16[128,512]{1,0:T(8,128)(2,1)S(1)}, bf16[128,512]{1,0:T(8,128)(2,1)S(1)}, u32[]{:S(2)}, u32[]{:S(2)}) collective-permute-start(bf16[128,512]{1,0:T(8,128)(2,1)S(1)} %get-tuple-element.65), channel_id=1, source_target_pairs={{0,1},{1,0},{2,3},{3,2},{4,5},{5,4},{6,7},{7,6},{8,9},{9,8},{10,11... | collective-permute-start | bytes 393224 | tf_op jit(solution)/shard_map/ppermute | solution.py:241
  26.6 2.9 %collective-permute-start.9 = (bf16[384,512]{1,0:T(8,128)(2,1)S(1)}, bf16[384,512]{1,0:T(8,128)(2,1)S(1)}, u32[]{:S(2)}, u32[]{:S(2)}) collective-permute-start(bf16[384,512]{1,0:T(8,128)(2,1)S(1)} %get-tuple-element.66), channel_id=1, source_target_pairs={{0,32},{1,33},{2,34},{3,35},{4,36},{5,37},{6,38},{7,39},{8,40},{9,... | collective-permute-start | bytes 1179656 | tf_op jit(solution)/shard_map/ppermute | solution.py:241
  26.7 6.6 %collective-permute-start.11 = (bf16[128,512]{1,0:T(8,128)(2,1)S(1)}, bf16[128,512]{1,0:T(8,128)(2,1)S(1)}, u32[]{:S(2)}, u32[]{:S(2)}) collective-permute-start(bf16[128,512]{1,0:T(8,128)(2,1)S(1)} %get-tuple-element.67), channel_id=1, source_target_pairs={{0,1},{1,0},{2,3},{3,2},{4,5},{5,4},{6,7},{7,6},{8,9},{9,8},{10,11... | collective-permute-start | bytes 393224 | tf_op jit(solution)/shard_map/ppermute | solution.py:241
  29.6 7.2 %collective-permute-start.10 = (bf16[128,512]{1,0:T(8,128)(2,1)S(1)}, bf16[128,512]{1,0:T(8,128)(2,1)S(1)}, u32[]{:S(2)}, u32[]{:S(2)}) collective-permute-start(bf16[128,512]{1,0:T(8,128)(2,1)S(1)} %merge_outer.1.refs_0_), channel_id=1, source_target_pairs={{0,31},{1,2},{2,1},{3,4},{4,3},{5,6},{6,5},{7,8},{8,7},{9,10},{10,... | collective-permute-start | bytes 393224 | tf_op jit(solution)/shard_map/ppermute | solution.py:241
  32.3 4.7 %collective-permute-start.13 = (bf16[128,512]{1,0:T(8,128)(2,1)S(1)}, bf16[128,512]{1,0:T(8,128)(2,1)S(1)}, u32[]{:S(2)}, u32[]{:S(2)}) collective-permute-start(bf16[128,512]{1,0:T(8,128)(2,1)S(1)} %get-tuple-element.68), channel_id=1, source_target_pairs={{0,1},{1,0},{2,3},{3,2},{4,5},{5,4},{6,7},{7,6},{8,9},{9,8},{10,11... | collective-permute-start | bytes 393224 | tf_op jit(solution)/shard_map/ppermute | solution.py:241
  33.4 5.5 %copy-start = (bf16[512,512]{1,0:T(8,128)(2,1)S(1)}, bf16[512,512]{1,0:T(8,128)(2,1)}, u32[]{:S(2)}) copy-start(bf16[512,512]{1,0:T(8,128)(2,1)} %w_send.1) | copy-start | bytes 1572868
  33.4 5.5 %copy-start.1 = (f32[1,1,128,512]{3,2,1,0:T(8,128)S(1)}, f32[1,1,128,512]{3,2,1,0:T(8,128)}, u32[]{:S(2)}) copy-start(f32[1,1,128,512]{3,2,1,0:T(8,128)} %param.15) | copy-start | bytes 786436
  33.4 5.5 %collective-permute-start.12 = (bf16[128,512]{1,0:T(8,128)(2,1)S(1)}, bf16[128,512]{1,0:T(8,128)(2,1)S(1)}, u32[]{:S(2)}, u32[]{:S(2)}) collective-permute-start(bf16[128,512]{1,0:T(8,128)(2,1)S(1)} %merge_inner.1), channel_id=1, source_target_pairs={{0,1},{1,0},{2,3},{3,2},{4,5},{5,4},{6,7},{7,6},{8,9},{9,8},{10,11... | collective-permute-start | bytes 393224 | tf_op jit(solution)/shard_map/ppermute | solution.py:241
  36.8 23.1 %copy-start.2 = (f32[1,1,128,512]{3,2,1,0:T(8,128)S(1)}, f32[1,1,128,512]{3,2,1,0:T(8,128)}, u32[]{:S(2)}) copy-start(f32[1,1,128,512]{3,2,1,0:T(8,128)} %param.14) | copy-start | bytes 786436

commit v7 on v6

--- a/solution.py
+++ b/solution.py
@@ -250,7 +250,7 @@
         for x in range(4)
     ]
     second = [
-        [(2 * y + c) * n_lon + x * near + z for y in range(n_lat // 2) for x in range(4)]
+        [(2 * y + c) * n_lon + x * near + z for x in range(4) for y in range(n_lat // 2)]
         for c in range(2)
         for z in range(near)
     ]

time: 61.2 us -> 61.2 us (level)
  no operation moved by 1% of the time
where the time goes in v7:
time: 61.2 us; the launch traced here: 61 us
  starting transfers between devices  21.5 us (35%)
  blocking collectives  20.5 us (33%)
  Pallas kernels  12 us (20%)
  waiting for transfers between devices  6.07 us (10%)
  between operations  0.81 us (1%)
    ppermute x14, starting transfers between devices, swapped(): return lax.ppermute(value, ('lat', 'lon'), pairs)  21.5 us
    all_to_all x2, blocking collectives, sums_everywhere(): lax.all_to_all(value, ('lat', 'lon'), 0, 0, tiled=True, axis_index_groups...  20.5 us
    pallas_call x16, Pallas kernels, call(): pl.pallas_call(kernel, out_shape=out_shape, in_specs=[here] * first + [th...  12 us
    ppermute x14, waiting for transfers between devices, swapped(): return lax.ppermute(value, ('lat', 'lon'), pairs)  6.07 us
  transfers between devices with their start and end apart: 14, of which 5 were waited for; matrix products, arithmetic and copies ran while one was open for 0% of the time, Pallas kernels for 12%

profile of v7, /device:TPU:1, one launch (start us, length us, event | category | flops | bytes accessed | tf_op | source)
XLA Modules:
  0.0 61.0 jit_solution(4020500402422110529)
XLA Ops:
  0.6 1.4 %send_term.1 = (bf16[128,512]{1,0:T(8,128)(2,1)S(1)}, s32[1,1024]{1,0:T(1,128)S(1)}, s32[1,1024]{1,0:T(1,128)S(1)}, f32[1,128]{1,0:T(1,128)S(1)}, f32[128,512]{1,0:T(8,128)S(1)}) custom-call(s32[1,1024]{1,0:T(1,128)} %bitcast.23, s32[1,1024]{1,0:T(1,128)} %bitcast.24, f32[1,128]{1,0:T(1,128)} %bitcast.25, f32[128,512]{1,0:T(8,128)} %bitcast.21, ...), custom_call_target="tpu_custom_call" | custom-call | tf_op jit(solution)/shard_map/send_term/pallas_call | solution.py:35
  2.0 2.6 %collective-permute-start.1 = (bf16[128,512]{1,0:T(8,128)(2,1)S(1)}, bf16[128,512]{1,0:T(8,128)(2,1)S(1)}, u32[]{:S(2)}, u32[]{:S(2)}) collective-permute-start(bf16[128,512]{1,0:T(8,128)(2,1)S(1)} %get-tuple-element.39.own), channel_id=1, source_target_pairs={{0,1},{1,0},{2,3},{3,2},{4,5},{5,4},{6,7},{7,6},{8,9},{9,8},{10,11... | collective-permute-start | bytes 393224 | tf_op jit(solution)/shard_map/ppermute | solution.py:241
  4.6 6.9 %collective-permute-start = (bf16[128,512]{1,0:T(8,128)(2,1)S(1)}, bf16[128,512]{1,0:T(8,128)(2,1)S(1)}, u32[]{:S(2)}, u32[]{:S(2)}) collective-permute-start(bf16[128,512]{1,0:T(8,128)(2,1)S(1)} %get-tuple-element.39.own), channel_id=1, source_target_pairs={{0,31},{1,2},{2,1},{3,4},{4,3},{5,6},{6,5},{7,8},{8,7},{9,10},{10,... | collective-permute-start | bytes 393224 | tf_op jit(solution)/shard_map/ppermute | solution.py:241
  11.5 2.4 %collective-permute-start.5 = (bf16[128,512]{1,0:T(8,128)(2,1)S(1)}, bf16[128,512]{1,0:T(8,128)(2,1)S(1)}, u32[]{:S(2)}, u32[]{:S(2)}) collective-permute-start(bf16[128,512]{1,0:T(8,128)(2,1)S(1)} %get-tuple-element.39.own), channel_id=1, source_target_pairs={{0,1},{1,0},{2,3},{3,2},{4,5},{5,4},{6,7},{7,6},{8,9},{9,8},{10,11... | collective-permute-start | bytes 393224 | tf_op jit(solution)/shard_map/ppermute | solution.py:241
  13.9 0.0 collective-permute-start.6
  13.9 2.4 %prepare.1 = (bf16[1024,1280]{1,0:T(8,128)(2,1)S(1)}, bf16[1280,1024]{1,0:T(8,128)(2,1)S(1)}, bf16[1024,512]{1,0:T(8,128)(2,1)S(1)}, bf16[128,512]{1,0:T(8,128)(...) custom-call(s32[1,1024]{1,0:T(1,128)S(1)} %get-tuple-element.40.send, ...), custom_call_target="tpu_custom_call" | custom-call | tf_op jit(solution)/shard_map/prepare/pallas_call | solution.py:35
  16.3 0.0 collective-permute-done.1.block
  16.3 1.8 %collective-permute-start.3 = (bf16[128,512]{1,0:T(8,128)(2,1)S(1)}, bf16[128,512]{1,0:T(8,128)(2,1)S(1)}, u32[]{:S(2)}, u32[]{:S(2)}) collective-permute-start(bf16[128,512]{1,0:T(8,128)(2,1)S(1)} %pass_inner.1.after.inner), channel_id=1, source_target_pairs={{0,1},{1,0},{2,3},{3,2},{4,5},{5,4},{6,7},{7,6},{8,9},{9,8},{10,11... | collective-permute-start | bytes 393224 | tf_op jit(solution)/shard_map/ppermute | solution.py:241
  18.1 0.0 collective-permute-start.4
  18.1 0.0 collective-permute-done.block
  18.1 1.5 %collective-permute-start.2 = (bf16[128,512]{1,0:T(8,128)(2,1)S(1)}, bf16[128,512]{1,0:T(8,128)(2,1)S(1)}, u32[]{:S(2)}, u32[]{:S(2)}) collective-permute-start(bf16[128,512]{1,0:T(8,128)(2,1)S(1)} %pass_outer.1.outer), channel_id=1, source_target_pairs={{0,1},{1,0},{2,3},{3,2},{4,5},{5,4},{6,7},{7,6},{8,9},{9,8},{10,11... | collective-permute-start | bytes 393224 | tf_op jit(solution)/shard_map/ppermute | solution.py:241
  19.6 0.0 collective-permute-done.5.far
  19.6 0.0 collective-permute-start.7
  19.6 0.0 collective-permute-done.6.near
  19.6 2.4 %base.1 = (f32[1024,512]{1,0:T(8,128)S(1)}, f32[1024,512]{1,0:T(8,128)S(1)}, f32[128,512]{1,0:T(8,128)S(1)}, f32[128,512]{1,0:T(8,128)S(1)}, f32[128,512]{1,0:T(...) custom-call(bf16[128,512]{1,0:T(8,128)(2,1)S(1)} %collective-permute-done.5.far, ...), custom_call_target="tpu_custom_call" | custom-call | flops 1000000000 | bytes 10000000 | tf_op jit(solution)/shard_map/base/pallas_call | solution.py:35
  22.0 0.0 collective-permute-done.3.far_inner
  22.0 0.0 collective-permute-done.4.near_inner
  22.0 0.4 inner.1.after.base
  22.4 0.4 collective-permute-done.2.block
  22.9 0.0 collective-permute-done.7.near_outer
  22.9 1.8 %main.1 = (bf16[128,512]{1,0:T(8,128)(2,1)S(1)}, bf16[1024,512]{1,0:T(8,128)(2,1)S(1)}, bf16[128,512]{1,0:T(8,128)(2,1)S(1)}, bf16[128,512]{1,0:T(8,128)(2,1)S(1)}) custom-call(bf16[128,512]{1,0:T(8,128)(2,1)S(1)} %gate.2.far_outer, bf16[128,512]{1,0:T(8,128)(2,1)S(1)} %collective-permute-done.7.near_outer, f32[1024,512]{1,0:T(8,128)S(1)} %inner.1.after.base, ...), custom_call_target="tpu_custom_call" | custom-call | tf_op jit(solution)/shard_map/main/pallas_call | solution.py:35
  24.7 1.2 %collective-permute-start.8 = (bf16[128,512]{1,0:T(8,128)(2,1)S(1)}, bf16[128,512]{1,0:T(8,128)(2,1)S(1)}, u32[]{:S(2)}, u32[]{:S(2)}) collective-permute-start(bf16[128,512]{1,0:T(8,128)(2,1)S(1)} %get-tuple-element.65), channel_id=1, source_target_pairs={{0,1},{1,0},{2,3},{3,2},{4,5},{5,4},{6,7},{7,6},{8,9},{9,8},{10,11... | collective-permute-start | bytes 393224 | tf_op jit(solution)/shard_map/ppermute | solution.py:241
  25.9 0.7 %corner.1 = (bf16[128,512]{1,0:T(8,128)(2,1)S(1)}, bf16[384,512]{1,0:T(8,128)(2,1)S(1)}) custom-call(bf16[1024,512]{1,0:T(8,128)(2,1)S(1)} %get-tuple-element.60.edge_grad, bf16[1280,1024]{1,0:T(8,128)(2,1)S(1)} %get-tuple-element.53.pick_t), custom_call_target="tpu_custom_call" | custom-call | tf_op jit(solution)/shard_map/corner/pallas_call | solution.py:35
  26.6 0.1 collective-permute-start.9
  26.7 1.3 %collective-permute-start.11 = (bf16[128,512]{1,0:T(8,128)(2,1)S(1)}, bf16[128,512]{1,0:T(8,128)(2,1)S(1)}, u32[]{:S(2)}, u32[]{:S(2)}) collective-permute-start(bf16[128,512]{1,0:T(8,128)(2,1)S(1)} %get-tuple-element.67), channel_id=1, source_target_pairs={{0,1},{1,0},{2,3},{3,2},{4,5},{5,4},{6,7},{7,6},{8,9},{9,8},{10,11... | collective-permute-start | bytes 393224 | tf_op jit(solution)/shard_map/ppermute | solution.py:241
  28.0 1.2 %rest.1 = (bf16[128,512]{1,0:T(8,128)(2,1)S(1)}, f32[384,512]{1,0:T(8,128)S(1)}, f32[128,512]{1,0:T(8,128)S(1)}) custom-call(bf16[1024,512]{1,0:T(8,128)(2,1)S(1)} %get-tuple-element.60.edge_grad, bf16[1280,1024]{1,0:T(8,128)(2,1)S(1)} %get-tuple-element.53.pick_t, bf16[128,512]{1,0:T(8,128)(2,1)S(1)} %get-tuple-element.61.node_grad, ...), custom_call_target="tpu_custom_call" | custom-call | flops 10000000 | bytes 100000 | tf_op jit(solution)/shard_map/rest/pallas_call | solution.py:35
  29.3 0.2 collective-permute-done.8.block
  29.5 0.0 collective-permute-done.9.from_near
  29.6 2.7 %collective-permute-start.10 = (bf16[128,512]{1,0:T(8,128)(2,1)S(1)}, bf16[128,512]{1,0:T(8,128)(2,1)S(1)}, u32[]{:S(2)}, u32[]{:S(2)}) collective-permute-start(bf16[128,512]{1,0:T(8,128)(2,1)S(1)} %merge_outer.1.refs_0_), channel_id=1, source_target_pairs={{0,31},{1,2},{2,1},{3,4},{4,3},{5,6},{6,5},{7,8},{8,7},{9,10},{10,... | collective-permute-start | bytes 393224 | tf_op jit(solution)/shard_map/ppermute | solution.py:241
  32.3 1.1 %collective-permute-start.13 = (bf16[128,512]{1,0:T(8,128)(2,1)S(1)}, bf16[128,512]{1,0:T(8,128)(2,1)S(1)}, u32[]{:S(2)}, u32[]{:S(2)}) collective-permute-start(bf16[128,512]{1,0:T(8,128)(2,1)S(1)} %get-tuple-element.68), channel_id=1, source_target_pairs={{0,1},{1,0},{2,3},{3,2},{4,5},{5,4},{6,7},{7,6},{8,9},{9,8},{10,11... | collective-permute-start | bytes 393224 | tf_op jit(solution)/shard_map/ppermute | solution.py:241
  33.3 0.0 collective-permute-done.11.from_far
  33.3 0.1 merge_inner.1
  33.4 0.0 copy-start
  33.4 0.0 copy-start.1
  33.4 0.1 collective-permute-start.12
  33.5 3.3 %collective-permute-done.10.from_outer = bf16[128,512]{1,0:T(8,128)(2,1)S(1)} collective-permute-done((bf16[128,512]{1,0:T(8,128)(2,1)S(1)}, bf16[128,512]{1,0:T(8,128)(2,1)S(1)}, u32[]{:S(2)}, u32[]{:S(2)}) %collective-permute-start.10) | collective-permute-done | bytes 131104 | tf_op jit(solution)/shard_map/ppermute | solution.py:241
  36.8 0.0 copy-start.2
  36.9 0.1 collective-permute-done.13.from_far
  36.9 2.0 %collective-permute-done.12.from_inner = bf16[128,512]{1,0:T(8,128)(2,1)S(1)} collective-permute-done((bf16[128,512]{1,0:T(8,128)(2,1)S(1)}, bf16[128,512]{1,0:T(8,128)(2,1)S(1)}, u32[]{:S(2)}, u32[]{:S(2)}) %collective-permute-start.12) | collective-permute-done | bytes 131104 | tf_op jit(solution)/shard_map/ppermute | solution.py:241
  38.9 0.0 copy-done
  38.9 0.0 copy-done.1
  38.9 0.5 product.1
  39.4 11.3 %all_to_all.17 = f32[16,1,128]{2,1,0:T(1,128)S(1)} all-to-all(f32[16,1,128]{2,1,0:T(1,128)S(1)} %bitcast.19), channel_id=1, replica_groups={{0,1,2,3,4,5,6,7,32,33,34,35,36,37,38,39},{8,9,10,11,12,13,14,15,40,41,..., dimensions={0} | all-to-all | bytes 16384 | tf_op jit(solution)/shard_map/all_to_all | solution.py:257
  50.7 9.3 %all_to_all.18 = f32[16,1,128]{2,1,0:T(1,128)S(1)} all-to-all(f32[16,1,128]{2,1,0:T(1,128)S(1)} %broadcast_in_dim.2), channel_id=1, replica_groups={{0,64,128,192,8,72,136,200,16,80,144,208,24,88,152,216},{1,65,129,193,9..., dimensions={0} | all-to-all | bytes 16384 | tf_op jit(solution)/shard_map/all_to_all | solution.py:260
  60.0 0.0 copy-done.2
  60.0 1.0 %final.1 = (f32[128,512]{1,0:T(8,128)}, f32[128,512]{1,0:T(8,128)}, f32[128,512]{1,0:T(8,128)}) custom-call(f32[16,128]{1,0:T(8,128)S(1)} %bitcast.18, f32[128,512]{1,0:T(8,128)S(1)} %bitcast.17, f32[128,512]{1,0:T(8,128)S(1)} %bitcast.16, f32[128,512]{1,0:T(8,128)S(1)} %get-tuple-element.42.d, f32[128,512]{1,0:T(8,128)S(1)} %get-tuple-element.71.product), custom_call_target="tpu_custom_call" | custom-call | tf_op jit(solution)/shard_map/final/pallas_call | solution.py:35
  (8 shorter events, 0.2 us)
Async XLA Ops:
  2.0 14.2 %collective-permute-start.1 = (bf16[128,512]{1,0:T(8,128)(2,1)S(1)}, bf16[128,512]{1,0:T(8,128)(2,1)S(1)}, u32[]{:S(2)}, u32[]{:S(2)}) collective-permute-start(bf16[128,512]{1,0:T(8,128)(2,1)S(1)} %get-tuple-element.39.own), channel_id=1, source_target_pairs={{0,1},{1,0},{2,3},{3,2},{4,5},{5,4},{6,7},{7,6},{8,9},{9,8},{10,11... | collective-permute-start | bytes 393224 | tf_op jit(solution)/shard_map/ppermute | solution.py:241
  4.6 13.5 %collective-permute-start = (bf16[128,512]{1,0:T(8,128)(2,1)S(1)}, bf16[128,512]{1,0:T(8,128)(2,1)S(1)}, u32[]{:S(2)}, u32[]{:S(2)}) collective-permute-start(bf16[128,512]{1,0:T(8,128)(2,1)S(1)} %get-tuple-element.39.own), channel_id=1, source_target_pairs={{0,31},{1,2},{2,1},{3,4},{4,3},{5,6},{6,5},{7,8},{8,7},{9,10},{10,... | collective-permute-start | bytes 393224 | tf_op jit(solution)/shard_map/ppermute | solution.py:241
  11.5 8.1 %collective-permute-start.5 = (bf16[128,512]{1,0:T(8,128)(2,1)S(1)}, bf16[128,512]{1,0:T(8,128)(2,1)S(1)}, u32[]{:S(2)}, u32[]{:S(2)}) collective-permute-start(bf16[128,512]{1,0:T(8,128)(2,1)S(1)} %get-tuple-element.39.own), channel_id=1, source_target_pairs={{0,1},{1,0},{2,3},{3,2},{4,5},{5,4},{6,7},{7,6},{8,9},{9,8},{10,11... | collective-permute-start | bytes 393224 | tf_op jit(solution)/shard_map/ppermute | solution.py:241
  13.9 5.7 %collective-permute-start.6 = (bf16[128,512]{1,0:T(8,128)(2,1)S(1)}, bf16[128,512]{1,0:T(8,128)(2,1)S(1)}, u32[]{:S(2)}, u32[]{:S(2)}) collective-permute-start(bf16[128,512]{1,0:T(8,128)(2,1)S(1)} %get-tuple-element.39.own), channel_id=1, source_target_pairs={{0,32},{1,33},{2,34},{3,35},{4,36},{5,37},{6,38},{7,39},{8,40},{9,... | collective-permute-start | bytes 393224 | tf_op jit(solution)/shard_map/ppermute | solution.py:241
  16.3 5.7 %collective-permute-start.3 = (bf16[128,512]{1,0:T(8,128)(2,1)S(1)}, bf16[128,512]{1,0:T(8,128)(2,1)S(1)}, u32[]{:S(2)}, u32[]{:S(2)}) collective-permute-start(bf16[128,512]{1,0:T(8,128)(2,1)S(1)} %pass_inner.1.after.inner), channel_id=1, source_target_pairs={{0,1},{1,0},{2,3},{3,2},{4,5},{5,4},{6,7},{7,6},{8,9},{9,8},{10,11... | collective-permute-start | bytes 393224 | tf_op jit(solution)/shard_map/ppermute | solution.py:241
  18.1 3.9 %collective-permute-start.4 = (bf16[128,512]{1,0:T(8,128)(2,1)S(1)}, bf16[128,512]{1,0:T(8,128)(2,1)S(1)}, u32[]{:S(2)}, u32[]{:S(2)}) collective-permute-start(bf16[128,512]{1,0:T(8,128)(2,1)S(1)} %pass_inner.1.after.inner), channel_id=1, source_target_pairs={{0,32},{1,33},{2,34},{3,35},{4,36},{5,37},{6,38},{7,39},{8,40},{9,... | collective-permute-start | bytes 393224 | tf_op jit(solution)/shard_map/ppermute | solution.py:241
  18.1 4.8 %collective-permute-start.2 = (bf16[128,512]{1,0:T(8,128)(2,1)S(1)}, bf16[128,512]{1,0:T(8,128)(2,1)S(1)}, u32[]{:S(2)}, u32[]{:S(2)}) collective-permute-start(bf16[128,512]{1,0:T(8,128)(2,1)S(1)} %pass_outer.1.outer), channel_id=1, source_target_pairs={{0,1},{1,0},{2,3},{3,2},{4,5},{5,4},{6,7},{7,6},{8,9},{9,8},{10,11... | collective-permute-start | bytes 393224 | tf_op jit(solution)/shard_map/ppermute | solution.py:241
  19.6 3.3 %collective-permute-start.7 = (bf16[128,512]{1,0:T(8,128)(2,1)S(1)}, bf16[128,512]{1,0:T(8,128)(2,1)S(1)}, u32[]{:S(2)}, u32[]{:S(2)}) collective-permute-start(bf16[128,512]{1,0:T(8,128)(2,1)S(1)} %pass_outer.1.outer), channel_id=1, source_target_pairs={{0,32},{1,33},{2,34},{3,35},{4,36},{5,37},{6,38},{7,39},{8,40},{9,... | collective-permute-start | bytes 393224 | tf_op jit(solution)/shard_map/ppermute | solution.py:241
  24.7 4.8 %collective-permute-start.8 = (bf16[128,512]{1,0:T(8,128)(2,1)S(1)}, bf16[128,512]{1,0:T(8,128)(2,1)S(1)}, u32[]{:S(2)}, u32[]{:S(2)}) collective-permute-start(bf16[128,512]{1,0:T(8,128)(2,1)S(1)} %get-tuple-element.65), channel_id=1, source_target_pairs={{0,1},{1,0},{2,3},{3,2},{4,5},{5,4},{6,7},{7,6},{8,9},{9,8},{10,11... | collective-permute-start | bytes 393224 | tf_op jit(solution)/shard_map/ppermute | solution.py:241
  26.6 2.9 %collective-permute-start.9 = (bf16[384,512]{1,0:T(8,128)(2,1)S(1)}, bf16[384,512]{1,0:T(8,128)(2,1)S(1)}, u32[]{:S(2)}, u32[]{:S(2)}) collective-permute-start(bf16[384,512]{1,0:T(8,128)(2,1)S(1)} %get-tuple-element.66), channel_id=1, source_target_pairs={{0,32},{1,33},{2,34},{3,35},{4,36},{5,37},{6,38},{7,39},{8,40},{9,... | collective-permute-start | bytes 1179656 | tf_op jit(solution)/shard_map/ppermute | solution.py:241
  26.7 6.6 %collective-permute-start.11 = (bf16[128,512]{1,0:T(8,128)(2,1)S(1)}, bf16[128,512]{1,0:T(8,128)(2,1)S(1)}, u32[]{:S(2)}, u32[]{:S(2)}) collective-permute-start(bf16[128,512]{1,0:T(8,128)(2,1)S(1)} %get-tuple-element.67), channel_id=1, source_target_pairs={{0,1},{1,0},{2,3},{3,2},{4,5},{5,4},{6,7},{7,6},{8,9},{9,8},{10,11... | collective-permute-start | bytes 393224 | tf_op jit(solution)/shard_map/ppermute | solution.py:241
  29.6 7.2 %collective-permute-start.10 = (bf16[128,512]{1,0:T(8,128)(2,1)S(1)}, bf16[128,512]{1,0:T(8,128)(2,1)S(1)}, u32[]{:S(2)}, u32[]{:S(2)}) collective-permute-start(bf16[128,512]{1,0:T(8,128)(2,1)S(1)} %merge_outer.1.refs_0_), channel_id=1, source_target_pairs={{0,31},{1,2},{2,1},{3,4},{4,3},{5,6},{6,5},{7,8},{8,7},{9,10},{10,... | collective-permute-start | bytes 393224 | tf_op jit(solution)/shard_map/ppermute | solution.py:241
  32.3 4.7 %collective-permute-start.13 = (bf16[128,512]{1,0:T(8,128)(2,1)S(1)}, bf16[128,512]{1,0:T(8,128)(2,1)S(1)}, u32[]{:S(2)}, u32[]{:S(2)}) collective-permute-start(bf16[128,512]{1,0:T(8,128)(2,1)S(1)} %get-tuple-element.68), channel_id=1, source_target_pairs={{0,1},{1,0},{2,3},{3,2},{4,5},{5,4},{6,7},{7,6},{8,9},{9,8},{10,11... | collective-permute-start | bytes 393224 | tf_op jit(solution)/shard_map/ppermute | solution.py:241
  33.4 5.5 %copy-start = (bf16[512,512]{1,0:T(8,128)(2,1)S(1)}, bf16[512,512]{1,0:T(8,128)(2,1)}, u32[]{:S(2)}) copy-start(bf16[512,512]{1,0:T(8,128)(2,1)} %w_send.1) | copy-start | bytes 1572868
  33.4 5.5 %copy-start.1 = (f32[1,1,128,512]{3,2,1,0:T(8,128)S(1)}, f32[1,1,128,512]{3,2,1,0:T(8,128)}, u32[]{:S(2)}) copy-start(f32[1,1,128,512]{3,2,1,0:T(8,128)} %param.15) | copy-start | bytes 786436
  33.4 5.5 %collective-permute-start.12 = (bf16[128,512]{1,0:T(8,128)(2,1)S(1)}, bf16[128,512]{1,0:T(8,128)(2,1)S(1)}, u32[]{:S(2)}, u32[]{:S(2)}) collective-permute-start(bf16[128,512]{1,0:T(8,128)(2,1)S(1)} %merge_inner.1), channel_id=1, source_target_pairs={{0,1},{1,0},{2,3},{3,2},{4,5},{5,4},{6,7},{7,6},{8,9},{9,8},{10,11... | collective-permute-start | bytes 393224 | tf_op jit(solution)/shard_map/ppermute | solution.py:241
  36.8 23.1 %copy-start.2 = (f32[1,1,128,512]{3,2,1,0:T(8,128)S(1)}, f32[1,1,128,512]{3,2,1,0:T(8,128)}, u32[]{:S(2)}) copy-start(f32[1,1,128,512]{3,2,1,0:T(8,128)} %param.14) | copy-start | bytes 786436

commit v8 on v6

--- a/solution.py
+++ b/solution.py
@@ -202,11 +202,15 @@
     prod = partial[...] + dot_back(total.astype(BF), w_send[...])
     product[...] = prod
     res = r[...]
-    lane = lax.broadcasted_iota(jnp.int32, sums.shape, 1)
-    out = jnp.zeros(sums.shape, F32)
+    row = lax.broadcasted_iota(jnp.int32, (8, 128), 0)
+    lane = lax.broadcasted_iota(jnp.int32, (8, 128), 1)
+    folds = jnp.zeros((8, 128), F32)
     for k, value in enumerate((res * res, d[...] * prod, res * prod, prod * prod)):
-        out = jnp.where(lane == k, jnp.sum(value), out)
-    sums[...] = out
+        fold = jnp.sum(value, axis=0, keepdims=True)
+        fold = fold[:, 0:128] + fold[:, 128:256] + fold[:, 256:384] + fold[:, 384:512]
+        folds = jnp.where(row == k, fold, folds)
+    spread = jnp.where(row == lane, jnp.sum(folds, axis=1, keepdims=True), 0.0)
+    sums[...] = jnp.broadcast_to(jnp.sum(spread, axis=0, keepdims=True), sums.shape)
 
 
 def final_kernel(sums, x, r, d, product, new_x, new_r, new_d):

time: 61.2 us -> 61.2 us (level)
  no operation moved by 1% of the time
where the time goes in v8:
time: 61.2 us; the launch traced here: 61 us
  starting transfers between devices  21.5 us (35%)
  blocking collectives  20.5 us (33%)
  Pallas kernels  12 us (20%)
  waiting for transfers between devices  6.07 us (10%)
  between operations  0.8 us (1%)
    ppermute x14, starting transfers between devices, swapped(): return lax.ppermute(value, ('lat', 'lon'), pairs)  21.5 us
    all_to_all x2, blocking collectives, sums_everywhere(): lax.all_to_all(value, ('lat', 'lon'), 0, 0, tiled=True, axis_index_groups...  20.5 us
    pallas_call x16, Pallas kernels, call(): pl.pallas_call(kernel, out_shape=out_shape, in_specs=[here] * first + [th...  12 us
    ppermute x14, waiting for transfers between devices, swapped(): return lax.ppermute(value, ('lat', 'lon'), pairs)  6.07 us
  transfers between devices with their start and end apart: 14, of which 5 were waited for; matrix products, arithmetic and copies ran while one was open for 0% of the time, Pallas kernels for 12%

profile of v8, /device:TPU:1, one launch (start us, length us, event | category | flops | bytes accessed | tf_op | source)
XLA Modules:
  0.0 61.0 jit_solution(3816984780979899788)
XLA Ops:
  0.6 1.4 %send_term.1 = (bf16[128,512]{1,0:T(8,128)(2,1)S(1)}, s32[1,1024]{1,0:T(1,128)S(1)}, s32[1,1024]{1,0:T(1,128)S(1)}, f32[1,128]{1,0:T(1,128)S(1)}, f32[128,512]{1,0:T(8,128)S(1)}) custom-call(s32[1,1024]{1,0:T(1,128)} %bitcast.23, s32[1,1024]{1,0:T(1,128)} %bitcast.24, f32[1,128]{1,0:T(1,128)} %bitcast.25, f32[128,512]{1,0:T(8,128)} %bitcast.21, ...), custom_call_target="tpu_custom_call" | custom-call | tf_op jit(solution)/shard_map/send_term/pallas_call | solution.py:35
  2.0 2.6 %collective-permute-start.1 = (bf16[128,512]{1,0:T(8,128)(2,1)S(1)}, bf16[128,512]{1,0:T(8,128)(2,1)S(1)}, u32[]{:S(2)}, u32[]{:S(2)}) collective-permute-start(bf16[128,512]{1,0:T(8,128)(2,1)S(1)} %get-tuple-element.39.own), channel_id=1, source_target_pairs={{0,1},{1,0},{2,3},{3,2},{4,5},{5,4},{6,7},{7,6},{8,9},{9,8},{10,11... | collective-permute-start | bytes 393224 | tf_op jit(solution)/shard_map/ppermute | solution.py:245
  4.6 6.9 %collective-permute-start = (bf16[128,512]{1,0:T(8,128)(2,1)S(1)}, bf16[128,512]{1,0:T(8,128)(2,1)S(1)}, u32[]{:S(2)}, u32[]{:S(2)}) collective-permute-start(bf16[128,512]{1,0:T(8,128)(2,1)S(1)} %get-tuple-element.39.own), channel_id=1, source_target_pairs={{0,31},{1,2},{2,1},{3,4},{4,3},{5,6},{6,5},{7,8},{8,7},{9,10},{10,... | collective-permute-start | bytes 393224 | tf_op jit(solution)/shard_map/ppermute | solution.py:245
  11.5 2.4 %collective-permute-start.5 = (bf16[128,512]{1,0:T(8,128)(2,1)S(1)}, bf16[128,512]{1,0:T(8,128)(2,1)S(1)}, u32[]{:S(2)}, u32[]{:S(2)}) collective-permute-start(bf16[128,512]{1,0:T(8,128)(2,1)S(1)} %get-tuple-element.39.own), channel_id=1, source_target_pairs={{0,1},{1,0},{2,3},{3,2},{4,5},{5,4},{6,7},{7,6},{8,9},{9,8},{10,11... | collective-permute-start | bytes 393224 | tf_op jit(solution)/shard_map/ppermute | solution.py:245
  13.9 0.0 collective-permute-start.6
  13.9 2.4 %prepare.1 = (bf16[1024,1280]{1,0:T(8,128)(2,1)S(1)}, bf16[1280,1024]{1,0:T(8,128)(2,1)S(1)}, bf16[1024,512]{1,0:T(8,128)(2,1)S(1)}, bf16[128,512]{1,0:T(8,128)(...) custom-call(s32[1,1024]{1,0:T(1,128)S(1)} %get-tuple-element.40.send, ...), custom_call_target="tpu_custom_call" | custom-call | tf_op jit(solution)/shard_map/prepare/pallas_call | solution.py:35
  16.3 0.0 collective-permute-done.1.block
  16.3 1.8 %collective-permute-start.3 = (bf16[128,512]{1,0:T(8,128)(2,1)S(1)}, bf16[128,512]{1,0:T(8,128)(2,1)S(1)}, u32[]{:S(2)}, u32[]{:S(2)}) collective-permute-start(bf16[128,512]{1,0:T(8,128)(2,1)S(1)} %pass_inner.1.after.inner), channel_id=1, source_target_pairs={{0,1},{1,0},{2,3},{3,2},{4,5},{5,4},{6,7},{7,6},{8,9},{9,8},{10,11... | collective-permute-start | bytes 393224 | tf_op jit(solution)/shard_map/ppermute | solution.py:245
  18.1 0.0 collective-permute-start.4
  18.1 0.0 collective-permute-done.block
  18.1 1.5 %collective-permute-start.2 = (bf16[128,512]{1,0:T(8,128)(2,1)S(1)}, bf16[128,512]{1,0:T(8,128)(2,1)S(1)}, u32[]{:S(2)}, u32[]{:S(2)}) collective-permute-start(bf16[128,512]{1,0:T(8,128)(2,1)S(1)} %pass_outer.1.outer), channel_id=1, source_target_pairs={{0,1},{1,0},{2,3},{3,2},{4,5},{5,4},{6,7},{7,6},{8,9},{9,8},{10,11... | collective-permute-start | bytes 393224 | tf_op jit(solution)/shard_map/ppermute | solution.py:245
  19.6 0.0 collective-permute-done.5.far
  19.6 0.0 collective-permute-start.7
  19.6 0.0 collective-permute-done.6.near
  19.6 2.4 %base.1 = (f32[1024,512]{1,0:T(8,128)S(1)}, f32[1024,512]{1,0:T(8,128)S(1)}, f32[128,512]{1,0:T(8,128)S(1)}, f32[128,512]{1,0:T(8,128)S(1)}, f32[128,512]{1,0:T(...) custom-call(bf16[128,512]{1,0:T(8,128)(2,1)S(1)} %collective-permute-done.5.far, ...), custom_call_target="tpu_custom_call" | custom-call | flops 1000000000 | bytes 10000000 | tf_op jit(solution)/shard_map/base/pallas_call | solution.py:35
  22.0 0.0 collective-permute-done.3.far_inner
  22.0 0.0 collective-permute-done.4.near_inner
  22.0 0.4 inner.1.after.base
  22.4 0.4 collective-permute-done.2.block
  22.9 0.0 collective-permute-done.7.near_outer
  22.9 1.8 %main.1 = (bf16[128,512]{1,0:T(8,128)(2,1)S(1)}, bf16[1024,512]{1,0:T(8,128)(2,1)S(1)}, bf16[128,512]{1,0:T(8,128)(2,1)S(1)}, bf16[128,512]{1,0:T(8,128)(2,1)S(1)}) custom-call(bf16[128,512]{1,0:T(8,128)(2,1)S(1)} %gate.2.far_outer, bf16[128,512]{1,0:T(8,128)(2,1)S(1)} %collective-permute-done.7.near_outer, f32[1024,512]{1,0:T(8,128)S(1)} %inner.1.after.base, ...), custom_call_target="tpu_custom_call" | custom-call | tf_op jit(solution)/shard_map/main/pallas_call | solution.py:35
  24.7 1.2 %collective-permute-start.8 = (bf16[128,512]{1,0:T(8,128)(2,1)S(1)}, bf16[128,512]{1,0:T(8,128)(2,1)S(1)}, u32[]{:S(2)}, u32[]{:S(2)}) collective-permute-start(bf16[128,512]{1,0:T(8,128)(2,1)S(1)} %get-tuple-element.65), channel_id=1, source_target_pairs={{0,1},{1,0},{2,3},{3,2},{4,5},{5,4},{6,7},{7,6},{8,9},{9,8},{10,11... | collective-permute-start | bytes 393224 | tf_op jit(solution)/shard_map/ppermute | solution.py:245
  25.9 0.7 %corner.1 = (bf16[128,512]{1,0:T(8,128)(2,1)S(1)}, bf16[384,512]{1,0:T(8,128)(2,1)S(1)}) custom-call(bf16[1024,512]{1,0:T(8,128)(2,1)S(1)} %get-tuple-element.60.edge_grad, bf16[1280,1024]{1,0:T(8,128)(2,1)S(1)} %get-tuple-element.53.pick_t), custom_call_target="tpu_custom_call" | custom-call | tf_op jit(solution)/shard_map/corner/pallas_call | solution.py:35
  26.6 0.1 collective-permute-start.9
  26.7 1.3 %collective-permute-start.11 = (bf16[128,512]{1,0:T(8,128)(2,1)S(1)}, bf16[128,512]{1,0:T(8,128)(2,1)S(1)}, u32[]{:S(2)}, u32[]{:S(2)}) collective-permute-start(bf16[128,512]{1,0:T(8,128)(2,1)S(1)} %get-tuple-element.67), channel_id=1, source_target_pairs={{0,1},{1,0},{2,3},{3,2},{4,5},{5,4},{6,7},{7,6},{8,9},{9,8},{10,11... | collective-permute-start | bytes 393224 | tf_op jit(solution)/shard_map/ppermute | solution.py:245
  28.0 1.2 %rest.1 = (bf16[128,512]{1,0:T(8,128)(2,1)S(1)}, f32[384,512]{1,0:T(8,128)S(1)}, f32[128,512]{1,0:T(8,128)S(1)}) custom-call(bf16[1024,512]{1,0:T(8,128)(2,1)S(1)} %get-tuple-element.60.edge_grad, bf16[1280,1024]{1,0:T(8,128)(2,1)S(1)} %get-tuple-element.53.pick_t, bf16[128,512]{1,0:T(8,128)(2,1)S(1)} %get-tuple-element.61.node_grad, ...), custom_call_target="tpu_custom_call" | custom-call | flops 10000000 | bytes 100000 | tf_op jit(solution)/shard_map/rest/pallas_call | solution.py:35
  29.3 0.2 collective-permute-done.8.block
  29.5 0.0 collective-permute-done.9.from_near
  29.6 2.7 %collective-permute-start.10 = (bf16[128,512]{1,0:T(8,128)(2,1)S(1)}, bf16[128,512]{1,0:T(8,128)(2,1)S(1)}, u32[]{:S(2)}, u32[]{:S(2)}) collective-permute-start(bf16[128,512]{1,0:T(8,128)(2,1)S(1)} %merge_outer.1.refs_0_), channel_id=1, source_target_pairs={{0,31},{1,2},{2,1},{3,4},{4,3},{5,6},{6,5},{7,8},{8,7},{9,10},{10,... | collective-permute-start | bytes 393224 | tf_op jit(solution)/shard_map/ppermute | solution.py:245
  32.3 1.1 %collective-permute-start.13 = (bf16[128,512]{1,0:T(8,128)(2,1)S(1)}, bf16[128,512]{1,0:T(8,128)(2,1)S(1)}, u32[]{:S(2)}, u32[]{:S(2)}) collective-permute-start(bf16[128,512]{1,0:T(8,128)(2,1)S(1)} %get-tuple-element.68), channel_id=1, source_target_pairs={{0,1},{1,0},{2,3},{3,2},{4,5},{5,4},{6,7},{7,6},{8,9},{9,8},{10,11... | collective-permute-start | bytes 393224 | tf_op jit(solution)/shard_map/ppermute | solution.py:245
  33.3 0.0 collective-permute-done.11.from_far
  33.3 0.1 merge_inner.1
  33.4 0.0 copy-start
  33.4 0.0 copy-start.1
  33.4 0.1 collective-permute-start.12
  33.5 3.3 %collective-permute-done.10.from_outer = bf16[128,512]{1,0:T(8,128)(2,1)S(1)} collective-permute-done((bf16[128,512]{1,0:T(8,128)(2,1)S(1)}, bf16[128,512]{1,0:T(8,128)(2,1)S(1)}, u32[]{:S(2)}, u32[]{:S(2)}) %collective-permute-start.10) | collective-permute-done | bytes 131104 | tf_op jit(solution)/shard_map/ppermute | solution.py:245
  36.8 0.0 copy-start.2
  36.9 0.1 collective-permute-done.13.from_far
  36.9 2.0 %collective-permute-done.12.from_inner = bf16[128,512]{1,0:T(8,128)(2,1)S(1)} collective-permute-done((bf16[128,512]{1,0:T(8,128)(2,1)S(1)}, bf16[128,512]{1,0:T(8,128)(2,1)S(1)}, u32[]{:S(2)}, u32[]{:S(2)}) %collective-permute-start.12) | collective-permute-done | bytes 131104 | tf_op jit(solution)/shard_map/ppermute | solution.py:245
  38.9 0.0 copy-done
  38.9 0.0 copy-done.1
  38.9 0.4 product.1
  39.4 11.3 %all_to_all.17 = f32[16,1,128]{2,1,0:T(1,128)S(1)} all-to-all(f32[16,1,128]{2,1,0:T(1,128)S(1)} %bitcast.19), channel_id=1, replica_groups={{0,1,2,3,4,5,6,7,32,33,34,35,36,37,38,39},{8,9,10,11,12,13,14,15,40,41,..., dimensions={0} | all-to-all | bytes 16384 | tf_op jit(solution)/shard_map/all_to_all | solution.py:261
  50.7 9.3 %all_to_all.18 = f32[16,1,128]{2,1,0:T(1,128)S(1)} all-to-all(f32[16,1,128]{2,1,0:T(1,128)S(1)} %broadcast_in_dim.2), channel_id=1, replica_groups={{0,8,16,24,64,72,80,88,128,136,144,152,192,200,208,216},{1,9,17,25,65,7..., dimensions={0} | all-to-all | bytes 16384 | tf_op jit(solution)/shard_map/all_to_all | solution.py:264
  59.9 0.0 copy-done.2
  59.9 1.0 %final.1 = (f32[128,512]{1,0:T(8,128)}, f32[128,512]{1,0:T(8,128)}, f32[128,512]{1,0:T(8,128)}) custom-call(f32[16,128]{1,0:T(8,128)S(1)} %bitcast.18, f32[128,512]{1,0:T(8,128)S(1)} %bitcast.17, f32[128,512]{1,0:T(8,128)S(1)} %bitcast.16, f32[128,512]{1,0:T(8,128)S(1)} %get-tuple-element.42.d, f32[128,512]{1,0:T(8,128)S(1)} %get-tuple-element.71.product), custom_call_target="tpu_custom_call" | custom-call | tf_op jit(solution)/shard_map/final/pallas_call | solution.py:35
  (8 shorter events, 0.2 us)
Async XLA Ops:
  2.0 14.2 %collective-permute-start.1 = (bf16[128,512]{1,0:T(8,128)(2,1)S(1)}, bf16[128,512]{1,0:T(8,128)(2,1)S(1)}, u32[]{:S(2)}, u32[]{:S(2)}) collective-permute-start(bf16[128,512]{1,0:T(8,128)(2,1)S(1)} %get-tuple-element.39.own), channel_id=1, source_target_pairs={{0,1},{1,0},{2,3},{3,2},{4,5},{5,4},{6,7},{7,6},{8,9},{9,8},{10,11... | collective-permute-start | bytes 393224 | tf_op jit(solution)/shard_map/ppermute | solution.py:245
  4.6 13.5 %collective-permute-start = (bf16[128,512]{1,0:T(8,128)(2,1)S(1)}, bf16[128,512]{1,0:T(8,128)(2,1)S(1)}, u32[]{:S(2)}, u32[]{:S(2)}) collective-permute-start(bf16[128,512]{1,0:T(8,128)(2,1)S(1)} %get-tuple-element.39.own), channel_id=1, source_target_pairs={{0,31},{1,2},{2,1},{3,4},{4,3},{5,6},{6,5},{7,8},{8,7},{9,10},{10,... | collective-permute-start | bytes 393224 | tf_op jit(solution)/shard_map/ppermute | solution.py:245
  11.5 8.1 %collective-permute-start.5 = (bf16[128,512]{1,0:T(8,128)(2,1)S(1)}, bf16[128,512]{1,0:T(8,128)(2,1)S(1)}, u32[]{:S(2)}, u32[]{:S(2)}) collective-permute-start(bf16[128,512]{1,0:T(8,128)(2,1)S(1)} %get-tuple-element.39.own), channel_id=1, source_target_pairs={{0,1},{1,0},{2,3},{3,2},{4,5},{5,4},{6,7},{7,6},{8,9},{9,8},{10,11... | collective-permute-start | bytes 393224 | tf_op jit(solution)/shard_map/ppermute | solution.py:245
  13.9 5.7 %collective-permute-start.6 = (bf16[128,512]{1,0:T(8,128)(2,1)S(1)}, bf16[128,512]{1,0:T(8,128)(2,1)S(1)}, u32[]{:S(2)}, u32[]{:S(2)}) collective-permute-start(bf16[128,512]{1,0:T(8,128)(2,1)S(1)} %get-tuple-element.39.own), channel_id=1, source_target_pairs={{0,32},{1,33},{2,34},{3,35},{4,36},{5,37},{6,38},{7,39},{8,40},{9,... | collective-permute-start | bytes 393224 | tf_op jit(solution)/shard_map/ppermute | solution.py:245
  16.3 5.7 %collective-permute-start.3 = (bf16[128,512]{1,0:T(8,128)(2,1)S(1)}, bf16[128,512]{1,0:T(8,128)(2,1)S(1)}, u32[]{:S(2)}, u32[]{:S(2)}) collective-permute-start(bf16[128,512]{1,0:T(8,128)(2,1)S(1)} %pass_inner.1.after.inner), channel_id=1, source_target_pairs={{0,1},{1,0},{2,3},{3,2},{4,5},{5,4},{6,7},{7,6},{8,9},{9,8},{10,11... | collective-permute-start | bytes 393224 | tf_op jit(solution)/shard_map/ppermute | solution.py:245
  18.1 3.9 %collective-permute-start.4 = (bf16[128,512]{1,0:T(8,128)(2,1)S(1)}, bf16[128,512]{1,0:T(8,128)(2,1)S(1)}, u32[]{:S(2)}, u32[]{:S(2)}) collective-permute-start(bf16[128,512]{1,0:T(8,128)(2,1)S(1)} %pass_inner.1.after.inner), channel_id=1, source_target_pairs={{0,32},{1,33},{2,34},{3,35},{4,36},{5,37},{6,38},{7,39},{8,40},{9,... | collective-permute-start | bytes 393224 | tf_op jit(solution)/shard_map/ppermute | solution.py:245
  18.1 4.8 %collective-permute-start.2 = (bf16[128,512]{1,0:T(8,128)(2,1)S(1)}, bf16[128,512]{1,0:T(8,128)(2,1)S(1)}, u32[]{:S(2)}, u32[]{:S(2)}) collective-permute-start(bf16[128,512]{1,0:T(8,128)(2,1)S(1)} %pass_outer.1.outer), channel_id=1, source_target_pairs={{0,1},{1,0},{2,3},{3,2},{4,5},{5,4},{6,7},{7,6},{8,9},{9,8},{10,11... | collective-permute-start | bytes 393224 | tf_op jit(solution)/shard_map/ppermute | solution.py:245
  19.6 3.3 %collective-permute-start.7 = (bf16[128,512]{1,0:T(8,128)(2,1)S(1)}, bf16[128,512]{1,0:T(8,128)(2,1)S(1)}, u32[]{:S(2)}, u32[]{:S(2)}) collective-permute-start(bf16[128,512]{1,0:T(8,128)(2,1)S(1)} %pass_outer.1.outer), channel_id=1, source_target_pairs={{0,32},{1,33},{2,34},{3,35},{4,36},{5,37},{6,38},{7,39},{8,40},{9,... | collective-permute-start | bytes 393224 | tf_op jit(solution)/shard_map/ppermute | solution.py:245
  24.7 4.8 %collective-permute-start.8 = (bf16[128,512]{1,0:T(8,128)(2,1)S(1)}, bf16[128,512]{1,0:T(8,128)(2,1)S(1)}, u32[]{:S(2)}, u32[]{:S(2)}) collective-permute-start(bf16[128,512]{1,0:T(8,128)(2,1)S(1)} %get-tuple-element.65), channel_id=1, source_target_pairs={{0,1},{1,0},{2,3},{3,2},{4,5},{5,4},{6,7},{7,6},{8,9},{9,8},{10,11... | collective-permute-start | bytes 393224 | tf_op jit(solution)/shard_map/ppermute | solution.py:245
  26.6 2.9 %collective-permute-start.9 = (bf16[384,512]{1,0:T(8,128)(2,1)S(1)}, bf16[384,512]{1,0:T(8,128)(2,1)S(1)}, u32[]{:S(2)}, u32[]{:S(2)}) collective-permute-start(bf16[384,512]{1,0:T(8,128)(2,1)S(1)} %get-tuple-element.66), channel_id=1, source_target_pairs={{0,32},{1,33},{2,34},{3,35},{4,36},{5,37},{6,38},{7,39},{8,40},{9,... | collective-permute-start | bytes 1179656 | tf_op jit(solution)/shard_map/ppermute | solution.py:245
  26.7 6.6 %collective-permute-start.11 = (bf16[128,512]{1,0:T(8,128)(2,1)S(1)}, bf16[128,512]{1,0:T(8,128)(2,1)S(1)}, u32[]{:S(2)}, u32[]{:S(2)}) collective-permute-start(bf16[128,512]{1,0:T(8,128)(2,1)S(1)} %get-tuple-element.67), channel_id=1, source_target_pairs={{0,1},{1,0},{2,3},{3,2},{4,5},{5,4},{6,7},{7,6},{8,9},{9,8},{10,11... | collective-permute-start | bytes 393224 | tf_op jit(solution)/shard_map/ppermute | solution.py:245
  29.6 7.2 %collective-permute-start.10 = (bf16[128,512]{1,0:T(8,128)(2,1)S(1)}, bf16[128,512]{1,0:T(8,128)(2,1)S(1)}, u32[]{:S(2)}, u32[]{:S(2)}) collective-permute-start(bf16[128,512]{1,0:T(8,128)(2,1)S(1)} %merge_outer.1.refs_0_), channel_id=1, source_target_pairs={{0,31},{1,2},{2,1},{3,4},{4,3},{5,6},{6,5},{7,8},{8,7},{9,10},{10,... | collective-permute-start | bytes 393224 | tf_op jit(solution)/shard_map/ppermute | solution.py:245
  32.3 4.7 %collective-permute-start.13 = (bf16[128,512]{1,0:T(8,128)(2,1)S(1)}, bf16[128,512]{1,0:T(8,128)(2,1)S(1)}, u32[]{:S(2)}, u32[]{:S(2)}) collective-permute-start(bf16[128,512]{1,0:T(8,128)(2,1)S(1)} %get-tuple-element.68), channel_id=1, source_target_pairs={{0,1},{1,0},{2,3},{3,2},{4,5},{5,4},{6,7},{7,6},{8,9},{9,8},{10,11... | collective-permute-start | bytes 393224 | tf_op jit(solution)/shard_map/ppermute | solution.py:245
  33.4 5.5 %copy-start = (bf16[512,512]{1,0:T(8,128)(2,1)S(1)}, bf16[512,512]{1,0:T(8,128)(2,1)}, u32[]{:S(2)}) copy-start(bf16[512,512]{1,0:T(8,128)(2,1)} %w_send.1) | copy-start | bytes 1572868
  33.4 5.5 %copy-start.1 = (f32[1,1,128,512]{3,2,1,0:T(8,128)S(1)}, f32[1,1,128,512]{3,2,1,0:T(8,128)}, u32[]{:S(2)}) copy-start(f32[1,1,128,512]{3,2,1,0:T(8,128)} %param.15) | copy-start | bytes 786436
  33.4 5.5 %collective-permute-start.12 = (bf16[128,512]{1,0:T(8,128)(2,1)S(1)}, bf16[128,512]{1,0:T(8,128)(2,1)S(1)}, u32[]{:S(2)}, u32[]{:S(2)}) collective-permute-start(bf16[128,512]{1,0:T(8,128)(2,1)S(1)} %merge_inner.1), channel_id=1, source_target_pairs={{0,1},{1,0},{2,3},{3,2},{4,5},{5,4},{6,7},{7,6},{8,9},{9,8},{10,11... | collective-permute-start | bytes 393224 | tf_op jit(solution)/shard_map/ppermute | solution.py:245
  36.8 23.1 %copy-start.2 = (f32[1,1,128,512]{3,2,1,0:T(8,128)S(1)}, f32[1,1,128,512]{3,2,1,0:T(8,128)}, u32[]{:S(2)}) copy-start(f32[1,1,128,512]{3,2,1,0:T(8,128)} %param.14) | copy-start | bytes 786436
